TPU v7x, 32 devices: a whole 2x2x4 slice. The times are simulated.
32 devices in a mesh: rows: 16 (over z, x, core), inner: 2 (over y).
Axes of the slice: x: 2, y: 2, z: 4, core: 2. Of those that a mesh axis runs over, the one named last changes fastest.
Arguments:
- hardness_blocks: float32 [80, 4, 128, 128], P('rows', None, 'inner'), may hold values from -0.046875 to 0.046875
- inverse_blocks: float32 [80, 6, 128, 128], P('rows', None, 'inner'), may hold values from -6 to 6
- hardness_pattern: int32 [80, 4], P('rows'), may hold values from 0 to 79, as said below
- inverse_pattern: int32 [80, 6], replicated, may hold values from 0 to 79, as said below
Outputs:
- updated_blocks: float32 [80, 6, 128, 128], P('rows', None, 'inner')
Inputs may be any that keep to these rules, and one draw needn't show every extreme that they name: `hardness_pattern`: row i lists 4 different block columns, the first being i, all within 5 of i. `inverse_pattern`: row i lists 6 different block columns, the first being i, all within 5 of i.
All inputs are finite; a program needn't handle non-finite values.
Results may differ from a plain program's by a relative error of at most 0.0001.
Values sent between devices are 32-bit elements; how exact they have to be, the bound alone decides.
No kernel may reach another device: no remote copies, remote signals or barrier semaphores. Data moves between devices by JAX's collectives and lax.ppermute only.
A program may use at most 64 MiB of HBM per device.

v0:
```python
import jax
import jax.numpy as jnp
from jax import lax
from jax.sharding import PartitionSpec as P

REACH = 5


def with_halo(cells, sides, width):
    for axis, dim in sides:
        count = lax.axis_size(axis)
        ends = count - 1
        head = lax.slice_in_dim(cells, 0, width, axis=dim)
        tail = lax.slice_in_dim(cells, cells.shape[dim] - width, cells.shape[dim], axis=dim)
        cells = jnp.concatenate(
            [
                lax.ppermute(tail, axis, [(i, (i + 1) % count) for i in range(ends)]),
                cells,
                lax.ppermute(head, axis, [((i + 1) % count, i) for i in range(ends)]),
            ],
            axis=dim,
        )
    return cells


def locate_blocks(left_pattern, target_pattern, right_pattern, base):
    local = left_pattern - base
    listed = jnp.take(right_pattern, local, axis=0)
    equal = listed[:, :, None, :] == target_pattern[:, None, :, None]
    width = right_pattern.shape[1]
    slot = jnp.sum(jnp.where(equal, jnp.arange(width, dtype=jnp.int32), 0), axis=3)
    flat = local[:, :, None] * width + slot
    sentinel = right_pattern.shape[0] * width
    return jnp.where(jnp.any(equal, axis=3), flat, sentinel)


def make_fold(left, flat, total, piece):
    count = piece.shape[2]
    lined = piece.reshape(piece.shape[0] * piece.shape[1], count, piece.shape[3])
    lined = jnp.concatenate([lined, jnp.zeros((1, count, piece.shape[3]), lined.dtype)], axis=0)
    for slot in range(flat.shape[1]):
        chosen = jnp.take(lined, flat[:, slot].reshape(-1), axis=0)
        chosen = chosen.reshape(flat.shape[0], flat.shape[2], count, piece.shape[3])
        total = total + jnp.einsum(
            "irp,ikpd->ikrd", left[:, slot], chosen, precision=lax.Precision.HIGHEST
        )
    return total


def shards(hardness_blocks, inverse_blocks, hardness_pattern, inverse_pattern):
    count_rows = inverse_blocks.shape[0]
    first_row = lax.axis_index("rows") * count_rows
    base = first_row - REACH
    padded = jnp.pad(inverse_pattern, ((REACH, REACH), (0, 0)), constant_values=-1)
    beside_all = lax.dynamic_slice_in_dim(padded, first_row, count_rows + 2 * REACH, 0)
    own_pattern = lax.dynamic_slice_in_dim(inverse_pattern, first_row, count_rows, 0)
    flat_one = locate_blocks(hardness_pattern, own_pattern, beside_all, base)
    flat_two = locate_blocks(own_pattern, own_pattern, beside_all, base)
    empty = jnp.zeros(
        (count_rows, own_pattern.shape[1], inverse_blocks.shape[2], inverse_blocks.shape[3]),
        jnp.float32,
    )
    extended = with_halo(inverse_blocks, (("rows", 0),), REACH)
    product = make_fold(
        hardness_blocks, flat_one, empty, lax.all_gather(extended, "inner", axis=2, tiled=True)
    )
    product_ext = with_halo(product, (("rows", 0),), REACH)
    carried = make_fold(
        inverse_blocks, flat_two, empty, lax.all_gather(product_ext, "inner", axis=2, tiled=True)
    )
    return 2.0 * inverse_blocks - carried


def solution(mesh):
    in_specs = (
        P("rows", None, "inner", None),
        P("rows", None, "inner", None),
        P("rows", None),
        P(),
    )
    out_specs = P("rows", None, "inner", None)
    return jax.shard_map(shards, mesh=mesh, in_specs=in_specs, out_specs=out_specs, check_vma=False)
```

profile of v0, /device:TPU:14, one launch (start us, length us, event | category | flops | bytes accessed | tf_op | source)
XLA Modules:
  0.0 299.9 jit_solution(56990677035787385)
XLA Ops:
  8.5 2.4 collective-permute-start
  10.9 20.0 %collective-permute-done.1 = f32[5,6,64,128]{3,2,1,0:T(8,128)S(1)} collective-permute-done((f32[5,6,64,128]{3,2,1,0:T(8,128)}, f32[5,6,64,128]{3,2,1,0:T(8,128)S(1)}, u32[]{:S(2)}, u32[]{:S(2)}) %collective-permute-start.1) | collective-permute-done | bytes 983072 | tf_op jit(solution)/shard_map/ppermute | solution.py:19
  30.9 2.7 collective-permute-done
  33.6 3.2 %pad_maximum_fusion = f32[15,6,64,128]{3,2,1,0:T(8,128)} fusion(f32[5,6,64,128]{3,2,1,0:T(8,128)S(1)} %collective-permute-done.1, f32[5,6,64,128]{3,2,1,0:T(8,128)} %param.7, f32[5,6,64,128]{3,2,1,0:T(8,128)S(1)} %collective-permute-done), kind=kLoop, calls=%fused_computation.12 | loop fusion | flops 1474560 | bytes 5898240 | tf_op jit(solution)/shard_map/concatenate | solution.py:15
  41.1 71.0 %all-gather.3.cloned.1.call-done = f32[15,6,128,128]{3,2,1,0:T(8,128)} async-done(((f32[15,6,64,128]{3,2,1,0:T(8,128)}), f32[15,6,128,128]{3,2,1,0:T(8,128)}) %all-gather.3.cloned.1.call-update) | async-done | bytes 5898256 | tf_op jit(solution)/shard_map/all_gather | solution.py:65
  112.1 5.9 %concatenate.13 = f32[91,128,128]{2,1,0:T(8,128)} pad(f32[90,128,128]{2,1,0:T(8,128)} %bitcast.120, f32[]{:T(128)} %constant.26.clone.1), padding=0_1x0_0x0_0 | pad | bytes 11862020 | tf_op jit(solution)/shard_map/concatenate | solution.py:40
  118.0 4.6 %gather_fusion.2 = f32[30,128,128]{2,1,0:T(8,128)} fusion(f32[91,128,128]{2,1,0:T(8,128)} %concatenate.13, s32[1024]{0:T(1024)S(1)} %pad_clamp_fusion.9), kind=kCustom, calls=%fused_computation.clone | custom fusion | bytes 3932280 | tf_op jit(solution)/shard_map/jit(_take)/gather | solution.py:42
  122.7 4.7 %gather_fusion.3 = f32[30,128,128]{2,1,0:T(8,128)} fusion(f32[91,128,128]{2,1,0:T(8,128)} %concatenate.13, s32[1024]{0:T(1024)S(1)} %pad_clamp_fusion.8), kind=kCustom, calls=%fused_computation.1.clone | custom fusion | bytes 3932280 | tf_op jit(solution)/shard_map/jit(_take)/gather | solution.py:42
  127.4 4.6 %gather_fusion.4 = f32[30,128,128]{2,1,0:T(8,128)} fusion(f32[91,128,128]{2,1,0:T(8,128)} %concatenate.13, s32[1024]{0:T(1024)S(1)} %pad_clamp_fusion.7), kind=kCustom, calls=%fused_computation.2.clone | custom fusion | bytes 3932280 | tf_op jit(solution)/shard_map/jit(_take)/gather | solution.py:42
  132.0 3.4 %gather_fusion.5 = f32[30,128,128]{2,1,0:T(8,128)S(1)} fusion(f32[91,128,128]{2,1,0:T(8,128)} %concatenate.13, s32[1024]{0:T(1024)S(1)} %pad_clamp_fusion.6), kind=kCustom, calls=%fused_computation.3.clone | custom fusion | bytes 3932280 | tf_op jit(solution)/shard_map/jit(_take)/gather | solution.py:42
  145.4 2.6 collective-permute-start.2
  147.9 19.5 %collective-permute-done.3 = f32[5,6,64,128]{3,2,1,0:T(8,128)S(1)} collective-permute-done((f32[5,6,64,128]{3,2,1,0:T(8,128)S(1)}, f32[5,6,64,128]{3,2,1,0:T(8,128)S(1)}, u32[]{:S(2)}, u32[]{:S(2)}) %collective-permute-start.3) | collective-permute-done | bytes 983072 | tf_op jit(solution)/shard_map/ppermute | solution.py:19
  167.5 2.8 collective-permute-done.2
  170.3 2.0 pad_maximum_fusion.1
  175.6 71.8 %all-gather.5.cloned.1.call-done = f32[15,6,128,128]{3,2,1,0:T(8,128)} async-done(((f32[15,6,64,128]{3,2,1,0:T(8,128)}), f32[15,6,128,128]{3,2,1,0:T(8,128)}) %all-gather.5.cloned.1.call-update) | async-done | bytes 5898256 | tf_op jit(solution)/shard_map/all_gather | solution.py:69
  247.5 5.9 %concatenate.15 = f32[91,128,128]{2,1,0:T(8,128)} pad(f32[90,128,128]{2,1,0:T(8,128)} %bitcast.121, f32[]{:T(128)} %constant.26.clone.1), padding=0_1x0_0x0_0 | pad | bytes 11862020 | tf_op jit(solution)/shard_map/concatenate | solution.py:40
  253.4 3.4 %gather_fusion.6 = f32[30,128,128]{2,1,0:T(8,128)S(1)} fusion(f32[91,128,128]{2,1,0:T(8,128)} %concatenate.15, s32[1024]{0:T(1024)S(1)} %pad_clamp_fusion.5), kind=kCustom, calls=%fused_computation.4.clone | custom fusion | bytes 3932280 | tf_op jit(solution)/shard_map/jit(_take)/gather | solution.py:42
  258.0 2.2 fusion.8
  260.2 4.6 %gather_fusion.7 = f32[30,128,128]{2,1,0:T(8,128)} fusion(f32[91,128,128]{2,1,0:T(8,128)} %concatenate.15, s32[1024]{0:T(1024)S(1)} %pad_clamp_fusion.4), kind=kCustom, calls=%fused_computation.5.clone | custom fusion | bytes 3932280 | tf_op jit(solution)/shard_map/jit(_take)/gather | solution.py:42
  264.8 4.7 %gather_fusion.8 = f32[30,128,128]{2,1,0:T(8,128)} fusion(f32[91,128,128]{2,1,0:T(8,128)} %concatenate.15, s32[1024]{0:T(1024)S(1)} %pad_clamp_fusion.3), kind=kCustom, calls=%fused_computation.6.clone | custom fusion | bytes 3932280 | tf_op jit(solution)/shard_map/jit(_take)/gather | solution.py:42
  269.5 4.6 %gather_fusion.9 = f32[30,128,128]{2,1,0:T(8,128)} fusion(f32[91,128,128]{2,1,0:T(8,128)} %concatenate.15, s32[1024]{0:T(1024)S(1)} %pad_clamp_fusion.2), kind=kCustom, calls=%fused_computation.7.clone | custom fusion | bytes 3932280 | tf_op jit(solution)/shard_map/jit(_take)/gather | solution.py:42
  274.2 4.8 %gather_fusion.10 = f32[30,128,128]{2,1,0:T(8,128)} fusion(f32[91,128,128]{2,1,0:T(8,128)} %concatenate.15, s32[1024]{0:T(1024)S(1)} %pad_clamp_fusion.1), kind=kCustom, calls=%fused_computation.8.clone | custom fusion | bytes 3932280 | tf_op jit(solution)/shard_map/jit(_take)/gather | solution.py:42
  278.9 3.4 %gather_fusion.11 = f32[30,128,128]{2,1,0:T(8,128)S(1)} fusion(f32[91,128,128]{2,1,0:T(8,128)} %concatenate.15, s32[1024]{0:T(1024)S(1)} %pad_clamp_fusion), kind=kCustom, calls=%fused_computation.9.clone | custom fusion | bytes 3932280 | tf_op jit(solution)/shard_map/jit(_take)/gather | solution.py:42
  290.8 2.3 fusion.1
  (107 shorter events, 28.8 us)
Async XLA Ops:
  6.5 105.5 %all-gather.3.cloned.1.call-start = ((), (), s32[]{:S(2)}) async-start(), calls=%async_computation | async-start | bytes 8847360 | tf_op jit(solution)/shard_map/all_gather | solution.py:65
  6.5 24.4 %collective-permute-start.1 = (f32[5,6,64,128]{3,2,1,0:T(8,128)}, f32[5,6,64,128]{3,2,1,0:T(8,128)S(1)}, u32[]{:S(2)}, u32[]{:S(2)}) collective-permute-start(f32[5,6,64,128]{3,2,1,0:T(8,128)} %param.7), channel_id=1, source_target_pairs={{2,0},{4,2},{6,4},{8,6},{10,8},{12,10},{14,12},{16,14},{18,16},{20... | collective-permute-start | bytes 2949128 | tf_op jit(solution)/shard_map/ppermute | solution.py:19
  8.5 25.1 %collective-permute-start = (f32[5,6,64,128]{3,2,1,0:T(8,128)}, f32[5,6,64,128]{3,2,1,0:T(8,128)S(1)}, u32[]{:S(2)}, u32[]{:S(2)}) collective-permute-start(f32[5,6,64,128]{3,2,1,0:T(8,128)} %param.7), channel_id=1, source_target_pairs={{0,2},{2,4},{4,6},{6,8},{8,10},{10,12},{12,14},{14,16},{16,18},{18... | collective-permute-start | bytes 2949128 | tf_op jit(solution)/shard_map/ppermute | solution.py:17
  36.8 0.7 copy-start.8
  36.8 1.0 copy-start.9
  36.8 210.7 %all-gather.5.cloned.1.call-start = ((), (), s32[]{:S(2)}) async-start(), calls=%async_computation.1 | async-start | bytes 8847360 | tf_op jit(solution)/shard_map/all_gather | solution.py:69
  135.4 1.8 copy-start.7
  137.2 1.5 copy-start.4
  139.0 1.5 copy-start.2
  143.4 24.1 %collective-permute-start.3 = (f32[5,6,64,128]{3,2,1,0:T(8,128)S(1)}, f32[5,6,64,128]{3,2,1,0:T(8,128)S(1)}, u32[]{:S(2)}, u32[]{:S(2)}) collective-permute-start(f32[5,6,64,128]{3,2,1,0:T(8,128)S(1)} %fusion.2), channel_id=1, source_target_pairs={{2,0},{4,2},{6,4},{8,6},{10,8},{12,10},{14,12},{16,14},{18,16},{20... | collective-permute-start | bytes 2949128 | tf_op jit(solution)/shard_map/ppermute | solution.py:19
  145.4 24.9 %collective-permute-start.2 = (f32[5,6,64,128]{3,2,1,0:T(8,128)S(1)}, f32[5,6,64,128]{3,2,1,0:T(8,128)S(1)}, u32[]{:S(2)}, u32[]{:S(2)}) collective-permute-start(f32[5,6,64,128]{3,2,1,0:T(8,128)S(1)} %fusion.2), channel_id=1, source_target_pairs={{0,2},{2,4},{4,6},{6,8},{8,10},{10,12},{12,14},{14,16},{16,18},{18... | collective-permute-start | bytes 2949128 | tf_op jit(solution)/shard_map/ppermute | solution.py:17
  256.8 1.2 copy-start.5
  282.3 1.8 copy-start.6
  284.2 1.5 copy-start.3
  285.9 1.5 copy-start.1
  287.7 1.5 copy-start
Sparse Core Ops, SparseCore 0:
  36.9 75.0 all-gather.2
  172.4 75.0 all-gather.4
where the time goes:
time: 303 us; the launch traced here: 300 us
  waiting for transfers between devices  188 us (62%)
  local copies, waits for them, and re-layouts  61.6 us (20%)
  matrix products  14.2 us (5%)
  between operations  13.9 us (5%)
  other arithmetic  13.4 us (4%)
  starting transfers between devices  8.87 us (3%)
    all_gather x1, waiting for transfers between devices, shards(): lax.all_gather(product_ext, 'inner', axis=2, tiled=True)  71.8 us
    all_gather x1, waiting for transfers between devices, shards(): lax.all_gather(extended, 'inner', axis=2, tiled=True)  71 us
    gather x10, local copies, waits for them, and re-layouts, make_fold(): chosen = jnp.take(lined, flat[:, slot].reshape(-1), axis=0)  42.9 us
    ppermute x2, waiting for transfers between devices, with_halo(): lax.ppermute(head, axis, [((i + 1) % count, i) for i in range(ends)])  39.6 us
    dot_general x10, matrix products, make_fold(): jnp.einsum('irp,ikpd->ikrd', left[:, slot], chosen, precision=lax.Precisi...  14.2 us
    concatenate x2, local copies, waits for them, and re-layouts, make_fold(): jnp.concatenate([lined, jnp.zeros((1, count, piece.shape[3]), lined.dtype...  11.9 us
  transfers between devices with their start and end apart: 6, of which 6 were waited for; matrix products, arithmetic and copies ran while one was open for 2% of the time, Pallas kernels for 0%

commit v1 on v0

--- a/solution.py
+++ b/solution.py
@@ -1,9 +1,15 @@
+import functools
+
 import jax
 import jax.numpy as jnp
 from jax import lax
+from jax.experimental import pallas as pl
+from jax.experimental.pallas import tpu as pltpu
 from jax.sharding import PartitionSpec as P
 
 REACH = 5
+CHUNKS = 1
+VMEM_BYTES = 32 * 1024 * 1024
 
 
 def with_halo(cells, sides, width):
@@ -23,15 +29,19 @@
     return cells
 
 
-def locate_blocks(left_pattern, target_pattern, right_pattern, base):
+def match_slots(left_pattern, target_pattern, right_pattern, base):
     local = left_pattern - base
     listed = jnp.take(right_pattern, local, axis=0)
     equal = listed[:, :, None, :] == target_pattern[:, None, :, None]
     width = right_pattern.shape[1]
     slot = jnp.sum(jnp.where(equal, jnp.arange(width, dtype=jnp.int32), 0), axis=3)
-    flat = local[:, :, None] * width + slot
-    sentinel = right_pattern.shape[0] * width
-    return jnp.where(jnp.any(equal, axis=3), flat, sentinel)
+    return local[:, :, None], slot, jnp.any(equal, axis=3)
+
+
+def locate_blocks(left_pattern, target_pattern, right_pattern, base):
+    local, slot, found = match_slots(left_pattern, target_pattern, right_pattern, base)
+    width = right_pattern.shape[1]
+    return jnp.where(found, local * width + slot, right_pattern.shape[0] * width)
 
 
 def make_fold(left, flat, total, piece):
@@ -47,13 +57,17 @@
     return total
 
 
-def shards(hardness_blocks, inverse_blocks, hardness_pattern, inverse_pattern):
-    count_rows = inverse_blocks.shape[0]
+def patterns_beside(inverse_pattern, count_rows):
     first_row = lax.axis_index("rows") * count_rows
-    base = first_row - REACH
     padded = jnp.pad(inverse_pattern, ((REACH, REACH), (0, 0)), constant_values=-1)
     beside_all = lax.dynamic_slice_in_dim(padded, first_row, count_rows + 2 * REACH, 0)
     own_pattern = lax.dynamic_slice_in_dim(inverse_pattern, first_row, count_rows, 0)
+    return first_row - REACH, beside_all, own_pattern
+
+
+def general_shards(hardness_blocks, inverse_blocks, hardness_pattern, inverse_pattern):
+    count_rows = inverse_blocks.shape[0]
+    base, beside_all, own_pattern = patterns_beside(inverse_pattern, count_rows)
     flat_one = locate_blocks(hardness_pattern, own_pattern, beside_all, base)
     flat_two = locate_blocks(own_pattern, own_pattern, beside_all, base)
     empty = jnp.zeros(
@@ -69,6 +83,238 @@
         inverse_blocks, flat_two, empty, lax.all_gather(product_ext, "inner", axis=2, tiled=True)
     )
     return 2.0 * inverse_blocks - carried
+
+
+def call(body, outs, name, scratch=(), specs=None, flops=0, nbytes=0):
+    params = dict(
+        out_shape=outs,
+        scratch_shapes=list(scratch),
+        compiler_params=pltpu.CompilerParams(vmem_limit_bytes=VMEM_BYTES),
+        name=name,
+        cost_estimate=pl.CostEstimate(flops=flops, bytes_accessed=nbytes, transcendentals=0),
+    )
+    if specs is not None:
+        params.update(grid=(1,), in_specs=specs)
+    return pl.pallas_call(body, **params)
+
+
+def is_low(shape):
+    return lax.broadcasted_iota(jnp.int32, shape, len(shape) - 1) < shape[-1] // 2
+
+
+def swapped(x):
+    return pltpu.roll(x, x.shape[-1] // 2, x.ndim - 1)
+
+
+def unzip_lanes(a, b):
+    low = is_low(a.shape)
+    return jnp.where(low, a, swapped(b)), jnp.where(low, swapped(a), b)
+
+
+def halves(x):
+    high = x.astype(jnp.bfloat16)
+    return high, (x - high.astype(jnp.float32)).astype(jnp.bfloat16)
+
+
+def split_columns(z_ref, own_ref, send_ref):
+    second = lax.axis_index("inner") == 1
+    rows, pairs, half, lanes = own_ref.shape
+    for i in range(rows):
+        for j in range(pairs):
+            turned = z_ref[i, 2 * j : 2 * j + 2].reshape(2 * half, lanes).T
+            top, bottom = turned[:half], turned[half:]
+            own_ref[i, j] = jnp.where(second, bottom, top)
+            send_ref[i, j] = jnp.where(second, top, bottom)
+
+
+def gather_dot(index_ref, i, right_slots, out_slots, high_ref, low_ref, lhs_high, lhs_low, right, dims):
+    depth = high_ref.shape[1]
+    for s in range(right_slots):
+        for k in range(out_slots):
+            at = index_ref[(i * right_slots + s) * out_slots + k]
+            place = (pl.ds(k * depth, depth), pl.ds(s * 128, 128))
+            lhs_high[place] = high_ref[at]
+            lhs_low[place] = low_ref[at]
+    dot = functools.partial(
+        lax.dot_general, dimension_numbers=(dims, ((), ())), preferred_element_type=jnp.float32
+    )
+    right_high, right_low = right
+    return (
+        dot(lhs_high[...], right_low)
+        + dot(lhs_low[...], right_high)
+        + dot(lhs_high[...], right_high)
+    )
+
+
+def first_product(index_ref, z_own, z_oth, on_own, on_oth, off_own, off_oth, j_own, j_oth, p_ref,
+                  z_high, z_low, j_high, j_low, lhs_high, lhs_low):
+    second = lax.axis_index("inner") == 1
+    rows, pairs, depth, lanes = z_own.shape
+    for g, (own, oth) in enumerate(((z_own, z_oth), (on_own, on_oth), (off_own, off_oth))):
+        for i in range(rows):
+            for j in range(pairs):
+                even, odd = unzip_lanes(own[i, j], oth[i, j])
+                at = ((g * rows + i) * pairs + j) * 2
+                z_high[at], z_low[at] = halves(even)
+                z_high[at + 1], z_low[at + 1] = halves(odd)
+    z_high[z_high.shape[0] - 1] = jnp.zeros(z_high.shape[1:], jnp.bfloat16)
+    z_low[z_low.shape[0] - 1] = jnp.zeros(z_low.shape[1:], jnp.bfloat16)
+    slots, half = j_own.shape[1:3]
+    for i in range(rows):
+        for s in range(slots):
+            for part, source in ((0, j_own), (1, j_oth)):
+                x = source[i, s]
+                place = (i, pl.ds(part * half, half), pl.ds(s * 128, 128))
+                j_high[place], j_low[place] = halves(jnp.where(second, swapped(x), x))
+
+    @pl.loop(0, rows)
+    def _(i):
+        total = gather_dot(index_ref, i, slots, 2 * pairs, z_high, z_low, lhs_high, lhs_low,
+                           (j_high[i], j_low[i]), ((1,), (1,)))
+        p_ref[i] = total.reshape(p_ref.shape[1:])
+
+
+def left_blocks(z_own, z_send, z_oth, z_rest, high_ref, low_ref):
+    rows, pairs, half, lanes = z_own.shape
+    for i in range(rows):
+        for j in range(pairs):
+            for part, (own, oth) in enumerate(((z_own, z_oth), (z_send, z_rest))):
+                for slot, x in enumerate(unzip_lanes(own[i, j], oth[i, j])):
+                    place = (i, pl.ds((2 * j + slot) * lanes + part * half, half))
+                    high_ref[place], low_ref[place] = halves(x)
+
+
+def second_product(index_ref, p_own, p_on, p_off, left_high, left_low, own_ref, send_ref,
+                   p_high, p_low, lhs_high, lhs_low):
+    rows, slots, depth, lanes = p_own.shape
+    for g, source in enumerate((p_own, p_on, p_off)):
+        for i in range(rows):
+            for k in range(slots):
+                at = (g * rows + i) * slots + k
+                p_high[at], p_low[at] = halves(source[i, k])
+    p_high[p_high.shape[0] - 1] = jnp.zeros(p_high.shape[1:], jnp.bfloat16)
+    p_low[p_low.shape[0] - 1] = jnp.zeros(p_low.shape[1:], jnp.bfloat16)
+
+    @pl.loop(0, rows)
+    def _(i):
+        total = gather_dot(index_ref, i, slots, slots, p_high, p_low, lhs_high, lhs_low,
+                           (left_high[i], left_low[i]), ((1,), (0,)))
+        total = total.reshape(slots, depth, lanes)
+        for j in range(slots // 2):
+            own_ref[i, j], send_ref[i, j] = unzip_lanes(total[2 * j], total[2 * j + 1])
+
+
+def finish(chunks, z_ref, *refs):
+    second = lax.axis_index("inner") == 1
+    own, oth, out_ref = refs[:chunks], refs[chunks : 2 * chunks], refs[-1]
+    rows, slots, half, lanes = z_ref.shape
+    for i in range(rows):
+        for j in range(slots // 2):
+            stack = jnp.concatenate([ref[i, j] for ref in own + oth], axis=0)
+            turned = stack.T
+            turned = jnp.where(second, swapped(turned), turned)
+            out_ref[i, 2 * j : 2 * j + 2] = (
+                2.0 * z_ref[i, 2 * j : 2 * j + 2] - turned.reshape(2, half, lanes)
+            )
+
+
+def half_shards(hardness_blocks, inverse_blocks, hardness_pattern, inverse_pattern):
+    rows, slots, half, lanes = inverse_blocks.shape
+    left_slots = hardness_blocks.shape[1]
+    pairs = slots // 2
+    count = lax.axis_size("rows")
+    f32 = functools.partial(jax.ShapeDtypeStruct, dtype=jnp.float32)
+    bf16 = functools.partial(jax.ShapeDtypeStruct, dtype=jnp.bfloat16)
+    pack = f32((rows, pairs, half, lanes))
+    smem = pl.BlockSpec(memory_space=pltpu.SMEM)
+    vmem = pl.BlockSpec(memory_space=pltpu.VMEM)
+
+    def across(x):
+        return lax.ppermute(x, "inner", [(0, 1), (1, 0)])
+
+    def on_swap(x):
+        return lax.ppermute(x, "rows", [(i, i ^ 1) for i in range(count)])
+
+    def off_swap(x):
+        inside = [(i, i + 1) for i in range(1, count - 1, 2)]
+        return lax.ppermute(x, "rows", inside + [(b, a) for a, b in inside])
+
+    z_own, z_send = call(split_columns, (pack, pack), "split_columns", nbytes=8 << 18)(inverse_blocks)
+    z_oth = across(z_send)
+    off_own = off_swap(z_own)
+    on_own = on_swap(z_own)
+    j_oth = across(hardness_blocks)
+    off_oth = off_swap(z_oth)
+    on_oth = on_swap(z_oth)
+    z_rest = across(z_own)
+
+    base, beside_all, own_pattern = patterns_beside(inverse_pattern, rows)
+    odd = lax.axis_index("rows") % 2
+
+    def flat_index(left_pattern):
+        local, slot, found = match_slots(left_pattern, own_pattern, beside_all, base)
+        offset = local - REACH
+        segment = jnp.where(offset < 0, 2 - odd, jnp.where(offset < rows, 0, 1 + odd))
+        flat = (segment * rows + jnp.where(offset < 0, offset + rows, offset % rows)) * slots + slot
+        return jnp.where(found, flat, 3 * rows * slots).astype(jnp.int32).reshape(-1)
+
+    flat_one = flat_index(hardness_pattern)
+    flat_two = flat_index(own_pattern)
+
+    left = call(
+        left_blocks, (bf16((rows, slots * lanes, lanes)),) * 2, "left_blocks", nbytes=16 << 18
+    )(z_own, z_send, z_oth, z_rest)
+
+    depth = half // CHUNKS
+    blocks = 3 * rows * slots + 1
+
+    def first(c):
+        part = pl.BlockSpec((rows, pairs, depth, lanes), lambda g: (0, 0, c, 0))
+        return call(
+            first_product,
+            f32((rows, slots, depth, lanes)),
+            "first_product",
+            scratch=[
+                pltpu.VMEM((blocks, depth, lanes), jnp.bfloat16),
+                pltpu.VMEM((blocks, depth, lanes), jnp.bfloat16),
+                pltpu.VMEM((rows, lanes, left_slots * lanes), jnp.bfloat16),
+                pltpu.VMEM((rows, lanes, left_slots * lanes), jnp.bfloat16),
+                pltpu.VMEM((slots * depth, left_slots * lanes), jnp.bfloat16),
+                pltpu.VMEM((slots * depth, left_slots * lanes), jnp.bfloat16),
+            ],
+            specs=[smem] + [part] * 6 + [vmem] * 2,
+            flops=6 * rows * left_slots * slots * depth * lanes * lanes,
+            nbytes=16 << 18,
+        )(flat_one, z_own, z_oth, on_own, on_oth, off_own, off_oth, hardness_blocks, j_oth)
+
+    def second(p, p_on, p_off):
+        return call(
+            second_product,
+            (f32((rows, pairs, depth, lanes)),) * 2,
+            "second_product",
+            scratch=[
+                pltpu.VMEM((blocks, depth, lanes), jnp.bfloat16),
+                pltpu.VMEM((blocks, depth, lanes), jnp.bfloat16),
+                pltpu.VMEM((slots * depth, slots * lanes), jnp.bfloat16),
+                pltpu.VMEM((slots * depth, slots * lanes), jnp.bfloat16),
+            ],
+            specs=[smem] + [vmem] * 5,
+            flops=6 * rows * slots * slots * depth * lanes * lanes,
+            nbytes=16 << 18,
+        )(flat_two, p, p_on, p_off, *left)
+
+    products = []
+    for c in range(CHUNKS):
+        p = first(c)
+        products.append((p, on_swap(p), off_swap(p)))
+    own, oth = [], []
+    for p, p_on, p_off in products:
+        mine, send = second(p, p_on, p_off)
+        own.append(mine)
+        oth.append(across(send))
+    return call(
+        functools.partial(finish, CHUNKS), f32(inverse_blocks.shape), "finish", nbytes=12 << 18
+    )(inverse_blocks, *own, *oth)
 
 
 def solution(mesh):
@@ -79,4 +325,6 @@
         P(),
     )
     out_specs = P("rows", None, "inner", None)
+    halved = mesh.shape["inner"] == 2 and mesh.shape["rows"] % 2 == 0
+    shards = half_shards if halved else general_shards
     return jax.shard_map(shards, mesh=mesh, in_specs=in_specs, out_specs=out_specs, check_vma=False)

time: 303 us -> 92.3 us (0.30)
  waiting for transfers between devices: 188 us -> 55.4 us
  local copies, waits for them, and re-layouts: 61.6 us -> 6.9 us
  matrix products: 14.2 us -> 0 us
  between operations: 13.9 us -> 0.2 us
  Pallas kernels: 0 us -> 13.7 us
  other arithmetic: 13.4 us -> 2.94 us
  starting transfers between devices: 8.87 us -> 12.7 us
    all_gather x2 -> x0, waiting for transfers between devices: 143 us -> none  [the longest x1 71.8 us: shards(): lax.all_gather(product_ext, 'inner', axis=2, tiled=True)]
    gather x15 -> x5, local copies, waits for them, and re-layouts: 44.2 us -> 1.3 us  [match_slots(): listed = jnp.take(right_pattern, local, axis=0)]
    dot_general x10 -> x0, matrix products: 14.2 us -> none  [make_fold(): jnp.einsum('irp,ikpd->ikrd', left[:, slot], chosen, precision=lax.Precisi...]
    pallas_call x0 -> x5, Pallas kernels: none -> 13.7 us  [the longest x1 5.25 us: second(): call(second_product, (f32((rows, pairs, depth, lanes)),) * 2, 'second_pro...]
    concatenate x2 -> x0, local copies, waits for them, and re-layouts: 11.9 us -> none  [make_fold(): jnp.concatenate([lined, jnp.zeros((1, count, piece.shape[3]), lined.dtype...]
    ppermute x4 -> x10, waiting for transfers between devices: 45.1 us -> 55.4 us  [the longest x4 31.3 us: across(): return lax.ppermute(x, 'inner', [(0, 1), (1, 0)])]
    select_n x19 -> x4, other arithmetic: 5.37 us -> 0.17 us  [the longest x2 0.08 us: match_slots(): listed = jnp.take(right_pattern, local, axis=0)]
    concatenate x2 -> x0, other arithmetic: 5.16 us -> none  [with_halo(): jnp.concatenate([lax.ppermute(tail, axis, [(i, (i + 1) % count) for i in...]
  transfers between devices with their start and end apart: 6 -> 10, of which waited for: 6 -> 4; matrix products, arithmetic and copies ran while one was open for 2% -> 6% of each run, Pallas kernels for 0% -> 7%
where the time goes in v1:
time: 92.3 us; the launch traced here: 91.9 us
  waiting for transfers between devices  55.4 us (60%)
  Pallas kernels  13.7 us (15%)
  starting transfers between devices  12.7 us (14%)
  local copies, waits for them, and re-layouts  6.9 us (7%)
  other arithmetic  2.94 us (3%)
    ppermute x4, waiting for transfers between devices, across(): return lax.ppermute(x, 'inner', [(0, 1), (1, 0)])  31.3 us
    ppermute x3, waiting for transfers between devices, off_swap(): return lax.ppermute(x, 'rows', inside + [(b, a) for a, b in inside])  24.1 us
    ppermute x3, starting transfers between devices, off_swap(): return lax.ppermute(x, 'rows', inside + [(b, a) for a, b in inside])  6.18 us
    pallas_call x1, Pallas kernels, second(): call(second_product, (f32((rows, pairs, depth, lanes)),) * 2, 'second_pro...  5.25 us
    pallas_call x1, Pallas kernels, first(): call(first_product, f32((rows, slots, depth, lanes)), 'first_product', sc...  4.95 us
    unnamed x19, local copies, waits for them, and re-layouts  4.31 us
    ppermute x3, starting transfers between devices, on_swap(): return lax.ppermute(x, 'rows', [(i, i ^ 1) for i in range(count)])  3.45 us
    ppermute x4, starting transfers between devices, across(): return lax.ppermute(x, 'inner', [(0, 1), (1, 0)])  3.1 us
  transfers between devices with their start and end apart: 10, of which 4 were waited for; matrix products, arithmetic and copies ran while one was open for 6% of the time, Pallas kernels for 7%

profile of v1, /device:TPU:14, one launch (start us, length us, event | category | flops | bytes accessed | tf_op | source)
XLA Modules:
  0.0 91.9 jit_solution(16751956617070620149)
XLA Ops:
  0.0 1.2 %copy-done = f32[5,6,64,128]{3,2,1,0:T(8,128)S(1)} copy-done((f32[5,6,64,128]{3,2,1,0:T(8,128)S(1)}, f32[5,6,64,128]{3,2,1,0:T(8,128)}, u32[]{:S(2)}) %copy-start) | copy-done | bytes 983064
  1.6 1.9 %collective-permute-start.3 = (f32[5,3,64,128]{3,2,1,0:T(8,128)S(1)}, f32[5,3,64,128]{3,2,1,0:T(8,128)S(1)}, u32[]{:S(2)}, u32[]{:S(2)}) collective-permute-start(f32[5,3,64,128]{3,2,1,0:T(8,128)S(1)} %get-tuple-element.11.z_own), channel_id=1, source_target_pairs={{2,4},{6,8},{10,12},{14,16},{18,20},{22,24},{26,28},{4,2},{8,6},{1... | collective-permute-start | bytes 1474568 | tf_op jit(solution)/shard_map/ppermute | solution.py:240
  3.5 1.7 %collective-permute-start.1 = (f32[5,3,64,128]{3,2,1,0:T(8,128)S(1)}, f32[5,3,64,128]{3,2,1,0:T(8,128)}, u32[]{:S(2)}, u32[]{:S(2)}) collective-permute-start(f32[5,3,64,128]{3,2,1,0:T(8,128)S(1)} %get-tuple-element.11.z_own), channel_id=1, source_target_pairs={{0,2},{2,0},{4,6},{6,4},{8,10},{10,8},{12,14},{14,12},{16,18},{18,... | collective-permute-start | bytes 1474568 | tf_op jit(solution)/shard_map/ppermute | solution.py:236
  5.7 1.5 %collective-permute-start = (f32[5,3,64,128]{3,2,1,0:T(8,128)S(1)}, f32[5,3,64,128]{3,2,1,0:T(8,128)S(1)}, u32[]{:S(2)}, u32[]{:S(2)}) collective-permute-start(f32[5,3,64,128]{3,2,1,0:T(8,128)S(1)} %get-tuple-element.12.z_send), channel_id=1, source_target_pairs={{0,1},{1,0},{2,3},{3,2},{4,5},{5,4},{6,7},{7,6},{8,9},{9,8},{10,11... | collective-permute-start | bytes 1474568 | tf_op jit(solution)/shard_map/ppermute | solution.py:233
  7.2 0.7 copy-done.8
  9.5 22.9 %collective-permute-done.z_oth = f32[5,3,64,128]{3,2,1,0:T(8,128)S(1)} collective-permute-done((f32[5,3,64,128]{3,2,1,0:T(8,128)S(1)}, f32[5,3,64,128]{3,2,1,0:T(8,128)S(1)}, u32[]{:S(2)}, u32[]{:S(2)}) %collective-permute-start) | collective-permute-done | bytes 491552 | tf_op jit(solution)/shard_map/ppermute | solution.py:233
  32.5 1.9 %collective-permute-start.4 = (f32[5,3,64,128]{3,2,1,0:T(8,128)S(1)}, f32[5,3,64,128]{3,2,1,0:T(8,128)}, u32[]{:S(2)}, u32[]{:S(2)}) collective-permute-start(f32[5,3,64,128]{3,2,1,0:T(8,128)S(1)} %collective-permute-done.z_oth), channel_id=1, source_target_pairs={{2,4},{6,8},{10,12},{14,16},{18,20},{22,24},{26,28},{4,2},{8,6},{1... | collective-permute-start | bytes 1474568 | tf_op jit(solution)/shard_map/ppermute | solution.py:240
  34.4 1.7 %collective-permute-start.2 = (f32[5,3,64,128]{3,2,1,0:T(8,128)S(1)}, f32[5,3,64,128]{3,2,1,0:T(8,128)}, u32[]{:S(2)}, u32[]{:S(2)}) collective-permute-start(f32[5,3,64,128]{3,2,1,0:T(8,128)S(1)} %collective-permute-done.z_oth), channel_id=1, source_target_pairs={{0,2},{2,0},{4,6},{6,4},{8,10},{10,8},{12,14},{14,12},{16,18},{18,... | collective-permute-start | bytes 1474568 | tf_op jit(solution)/shard_map/ppermute | solution.py:236
  36.3 0.7 compare_reduce_fusion.1
  37.0 0.7 fusion.1
  37.9 0.8 copy-done.5
  39.2 8.8 %collective-permute-done.4.off_oth = f32[5,3,64,128]{3,2,1,0:T(8,128)} collective-permute-done((f32[5,3,64,128]{3,2,1,0:T(8,128)S(1)}, f32[5,3,64,128]{3,2,1,0:T(8,128)}, u32[]{:S(2)}, u32[]{:S(2)}) %collective-permute-start.4) | collective-permute-done | bytes 491552 | tf_op jit(solution)/shard_map/ppermute | solution.py:240
  48.0 1.0 %copy-done.6 = f32[5,3,64,128]{3,2,1,0:T(8,128)S(1)} copy-done((f32[5,3,64,128]{3,2,1,0:T(8,128)S(1)}, f32[5,3,64,128]{3,2,1,0:T(8,128)}, u32[]{:S(2)}) %copy-start.6) | copy-done | bytes 491544
  49.0 5.0 %first_product.1.p_own = f32[5,6,64,128]{3,2,1,0:T(8,128)S(1)} custom-call(s32[120]{0:T(128)S(1)} %select_n.127.index_ref, f32[5,3,64,128]{3,2,1,0:T(8,128)S(1)} %get-tuple-element.11.z_own, f32[5,3,64,128]{3,2,1,0:T(8,128)S(1)} %collective-permute-done.z_oth, f32[5,3,64,128]{3,2,1,0:T(8,128)} %collective-permute-done.1.on_own, ...), custom_call_target="tpu_custom_call" | custom-call | flops 754974720 | bytes 4194304 | tf_op jit(solution)/shard_map/first_product/pallas_call | solution.py:273
  54.0 2.3 %collective-permute-start.7 = (f32[5,6,64,128]{3,2,1,0:T(8,128)S(1)}, f32[5,6,64,128]{3,2,1,0:T(8,128)S(1)}, u32[]{:S(2)}, u32[]{:S(2)}) collective-permute-start(f32[5,6,64,128]{3,2,1,0:T(8,128)S(1)} %first_product.1.p_own), channel_id=1, source_target_pairs={{2,4},{6,8},{10,12},{14,16},{18,20},{22,24},{26,28},{4,2},{8,6},{1... | collective-permute-start | bytes 2949128 | tf_op jit(solution)/shard_map/ppermute | solution.py:240
  56.7 0.6 gather_fusion
  57.7 0.7 compare_reduce_fusion
  58.3 0.7 fusion
  59.2 1.6 %left_blocks.1 = (bf16[5,768,128]{2,1,0:T(8,128)(2,1)S(1)}, bf16[5,768,128]{2,1,0:T(8,128)(2,1)S(1)}) custom-call(f32[5,3,64,128]{3,2,1,0:T(8,128)S(1)} %get-tuple-element.11.z_own, f32[5,3,64,128]{3,2,1,0:T(8,128)S(1)} %copy-done.4, f32[5,3,64,128]{3,2,1,0:T(8,128)S(1)} %collective-permute-done.z_oth, f32[5,3,64,128]{3,2,1,0:T(8,128)} %collective-permute-done.8.z_rest), custom_call_target="tpu_custom_call" | custom-call | bytes 4194304 | tf_op jit(solution)/shard_map/left_blocks/pallas_call | solution.py:264
  60.8 15.3 %collective-permute-done.7.p_off = f32[5,6,64,128]{3,2,1,0:T(8,128)S(1)} collective-permute-done((f32[5,6,64,128]{3,2,1,0:T(8,128)S(1)}, f32[5,6,64,128]{3,2,1,0:T(8,128)S(1)}, u32[]{:S(2)}, u32[]{:S(2)}) %collective-permute-start.7) | collective-permute-done | bytes 983072 | tf_op jit(solution)/shard_map/ppermute | solution.py:240
  76.1 5.3 %second_product.1 = (f32[5,3,64,128]{3,2,1,0:T(8,128)S(1)}, f32[5,3,64,128]{3,2,1,0:T(8,128)S(1)}) custom-call(s32[180]{0:T(256)S(1)} %select_n.118.index_ref, f32[5,6,64,128]{3,2,1,0:T(8,128)S(1)} %first_product.1.p_own, f32[5,6,64,128]{3,2,1,0:T(8,128)} %collective-permute-done.6.p_on, f32[5,6,64,128]{3,2,1,0:T(8,128)S(1)} %collective-permute-done.7.p_off, ...), custom_call_target="tpu_custom_call" | custom-call | flops 1132462080 | bytes 4194304 | tf_op jit(solution)/shard_map/second_product/pallas_call | solution.py:291
  81.4 0.6 collective-permute-start.9
  82.0 8.3 %collective-permute-done.9.refs_1_ = f32[5,3,64,128]{3,2,1,0:T(8,128)S(1)} collective-permute-done((f32[5,3,64,128]{3,2,1,0:T(8,128)S(1)}, f32[5,3,64,128]{3,2,1,0:T(8,128)S(1)}, u32[]{:S(2)}, u32[]{:S(2)}) %collective-permute-start.9) | collective-permute-done | bytes 491552 | tf_op jit(solution)/shard_map/ppermute | solution.py:233
  90.3 1.6 %finish.1 = f32[5,6,64,128]{3,2,1,0:T(8,128)} custom-call(f32[5,6,64,128]{3,2,1,0:T(8,128)S(1)} %copy-done.1, f32[5,3,64,128]{3,2,1,0:T(8,128)S(1)} %get-tuple-element.15.refs_0_, f32[5,3,64,128]{3,2,1,0:T(8,128)S(1)} %collective-permute-done.9.refs_1_), custom_call_target="tpu_custom_call" | custom-call | bytes 3145728 | tf_op jit(solution)/shard_map/finish/pallas_call | solution.py:315
  (53 shorter events, 4.4 us)
Async XLA Ops:
  0.0 1.2 %copy-start = (f32[5,6,64,128]{3,2,1,0:T(8,128)S(1)}, f32[5,6,64,128]{3,2,1,0:T(8,128)}, u32[]{:S(2)}) copy-start(f32[5,6,64,128]{3,2,1,0:T(8,128)} %z_ref.3) | copy-start | bytes 2949124
  1.2 4.0 %copy-start.2 = (f32[5,4,64,128]{3,2,1,0:T(8,128)S(1)}, f32[5,4,64,128]{3,2,1,0:T(8,128)}, u32[]{:S(2)}) copy-start(f32[5,4,64,128]{3,2,1,0:T(8,128)} %j_own.1) | copy-start | bytes 1966084
  1.5 46.4 %copy-start.3 = (f32[5,3,64,128]{3,2,1,0:T(8,128)}, f32[5,3,64,128]{3,2,1,0:T(8,128)S(1)}, u32[]{:S(2)}) copy-start(f32[5,3,64,128]{3,2,1,0:T(8,128)S(1)} %get-tuple-element.12.z_send) | copy-start | bytes 1474564
  1.6 36.3 %collective-permute-start.3 = (f32[5,3,64,128]{3,2,1,0:T(8,128)S(1)}, f32[5,3,64,128]{3,2,1,0:T(8,128)S(1)}, u32[]{:S(2)}, u32[]{:S(2)}) collective-permute-start(f32[5,3,64,128]{3,2,1,0:T(8,128)S(1)} %get-tuple-element.11.z_own), channel_id=1, source_target_pairs={{2,4},{6,8},{10,12},{14,16},{18,20},{22,24},{26,28},{4,2},{8,6},{1... | collective-permute-start | bytes 1474568 | tf_op jit(solution)/shard_map/ppermute | solution.py:240
  3.5 35.7 %collective-permute-start.1 = (f32[5,3,64,128]{3,2,1,0:T(8,128)S(1)}, f32[5,3,64,128]{3,2,1,0:T(8,128)}, u32[]{:S(2)}, u32[]{:S(2)}) collective-permute-start(f32[5,3,64,128]{3,2,1,0:T(8,128)S(1)} %get-tuple-element.11.z_own), channel_id=1, source_target_pairs={{0,2},{2,0},{4,6},{6,4},{8,10},{10,8},{12,14},{14,12},{16,18},{18,... | collective-permute-start | bytes 1474568 | tf_op jit(solution)/shard_map/ppermute | solution.py:236
  5.2 34.0 %collective-permute-start.5 = (f32[5,4,64,128]{3,2,1,0:T(8,128)S(1)}, f32[5,4,64,128]{3,2,1,0:T(8,128)S(1)}, u32[]{:S(2)}, u32[]{:S(2)}) collective-permute-start(f32[5,4,64,128]{3,2,1,0:T(8,128)S(1)} %copy-done.2), channel_id=1, source_target_pairs={{0,1},{1,0},{2,3},{3,2},{4,5},{5,4},{6,7},{7,6},{8,9},{9,8},{10,11... | collective-permute-start | bytes 1966088 | tf_op jit(solution)/shard_map/ppermute | solution.py:233
  5.7 26.8 %collective-permute-start = (f32[5,3,64,128]{3,2,1,0:T(8,128)S(1)}, f32[5,3,64,128]{3,2,1,0:T(8,128)S(1)}, u32[]{:S(2)}, u32[]{:S(2)}) collective-permute-start(f32[5,3,64,128]{3,2,1,0:T(8,128)S(1)} %get-tuple-element.12.z_send), channel_id=1, source_target_pairs={{0,1},{1,0},{2,3},{3,2},{4,5},{5,4},{6,7},{7,6},{8,9},{9,8},{10,11... | collective-permute-start | bytes 1474568 | tf_op jit(solution)/shard_map/ppermute | solution.py:233
  7.2 0.7 copy-start.8
  7.9 0.7 copy-start.7
  32.5 15.5 %collective-permute-start.4 = (f32[5,3,64,128]{3,2,1,0:T(8,128)S(1)}, f32[5,3,64,128]{3,2,1,0:T(8,128)}, u32[]{:S(2)}, u32[]{:S(2)}) collective-permute-start(f32[5,3,64,128]{3,2,1,0:T(8,128)S(1)} %collective-permute-done.z_oth), channel_id=1, source_target_pairs={{2,4},{6,8},{10,12},{14,16},{18,20},{22,24},{26,28},{4,2},{8,6},{1... | collective-permute-start | bytes 1474568 | tf_op jit(solution)/shard_map/ppermute | solution.py:240
  34.4 13.6 %collective-permute-start.2 = (f32[5,3,64,128]{3,2,1,0:T(8,128)S(1)}, f32[5,3,64,128]{3,2,1,0:T(8,128)}, u32[]{:S(2)}, u32[]{:S(2)}) collective-permute-start(f32[5,3,64,128]{3,2,1,0:T(8,128)S(1)} %collective-permute-done.z_oth), channel_id=1, source_target_pairs={{0,2},{2,0},{4,6},{6,4},{8,10},{10,8},{12,14},{14,12},{16,18},{18,... | collective-permute-start | bytes 1474568 | tf_op jit(solution)/shard_map/ppermute | solution.py:236
  37.9 0.8 copy-start.5
  38.7 20.5 %collective-permute-start.8 = (f32[5,3,64,128]{3,2,1,0:T(8,128)S(1)}, f32[5,3,64,128]{3,2,1,0:T(8,128)}, u32[]{:S(2)}, u32[]{:S(2)}) collective-permute-start(f32[5,3,64,128]{3,2,1,0:T(8,128)S(1)} %get-tuple-element.11.z_own), channel_id=1, source_target_pairs={{0,1},{1,0},{2,3},{3,2},{4,5},{5,4},{6,7},{7,6},{8,9},{9,8},{10,11... | collective-permute-start | bytes 1474568 | tf_op jit(solution)/shard_map/ppermute | solution.py:233
  48.0 1.0 %copy-start.6 = (f32[5,3,64,128]{3,2,1,0:T(8,128)S(1)}, f32[5,3,64,128]{3,2,1,0:T(8,128)}, u32[]{:S(2)}) copy-start(f32[5,3,64,128]{3,2,1,0:T(8,128)} %copy-done.5) | copy-start | bytes 1474564
  54.0 5.2 %copy-start.4 = (f32[5,3,64,128]{3,2,1,0:T(8,128)S(1)}, f32[5,3,64,128]{3,2,1,0:T(8,128)}, u32[]{:S(2)}) copy-start(f32[5,3,64,128]{3,2,1,0:T(8,128)} %copy-done.3) | copy-start | bytes 1474564
  54.0 22.1 %collective-permute-start.7 = (f32[5,6,64,128]{3,2,1,0:T(8,128)S(1)}, f32[5,6,64,128]{3,2,1,0:T(8,128)S(1)}, u32[]{:S(2)}, u32[]{:S(2)}) collective-permute-start(f32[5,6,64,128]{3,2,1,0:T(8,128)S(1)} %first_product.1.p_own), channel_id=1, source_target_pairs={{2,4},{6,8},{10,12},{14,16},{18,20},{22,24},{26,28},{4,2},{8,6},{1... | collective-permute-start | bytes 2949128 | tf_op jit(solution)/shard_map/ppermute | solution.py:240
  56.3 19.8 %collective-permute-start.6 = (f32[5,6,64,128]{3,2,1,0:T(8,128)S(1)}, f32[5,6,64,128]{3,2,1,0:T(8,128)}, u32[]{:S(2)}, u32[]{:S(2)}) collective-permute-start(f32[5,6,64,128]{3,2,1,0:T(8,128)S(1)} %first_product.1.p_own), channel_id=1, source_target_pairs={{0,2},{2,0},{4,6},{6,4},{8,10},{10,8},{12,14},{14,12},{16,18},{18,... | collective-permute-start | bytes 2949128 | tf_op jit(solution)/shard_map/ppermute | solution.py:236
  76.1 14.2 %copy-start.1 = (f32[5,6,64,128]{3,2,1,0:T(8,128)S(1)}, f32[5,6,64,128]{3,2,1,0:T(8,128)}, u32[]{:S(2)}) copy-start(f32[5,6,64,128]{3,2,1,0:T(8,128)} %z_ref.3) | copy-start | bytes 2949124
  81.4 8.9 %collective-permute-start.9 = (f32[5,3,64,128]{3,2,1,0:T(8,128)S(1)}, f32[5,3,64,128]{3,2,1,0:T(8,128)S(1)}, u32[]{:S(2)}, u32[]{:S(2)}) collective-permute-start(f32[5,3,64,128]{3,2,1,0:T(8,128)S(1)} %get-tuple-element.16), channel_id=1, source_target_pairs={{0,1},{1,0},{2,3},{3,2},{4,5},{5,4},{6,7},{7,6},{8,9},{9,8},{10,11... | collective-permute-start | bytes 1474568 | tf_op jit(solution)/shard_map/ppermute | solution.py:233

commit v2 on v1

--- a/solution.py
+++ b/solution.py
@@ -8,7 +8,7 @@
 from jax.sharding import PartitionSpec as P
 
 REACH = 5
-CHUNKS = 1
+CHUNKS = 2
 VMEM_BYTES = 32 * 1024 * 1024
 
 
@@ -243,10 +243,12 @@
     z_oth = across(z_send)
     off_own = off_swap(z_own)
     on_own = on_swap(z_own)
-    j_oth = across(hardness_blocks)
+    later, on_own = lax.optimization_barrier((hardness_blocks, on_own))
+    j_oth = across(later)
     off_oth = off_swap(z_oth)
     on_oth = on_swap(z_oth)
-    z_rest = across(z_own)
+    later, on_oth = lax.optimization_barrier((z_own, on_oth))
+    z_rest = across(later)
 
     base, beside_all, own_pattern = patterns_beside(inverse_pattern, rows)
     odd = lax.axis_index("rows") % 2

time: 92.3 us -> 77.2 us (0.84)
  waiting for transfers between devices: 55.4 us -> 25.6 us
  starting transfers between devices: 12.7 us -> 18.1 us
  local copies, waits for them, and re-layouts: 6.9 us -> 11.6 us
  Pallas kernels: 13.7 us -> 17.5 us
    ppermute x4 -> x5, waiting for transfers between devices: 31.3 us -> 12.1 us  [across(): return lax.ppermute(x, 'inner', [(0, 1), (1, 0)])]
    ppermute x3 -> x4, waiting for transfers between devices: 24.1 us -> 13.2 us  [off_swap(): return lax.ppermute(x, 'rows', inside + [(b, a) for a, b in inside])]
    unnamed x19 -> x29, local copies, waits for them, and re-layouts: 4.31 us -> 9.05 us
    ppermute x3 -> x4, starting transfers between devices: 6.18 us -> 9.39 us  [off_swap(): return lax.ppermute(x, 'rows', inside + [(b, a) for a, b in inside])]
    pallas_call x1 -> x2, Pallas kernels: 4.95 us -> 6.92 us  [first(): call(first_product, f32((rows, slots, depth, lanes)), 'first_product', sc...]
    pallas_call x1 -> x2, Pallas kernels: 5.25 us -> 7.02 us  [second(): call(second_product, (f32((rows, pairs, depth, lanes)),) * 2, 'second_pro...]
    ppermute x3 -> x4, starting transfers between devices: 3.45 us -> 5.01 us  [on_swap(): return lax.ppermute(x, 'rows', [(i, i ^ 1) for i in range(count)])]
    ppermute x4 -> x5, starting transfers between devices: 3.1 us -> 3.69 us  [across(): return lax.ppermute(x, 'inner', [(0, 1), (1, 0)])]
  transfers between devices with their start and end apart: 10 -> 13, of which waited for: 4 -> 6; matrix products, arithmetic and copies ran while one was open for 6% -> 7% of each run, Pallas kernels for 7% -> 20%
where the time goes in v2:
time: 77.2 us; the launch traced here: 75.9 us
  waiting for transfers between devices  25.6 us (33%)
  starting transfers between devices  18.1 us (23%)
  Pallas kernels  17.5 us (23%)
  local copies, waits for them, and re-layouts  11.6 us (15%)
  other arithmetic  2.93 us (4%)
    ppermute x4, waiting for transfers between devices, off_swap(): return lax.ppermute(x, 'rows', inside + [(b, a) for a, b in inside])  13.2 us
    ppermute x5, waiting for transfers between devices, across(): return lax.ppermute(x, 'inner', [(0, 1), (1, 0)])  12.1 us
    ppermute x4, starting transfers between devices, off_swap(): return lax.ppermute(x, 'rows', inside + [(b, a) for a, b in inside])  9.39 us
    unnamed x29, local copies, waits for them, and re-layouts  9.05 us
    pallas_call x2, Pallas kernels, second(): call(second_product, (f32((rows, pairs, depth, lanes)),) * 2, 'second_pro...  7.02 us
    pallas_call x2, Pallas kernels, first(): call(first_product, f32((rows, slots, depth, lanes)), 'first_product', sc...  6.92 us
    ppermute x4, starting transfers between devices, on_swap(): return lax.ppermute(x, 'rows', [(i, i ^ 1) for i in range(count)])  5.01 us
    ppermute x5, starting transfers between devices, across(): return lax.ppermute(x, 'inner', [(0, 1), (1, 0)])  3.69 us
  transfers between devices with their start and end apart: 13, of which 6 were waited for; matrix products, arithmetic and copies ran while one was open for 7% of the time, Pallas kernels for 20%

profile of v2, /device:TPU:14, one launch (start us, length us, event | category | flops | bytes accessed | tf_op | source)
XLA Modules:
  0.0 75.9 jit_solution(264000228066238025)
XLA Ops:
  0.0 1.2 %copy-done = f32[5,6,64,128]{3,2,1,0:T(8,128)S(1)} copy-done((f32[5,6,64,128]{3,2,1,0:T(8,128)S(1)}, f32[5,6,64,128]{3,2,1,0:T(8,128)}, u32[]{:S(2)}) %copy-start) | copy-done | bytes 983064
  1.5 1.9 %collective-permute-start.3 = (f32[5,3,64,128]{3,2,1,0:T(8,128)S(1)}, f32[5,3,64,128]{3,2,1,0:T(8,128)S(1)}, u32[]{:S(2)}, u32[]{:S(2)}) collective-permute-start(f32[5,3,64,128]{3,2,1,0:T(8,128)S(1)} %get-tuple-element.22.z_own), channel_id=1, source_target_pairs={{2,4},{6,8},{10,12},{14,16},{18,20},{22,24},{26,28},{4,2},{8,6},{1... | collective-permute-start | bytes 1474568 | tf_op jit(solution)/shard_map/ppermute | solution.py:240
  3.5 1.7 %collective-permute-start.1 = (f32[5,3,64,128]{3,2,1,0:T(8,128)S(1)}, f32[5,3,64,128]{3,2,1,0:T(8,128)S(1)}, u32[]{:S(2)}, u32[]{:S(2)}) collective-permute-start(f32[5,3,64,128]{3,2,1,0:T(8,128)S(1)} %get-tuple-element.22.z_own), channel_id=1, source_target_pairs={{0,2},{2,0},{4,6},{6,4},{8,10},{10,8},{12,14},{14,12},{16,18},{18,... | collective-permute-start | bytes 1474568 | tf_op jit(solution)/shard_map/ppermute | solution.py:236
  10.7 1.5 %collective-permute-start.5 = (f32[5,4,64,128]{3,2,1,0:T(8,128)S(1)}, f32[5,4,64,128]{3,2,1,0:T(8,128)S(1)}, u32[]{:S(2)}, u32[]{:S(2)}) collective-permute-start(f32[5,4,64,128]{3,2,1,0:T(8,128)S(1)} %copy-done.2), channel_id=1, source_target_pairs={{0,1},{1,0},{2,3},{3,2},{4,5},{5,4},{6,7},{7,6},{8,9},{9,8},{10,11... | collective-permute-start | bytes 1966088 | tf_op jit(solution)/shard_map/ppermute | solution.py:233
  12.9 6.4 %collective-permute-done.z_oth = f32[5,3,64,128]{3,2,1,0:T(8,128)S(1)} collective-permute-done((f32[5,3,64,128]{3,2,1,0:T(8,128)S(1)}, f32[5,3,64,128]{3,2,1,0:T(8,128)S(1)}, u32[]{:S(2)}, u32[]{:S(2)}) %collective-permute-start) | collective-permute-done | bytes 491552 | tf_op jit(solution)/shard_map/ppermute | solution.py:233
  19.3 1.9 %collective-permute-start.4 = (f32[5,3,64,128]{3,2,1,0:T(8,128)S(1)}, f32[5,3,64,128]{3,2,1,0:T(8,128)S(1)}, u32[]{:S(2)}, u32[]{:S(2)}) collective-permute-start(f32[5,3,64,128]{3,2,1,0:T(8,128)S(1)} %collective-permute-done.z_oth), channel_id=1, source_target_pairs={{2,4},{6,8},{10,12},{14,16},{18,20},{22,24},{26,28},{4,2},{8,6},{1... | collective-permute-start | bytes 1474568 | tf_op jit(solution)/shard_map/ppermute | solution.py:240
  21.2 1.7 %collective-permute-start.2 = (f32[5,3,64,128]{3,2,1,0:T(8,128)S(1)}, f32[5,3,64,128]{3,2,1,0:T(8,128)}, u32[]{:S(2)}, u32[]{:S(2)}) collective-permute-start(f32[5,3,64,128]{3,2,1,0:T(8,128)S(1)} %collective-permute-done.z_oth), channel_id=1, source_target_pairs={{0,2},{2,0},{4,6},{6,4},{8,10},{10,8},{12,14},{14,12},{16,18},{18,... | collective-permute-start | bytes 1474568 | tf_op jit(solution)/shard_map/ppermute | solution.py:236
  25.0 9.7 %collective-permute-done.4.off_oth = f32[5,3,64,128]{3,2,1,0:T(8,128)S(1)} collective-permute-done((f32[5,3,64,128]{3,2,1,0:T(8,128)S(1)}, f32[5,3,64,128]{3,2,1,0:T(8,128)S(1)}, u32[]{:S(2)}, u32[]{:S(2)}) %collective-permute-start.4) | collective-permute-done | bytes 491552 | tf_op jit(solution)/shard_map/ppermute | solution.py:240
  35.5 1.0 %copy-done.6 = f32[5,3,64,128]{3,2,1,0:T(8,128)S(1)} copy-done((f32[5,3,64,128]{3,2,1,0:T(8,128)S(1)}, f32[5,3,64,128]{3,2,1,0:T(8,128)}, u32[]{:S(2)}) %copy-start.6) | copy-done | bytes 491544
  36.5 1.0 %copy-done.9 = f32[5,3,64,128]{3,2,1,0:T(8,128)S(1)} copy-done((f32[5,3,64,128]{3,2,1,0:T(8,128)S(1)}, f32[5,3,64,128]{3,2,1,0:T(8,128)}, u32[]{:S(2)}) %copy-start.9) | copy-done | bytes 491544
  37.5 3.5 %first_product.2.p_own = f32[5,6,32,128]{3,2,1,0:T(8,128)S(1)} custom-call(s32[120]{0:T(128)S(1)} %select_n.127.index_ref, f32[5,3,64,128]{3,2,1,0:T(8,128)S(1)} %get-tuple-element.22.z_own, f32[5,3,64,128]{3,2,1,0:T(8,128)S(1)} %collective-permute-done.z_oth, f32[5,3,64,128]{3,2,1,0:T(8,128)S(1)} %copy-done.6, ...), custom_call_target="tpu_custom_call" | custom-call | flops 377487360 | bytes 4194304 | tf_op jit(solution)/shard_map/first_product/pallas_call | solution.py:275
  41.0 2.3 %collective-permute-start.7 = (f32[5,6,32,128]{3,2,1,0:T(8,128)S(1)}, f32[5,6,32,128]{3,2,1,0:T(8,128)}, u32[]{:S(2)}, u32[]{:S(2)}) collective-permute-start(f32[5,6,32,128]{3,2,1,0:T(8,128)S(1)} %first_product.2.p_own), channel_id=1, source_target_pairs={{2,4},{6,8},{10,12},{14,16},{18,20},{22,24},{26,28},{4,2},{8,6},{1... | collective-permute-start | bytes 1474568 | tf_op jit(solution)/shard_map/ppermute | solution.py:240
  43.5 1.0 %copy-done.4 = f32[5,3,64,128]{3,2,1,0:T(8,128)S(1)} copy-done((f32[5,3,64,128]{3,2,1,0:T(8,128)S(1)}, f32[5,3,64,128]{3,2,1,0:T(8,128)}, u32[]{:S(2)}) %copy-start.4) | copy-done | bytes 491544
  44.5 3.4 %first_product.3.p_own = f32[5,6,32,128]{3,2,1,0:T(8,128)S(1)} custom-call(s32[120]{0:T(128)S(1)} %select_n.127.index_ref, f32[5,3,64,128]{3,2,1,0:T(8,128)S(1)} %get-tuple-element.22.z_own, f32[5,3,64,128]{3,2,1,0:T(8,128)S(1)} %collective-permute-done.z_oth, f32[5,3,64,128]{3,2,1,0:T(8,128)S(1)} %copy-done.7, ...), custom_call_target="tpu_custom_call" | custom-call | flops 377487360 | bytes 4194304 | tf_op jit(solution)/shard_map/first_product/pallas_call | solution.py:275
  47.9 3.2 %collective-permute-start.10 = (f32[5,6,32,128]{3,2,1,0:T(8,128)S(1)}, f32[5,6,32,128]{3,2,1,0:T(8,128)S(1)}, u32[]{:S(2)}, u32[]{:S(2)}) collective-permute-start(f32[5,6,32,128]{3,2,1,0:T(8,128)S(1)} %first_product.3.p_own), channel_id=1, source_target_pairs={{2,4},{6,8},{10,12},{14,16},{18,20},{22,24},{26,28},{4,2},{8,6},{1... | collective-permute-start | bytes 1474568 | tf_op jit(solution)/shard_map/ppermute | solution.py:240
  51.2 1.6 %collective-permute-start.9 = (f32[5,6,32,128]{3,2,1,0:T(8,128)S(1)}, f32[5,6,32,128]{3,2,1,0:T(8,128)S(1)}, u32[]{:S(2)}, u32[]{:S(2)}) collective-permute-start(f32[5,6,32,128]{3,2,1,0:T(8,128)S(1)} %first_product.3.p_own), channel_id=1, source_target_pairs={{0,2},{2,0},{4,6},{6,4},{8,10},{10,8},{12,14},{14,12},{16,18},{18,... | collective-permute-start | bytes 1474568 | tf_op jit(solution)/shard_map/ppermute | solution.py:236
  54.3 1.0 %copy-done.11 = f32[5,3,64,128]{3,2,1,0:T(8,128)S(1)} copy-done((f32[5,3,64,128]{3,2,1,0:T(8,128)S(1)}, f32[5,3,64,128]{3,2,1,0:T(8,128)}, u32[]{:S(2)}) %copy-start.11) | copy-done | bytes 491544
  55.3 1.6 %left_blocks.1 = (bf16[5,768,128]{2,1,0:T(8,128)(2,1)S(1)}, bf16[5,768,128]{2,1,0:T(8,128)(2,1)S(1)}) custom-call(f32[5,3,64,128]{3,2,1,0:T(8,128)S(1)} %get-tuple-element.22.z_own, f32[5,3,64,128]{3,2,1,0:T(8,128)S(1)} %copy-done.11, f32[5,3,64,128]{3,2,1,0:T(8,128)S(1)} %collective-permute-done.z_oth, f32[5,3,64,128]{3,2,1,0:T(8,128)} %collective-permute-done.8.z_rest), custom_call_target="tpu_custom_call" | custom-call | bytes 4194304 | tf_op jit(solution)/shard_map/left_blocks/pallas_call | solution.py:266
  56.9 3.8 %second_product.2 = (f32[5,3,32,128]{3,2,1,0:T(8,128)S(1)}, f32[5,3,32,128]{3,2,1,0:T(8,128)S(1)}) custom-call(s32[180]{0:T(256)S(1)} %select_n.118.index_ref, f32[5,6,32,128]{3,2,1,0:T(8,128)S(1)} %first_product.2.p_own, f32[5,6,32,128]{3,2,1,0:T(8,128)} %collective-permute-done.6.p_on, f32[5,6,32,128]{3,2,1,0:T(8,128)} %collective-permute-done.7.p_off, ...), custom_call_target="tpu_custom_call" | custom-call | flops 566231040 | bytes 4194304 | tf_op jit(solution)/shard_map/second_product/pallas_call | solution.py:293
  61.3 3.5 %collective-permute-done.10.p_off = f32[5,6,32,128]{3,2,1,0:T(8,128)S(1)} collective-permute-done((f32[5,6,32,128]{3,2,1,0:T(8,128)S(1)}, f32[5,6,32,128]{3,2,1,0:T(8,128)S(1)}, u32[]{:S(2)}, u32[]{:S(2)}) %collective-permute-start.10) | collective-permute-done | bytes 491552 | tf_op jit(solution)/shard_map/ppermute | solution.py:240
  64.9 3.2 %second_product.3 = (f32[5,3,32,128]{3,2,1,0:T(8,128)S(1)}, f32[5,3,32,128]{3,2,1,0:T(8,128)S(1)}) custom-call(s32[180]{0:T(256)S(1)} %select_n.118.index_ref, f32[5,6,32,128]{3,2,1,0:T(8,128)S(1)} %first_product.3.p_own, f32[5,6,32,128]{3,2,1,0:T(8,128)S(1)} %collective-permute-done.9.p_on, f32[5,6,32,128]{3,2,1,0:T(8,128)S(1)} %collective-permute-done.10.p_off, ...), custom_call_target="tpu_custom_call" | custom-call | flops 566231040 | bytes 4194304 | tf_op jit(solution)/shard_map/second_product/pallas_call | solution.py:293
  68.6 1.0 %collective-permute-done.11.refs_2_ = f32[5,3,32,128]{3,2,1,0:T(8,128)S(1)} collective-permute-done((f32[5,3,32,128]{3,2,1,0:T(8,128)S(1)}, f32[5,3,32,128]{3,2,1,0:T(8,128)S(1)}, u32[]{:S(2)}, u32[]{:S(2)}) %collective-permute-start.11) | collective-permute-done | bytes 245792 | tf_op jit(solution)/shard_map/ppermute | solution.py:233
  69.6 4.7 %collective-permute-done.12.refs_3_ = f32[5,3,32,128]{3,2,1,0:T(8,128)S(1)} collective-permute-done((f32[5,3,32,128]{3,2,1,0:T(8,128)S(1)}, f32[5,3,32,128]{3,2,1,0:T(8,128)S(1)}, u32[]{:S(2)}, u32[]{:S(2)}) %collective-permute-start.12) | collective-permute-done | bytes 245792 | tf_op jit(solution)/shard_map/ppermute | solution.py:233
  74.3 1.6 %finish.1 = f32[5,6,64,128]{3,2,1,0:T(8,128)} custom-call(f32[5,6,64,128]{3,2,1,0:T(8,128)S(1)} %copy-done.1, f32[5,3,32,128]{3,2,1,0:T(8,128)S(1)} %get-tuple-element.25.refs_0_, f32[5,3,32,128]{3,2,1,0:T(8,128)S(1)} %get-tuple-element.26.refs_1_, f32[5,3,32,128]{3,2,1,0:T(8,128)S(1)} %collective-permute-done.11.refs_2_, ...), custom_call_target="tpu_custom_call" | custom-call | bytes 3145728 | tf_op jit(solution)/shard_map/finish/pallas_call | solution.py:317
  (71 shorter events, 12.1 us)
Async XLA Ops:
  0.0 1.2 %copy-start = (f32[5,6,64,128]{3,2,1,0:T(8,128)S(1)}, f32[5,6,64,128]{3,2,1,0:T(8,128)}, u32[]{:S(2)}) copy-start(f32[5,6,64,128]{3,2,1,0:T(8,128)} %z_ref.3) | copy-start | bytes 2949124
  1.2 9.5 %copy-start.2 = (f32[5,4,64,128]{3,2,1,0:T(8,128)S(1)}, f32[5,4,64,128]{3,2,1,0:T(8,128)}, u32[]{:S(2)}) copy-start(f32[5,4,64,128]{3,2,1,0:T(8,128)} %j_own.3) | copy-start | bytes 1966084
  1.5 23.4 %collective-permute-start.3 = (f32[5,3,64,128]{3,2,1,0:T(8,128)S(1)}, f32[5,3,64,128]{3,2,1,0:T(8,128)S(1)}, u32[]{:S(2)}, u32[]{:S(2)}) collective-permute-start(f32[5,3,64,128]{3,2,1,0:T(8,128)S(1)} %get-tuple-element.22.z_own), channel_id=1, source_target_pairs={{2,4},{6,8},{10,12},{14,16},{18,20},{22,24},{26,28},{4,2},{8,6},{1... | collective-permute-start | bytes 1474568 | tf_op jit(solution)/shard_map/ppermute | solution.py:240
  3.5 6.4 %collective-permute-start.1 = (f32[5,3,64,128]{3,2,1,0:T(8,128)S(1)}, f32[5,3,64,128]{3,2,1,0:T(8,128)S(1)}, u32[]{:S(2)}, u32[]{:S(2)}) collective-permute-start(f32[5,3,64,128]{3,2,1,0:T(8,128)S(1)} %get-tuple-element.22.z_own), channel_id=1, source_target_pairs={{0,2},{2,0},{4,6},{6,4},{8,10},{10,8},{12,14},{14,12},{16,18},{18,... | collective-permute-start | bytes 1474568 | tf_op jit(solution)/shard_map/ppermute | solution.py:236
  5.2 14.1 %collective-permute-start = (f32[5,3,64,128]{3,2,1,0:T(8,128)S(1)}, f32[5,3,64,128]{3,2,1,0:T(8,128)S(1)}, u32[]{:S(2)}, u32[]{:S(2)}) collective-permute-start(f32[5,3,64,128]{3,2,1,0:T(8,128)S(1)} %get-tuple-element.18.z_send), channel_id=1, source_target_pairs={{0,1},{1,0},{2,3},{3,2},{4,5},{5,4},{6,7},{7,6},{8,9},{9,8},{10,11... | collective-permute-start | bytes 1474568 | tf_op jit(solution)/shard_map/ppermute | solution.py:233
  5.7 0.8 %copy-start.10 = (f32[5,3,64,128]{3,2,1,0:T(8,128)}, f32[5,3,64,128]{3,2,1,0:T(8,128)S(1)}, u32[]{:S(2)}) copy-start(f32[5,3,64,128]{3,2,1,0:T(8,128)S(1)} %get-tuple-element.18.z_send) | copy-start | bytes 1474564
  10.7 24.8 %collective-permute-start.5 = (f32[5,4,64,128]{3,2,1,0:T(8,128)S(1)}, f32[5,4,64,128]{3,2,1,0:T(8,128)S(1)}, u32[]{:S(2)}, u32[]{:S(2)}) collective-permute-start(f32[5,4,64,128]{3,2,1,0:T(8,128)S(1)} %copy-done.2), channel_id=1, source_target_pairs={{0,1},{1,0},{2,3},{3,2},{4,5},{5,4},{6,7},{7,6},{8,9},{9,8},{10,11... | collective-permute-start | bytes 1966088 | tf_op jit(solution)/shard_map/ppermute | solution.py:233
  19.3 15.4 %collective-permute-start.4 = (f32[5,3,64,128]{3,2,1,0:T(8,128)S(1)}, f32[5,3,64,128]{3,2,1,0:T(8,128)S(1)}, u32[]{:S(2)}, u32[]{:S(2)}) collective-permute-start(f32[5,3,64,128]{3,2,1,0:T(8,128)S(1)} %collective-permute-done.z_oth), channel_id=1, source_target_pairs={{2,4},{6,8},{10,12},{14,16},{18,20},{22,24},{26,28},{4,2},{8,6},{1... | collective-permute-start | bytes 1474568 | tf_op jit(solution)/shard_map/ppermute | solution.py:240
  21.2 3.3 %collective-permute-start.2 = (f32[5,3,64,128]{3,2,1,0:T(8,128)S(1)}, f32[5,3,64,128]{3,2,1,0:T(8,128)}, u32[]{:S(2)}, u32[]{:S(2)}) collective-permute-start(f32[5,3,64,128]{3,2,1,0:T(8,128)S(1)} %collective-permute-done.z_oth), channel_id=1, source_target_pairs={{0,2},{2,0},{4,6},{6,4},{8,10},{10,8},{12,14},{14,12},{16,18},{18,... | collective-permute-start | bytes 1474568 | tf_op jit(solution)/shard_map/ppermute | solution.py:236
  24.5 29.8 %collective-permute-start.8 = (f32[5,3,64,128]{3,2,1,0:T(8,128)S(1)}, f32[5,3,64,128]{3,2,1,0:T(8,128)}, u32[]{:S(2)}, u32[]{:S(2)}) collective-permute-start(f32[5,3,64,128]{3,2,1,0:T(8,128)S(1)} %get-tuple-element.22.z_own), channel_id=1, source_target_pairs={{0,1},{1,0},{2,3},{3,2},{4,5},{5,4},{6,7},{7,6},{8,9},{9,8},{10,11... | collective-permute-start | bytes 1474568 | tf_op jit(solution)/shard_map/ppermute | solution.py:233
  25.0 16.0 %copy-start.3 = (f32[5,3,64,128]{3,2,1,0:T(8,128)}, f32[5,3,64,128]{3,2,1,0:T(8,128)S(1)}, u32[]{:S(2)}) copy-start(f32[5,3,64,128]{3,2,1,0:T(8,128)S(1)} %collective-permute-done.3.off_own) | copy-start | bytes 1474564
  34.7 0.8 %copy-start.8 = (f32[5,3,64,128]{3,2,1,0:T(8,128)}, f32[5,3,64,128]{3,2,1,0:T(8,128)S(1)}, u32[]{:S(2)}) copy-start(f32[5,3,64,128]{3,2,1,0:T(8,128)S(1)} %collective-permute-done.4.off_oth) | copy-start | bytes 1474564
  35.5 1.0 %copy-start.6 = (f32[5,3,64,128]{3,2,1,0:T(8,128)S(1)}, f32[5,3,64,128]{3,2,1,0:T(8,128)}, u32[]{:S(2)}) copy-start(f32[5,3,64,128]{3,2,1,0:T(8,128)} %copy-done.5) | copy-start | bytes 1474564
  36.5 1.0 %copy-start.9 = (f32[5,3,64,128]{3,2,1,0:T(8,128)S(1)}, f32[5,3,64,128]{3,2,1,0:T(8,128)}, u32[]{:S(2)}) copy-start(f32[5,3,64,128]{3,2,1,0:T(8,128)} %copy-done.8) | copy-start | bytes 1474564
  37.5 5.9 %copy-start.7 = (f32[5,3,64,128]{3,2,1,0:T(8,128)S(1)}, f32[5,3,64,128]{3,2,1,0:T(8,128)}, u32[]{:S(2)}) copy-start(f32[5,3,64,128]{3,2,1,0:T(8,128)} %copy-done.5) | copy-start | bytes 1474564
  41.0 15.9 %collective-permute-start.7 = (f32[5,6,32,128]{3,2,1,0:T(8,128)S(1)}, f32[5,6,32,128]{3,2,1,0:T(8,128)}, u32[]{:S(2)}, u32[]{:S(2)}) collective-permute-start(f32[5,6,32,128]{3,2,1,0:T(8,128)S(1)} %first_product.2.p_own), channel_id=1, source_target_pairs={{2,4},{6,8},{10,12},{14,16},{18,20},{22,24},{26,28},{4,2},{8,6},{1... | collective-permute-start | bytes 1474568 | tf_op jit(solution)/shard_map/ppermute | solution.py:240
  43.4 13.5 %collective-permute-start.6 = (f32[5,6,32,128]{3,2,1,0:T(8,128)S(1)}, f32[5,6,32,128]{3,2,1,0:T(8,128)}, u32[]{:S(2)}, u32[]{:S(2)}) collective-permute-start(f32[5,6,32,128]{3,2,1,0:T(8,128)S(1)} %first_product.2.p_own), channel_id=1, source_target_pairs={{0,2},{2,0},{4,6},{6,4},{8,10},{10,8},{12,14},{14,12},{16,18},{18,... | collective-permute-start | bytes 1474568 | tf_op jit(solution)/shard_map/ppermute | solution.py:236
  43.5 1.0 %copy-start.4 = (f32[5,3,64,128]{3,2,1,0:T(8,128)S(1)}, f32[5,3,64,128]{3,2,1,0:T(8,128)}, u32[]{:S(2)}) copy-start(f32[5,3,64,128]{3,2,1,0:T(8,128)} %copy-done.3) | copy-start | bytes 1474564
  47.9 17.0 %collective-permute-start.10 = (f32[5,6,32,128]{3,2,1,0:T(8,128)S(1)}, f32[5,6,32,128]{3,2,1,0:T(8,128)S(1)}, u32[]{:S(2)}, u32[]{:S(2)}) collective-permute-start(f32[5,6,32,128]{3,2,1,0:T(8,128)S(1)} %first_product.3.p_own), channel_id=1, source_target_pairs={{2,4},{6,8},{10,12},{14,16},{18,20},{22,24},{26,28},{4,2},{8,6},{1... | collective-permute-start | bytes 1474568 | tf_op jit(solution)/shard_map/ppermute | solution.py:240
  51.2 13.7 %collective-permute-start.9 = (f32[5,6,32,128]{3,2,1,0:T(8,128)S(1)}, f32[5,6,32,128]{3,2,1,0:T(8,128)S(1)}, u32[]{:S(2)}, u32[]{:S(2)}) collective-permute-start(f32[5,6,32,128]{3,2,1,0:T(8,128)S(1)} %first_product.3.p_own), channel_id=1, source_target_pairs={{0,2},{2,0},{4,6},{6,4},{8,10},{10,8},{12,14},{14,12},{16,18},{18,... | collective-permute-start | bytes 1474568 | tf_op jit(solution)/shard_map/ppermute | solution.py:236
  54.3 1.0 %copy-start.11 = (f32[5,3,64,128]{3,2,1,0:T(8,128)S(1)}, f32[5,3,64,128]{3,2,1,0:T(8,128)}, u32[]{:S(2)}) copy-start(f32[5,3,64,128]{3,2,1,0:T(8,128)} %copy-done.10) | copy-start | bytes 1474564
  60.7 13.6 %copy-start.1 = (f32[5,6,64,128]{3,2,1,0:T(8,128)S(1)}, f32[5,6,64,128]{3,2,1,0:T(8,128)}, u32[]{:S(2)}) copy-start(f32[5,6,64,128]{3,2,1,0:T(8,128)} %z_ref.3) | copy-start | bytes 2949124
  60.8 8.9 %collective-permute-start.11 = (f32[5,3,32,128]{3,2,1,0:T(8,128)S(1)}, f32[5,3,32,128]{3,2,1,0:T(8,128)S(1)}, u32[]{:S(2)}, u32[]{:S(2)}) collective-permute-start(f32[5,3,32,128]{3,2,1,0:T(8,128)S(1)} %get-tuple-element.27), channel_id=1, source_target_pairs={{0,1},{1,0},{2,3},{3,2},{4,5},{5,4},{6,7},{7,6},{8,9},{9,8},{10,11... | collective-permute-start | bytes 737288 | tf_op jit(solution)/shard_map/ppermute | solution.py:233
  68.1 6.3 %collective-permute-start.12 = (f32[5,3,32,128]{3,2,1,0:T(8,128)S(1)}, f32[5,3,32,128]{3,2,1,0:T(8,128)S(1)}, u32[]{:S(2)}, u32[]{:S(2)}) collective-permute-start(f32[5,3,32,128]{3,2,1,0:T(8,128)S(1)} %get-tuple-element.28), channel_id=1, source_target_pairs={{0,1},{1,0},{2,3},{3,2},{4,5},{5,4},{6,7},{7,6},{8,9},{9,8},{10,11... | collective-permute-start | bytes 737288 | tf_op jit(solution)/shard_map/ppermute | solution.py:233
  (3 other events, 2.1 us)

commit v3 on v2

--- a/solution.py
+++ b/solution.py
@@ -8,8 +8,8 @@
 from jax.sharding import PartitionSpec as P
 
 REACH = 5
-CHUNKS = 2
-VMEM_BYTES = 32 * 1024 * 1024
+CHUNKS = (32, 32)
+VMEM_BYTES = 14 * 1024 * 1024
 
 
 def with_halo(cells, sides, width):
@@ -85,7 +85,7 @@
     return 2.0 * inverse_blocks - carried
 
 
-def call(body, outs, name, scratch=(), specs=None, flops=0, nbytes=0):
+def call(body, outs, name, scratch=(), specs=None, out_specs=None, flops=0, nbytes=0):
     params = dict(
         out_shape=outs,
         scratch_shapes=list(scratch),
@@ -94,7 +94,9 @@
         cost_estimate=pl.CostEstimate(flops=flops, bytes_accessed=nbytes, transcendentals=0),
     )
     if specs is not None:
-        params.update(grid=(1,), in_specs=specs)
+        params.update(in_specs=specs)
+    if out_specs is not None:
+        params.update(out_specs=out_specs)
     return pl.pallas_call(body, **params)
 
 
@@ -116,15 +118,62 @@
     return high, (x - high.astype(jnp.float32)).astype(jnp.bfloat16)
 
 
-def split_columns(z_ref, own_ref, send_ref):
+def find_blocks(left_ref, pattern_ref, one_ref, two_ref, table):
+    rows = left_ref.shape[0]
+    slots = pattern_ref.shape[1]
+    device = lax.axis_index("rows")
+    first = device * rows
+    last = pattern_ref.shape[0] - 1
+    odd = device % 2
+    width = 2 * REACH + 1
+    none = 3 * rows * slots
+
+    @pl.loop(0, table.shape[0])
+    def _(n):
+        table[n] = none
+
+    def segment(n):
+        return (2 - odd, 0, 1 + odd)[n]
+
+    for n in range(3):
+        base = segment(n) * rows
+
+        @pl.loop(0, rows)
+        def _(r):
+            local = (n - 1) * rows + r
+            row = jnp.clip(first + local, 0, last)
+            for k in range(slots):
+                shift = pattern_ref[row, k] - row + REACH
+                table[(local + rows) * width + shift] = (base + r) * slots + k
+
+    def look_up(i, row, k):
+        column = pattern_ref[first + i, k]
+        shift = column - row + REACH
+        inside = (shift >= 0) & (shift < width)
+        found = table[(row - first + rows) * width + jnp.clip(shift, 0, width - 1)]
+        return jnp.where(inside, found, none)
+
+    @pl.loop(0, rows)
+    def _(i):
+        for count, row_of, out_ref in (
+            (left_ref.shape[1], lambda s: left_ref[i, s], one_ref),
+            (slots, lambda m: pattern_ref[first + i, m], two_ref),
+        ):
+            for s in range(count):
+                row = row_of(s)
+                for k in range(slots):
+                    out_ref[(i * count + s) * slots + k] = look_up(i, row, k)
+
+
+def split_columns(send, z_ref, *refs):
+    out_ref = refs[-1]
     second = lax.axis_index("inner") == 1
-    rows, pairs, half, lanes = own_ref.shape
+    rows, pairs, half, lanes = out_ref.shape
     for i in range(rows):
         for j in range(pairs):
             turned = z_ref[i, 2 * j : 2 * j + 2].reshape(2 * half, lanes).T
             top, bottom = turned[:half], turned[half:]
-            own_ref[i, j] = jnp.where(second, bottom, top)
-            send_ref[i, j] = jnp.where(second, top, bottom)
+            out_ref[i, j] = jnp.where(second, top, bottom) if send else jnp.where(second, bottom, top)
 
 
 def gather_dot(index_ref, i, right_slots, out_slots, high_ref, low_ref, lhs_high, lhs_low, right, dims):
@@ -146,32 +195,70 @@
     )
 
 
-def first_product(index_ref, z_own, z_oth, on_own, on_oth, off_own, off_oth, j_own, j_oth, p_ref,
-                  z_high, z_low, j_high, j_low, lhs_high, lhs_low):
-    second = lax.axis_index("inner") == 1
-    rows, pairs, depth, lanes = z_own.shape
-    for g, (own, oth) in enumerate(((z_own, z_oth), (on_own, on_oth), (off_own, off_oth))):
+def turn_lanes(x):
+    return jnp.where(lax.axis_index("inner") == 1, swapped(x), x)
+
+
+def left_rows(j_ref, high_ref, low_ref):
+    for i in range(j_ref.shape[0]):
+        for s in range(j_ref.shape[1]):
+            place = (i, slice(None), pl.ds(s * 128, 128))
+            high_ref[place], low_ref[place] = halves(turn_lanes(j_ref[i, s]))
+
+
+def merge_near(z_own, z_oth, on_own, on_oth, high_ref, low_ref):
+    rows, pairs, half, lanes = z_own.shape
+    for g, (own, oth) in enumerate(((z_own, z_oth), (on_own, on_oth))):
         for i in range(rows):
             for j in range(pairs):
+                at = ((g * rows + i) * pairs + j) * 2
                 even, odd = unzip_lanes(own[i, j], oth[i, j])
-                at = ((g * rows + i) * pairs + j) * 2
-                z_high[at], z_low[at] = halves(even)
-                z_high[at + 1], z_low[at + 1] = halves(odd)
-    z_high[z_high.shape[0] - 1] = jnp.zeros(z_high.shape[1:], jnp.bfloat16)
-    z_low[z_low.shape[0] - 1] = jnp.zeros(z_low.shape[1:], jnp.bfloat16)
-    slots, half = j_own.shape[1:3]
+                high_ref[at], low_ref[at] = halves(even)
+                high_ref[at + 1], low_ref[at + 1] = halves(odd)
+
+
+def first_product(index_ref, near_high, near_low, off_own, off_oth, j_own_high, j_own_low, j_oth, *refs):
+    *p_refs, off_in, z_high, z_low, j_high, j_low, lhs_high, lhs_low, sems = refs
+    rows, pairs, half, lanes = off_oth.shape
+    slots = j_oth.shape[1]
+    near = near_high.shape[0]
+    copies = [
+        pltpu.make_async_copy(src, dst, sems.at[n])
+        for n, (src, dst) in enumerate((
+            (off_own, off_in),
+            (near_high, z_high.at[pl.ds(0, near)]),
+            (near_low, z_low.at[pl.ds(0, near)]),
+            (j_own_high, j_high.at[:, pl.ds(0, half)]),
+            (j_own_low, j_low.at[:, pl.ds(0, half)]),
+        ))
+    ]
+    for copy in copies:
+        copy.start()
+    blank = z_high.shape[0] - 1
+    z_high[blank] = jnp.zeros(z_high.shape[1:], jnp.bfloat16)
+    z_low[blank] = jnp.zeros(z_low.shape[1:], jnp.bfloat16)
     for i in range(rows):
         for s in range(slots):
-            for part, source in ((0, j_own), (1, j_oth)):
-                x = source[i, s]
-                place = (i, pl.ds(part * half, half), pl.ds(s * 128, 128))
-                j_high[place], j_low[place] = halves(jnp.where(second, swapped(x), x))
-
-    @pl.loop(0, rows)
-    def _(i):
+            place = (i, pl.ds(half, half), pl.ds(s * 128, 128))
+            j_high[place], j_low[place] = halves(turn_lanes(j_oth[i, s]))
+    copies[0].wait()
+    for i in range(rows):
+        for j in range(pairs):
+            even, odd = unzip_lanes(off_in[i, j], off_oth[i, j])
+            at = near + (i * pairs + j) * 2
+            z_high[at], z_low[at] = halves(even)
+            z_high[at + 1], z_low[at + 1] = halves(odd)
+    for copy in copies[1:]:
+        copy.wait()
+    for i in range(rows):
         total = gather_dot(index_ref, i, slots, 2 * pairs, z_high, z_low, lhs_high, lhs_low,
                            (j_high[i], j_low[i]), ((1,), (1,)))
-        p_ref[i] = total.reshape(p_ref.shape[1:])
+        total = total.reshape(2 * pairs, half, lanes)
+        start = 0
+        for p_ref in p_refs:
+            depth = p_ref.shape[2]
+            p_ref[i] = total[:, start : start + depth]
+            start += depth
 
 
 def left_blocks(z_own, z_send, z_oth, z_rest, high_ref, low_ref):
@@ -184,21 +271,20 @@
                     high_ref[place], low_ref[place] = halves(x)
 
 
-def second_product(index_ref, p_own, p_on, p_off, left_high, left_low, own_ref, send_ref,
+def second_product(index_ref, p_own, p_on, p_off, l_high, l_low, own_ref, send_ref,
                    p_high, p_low, lhs_high, lhs_low):
     rows, slots, depth, lanes = p_own.shape
+    blank = p_high.shape[0] - 1
+    p_high[blank] = jnp.zeros(p_high.shape[1:], jnp.bfloat16)
+    p_low[blank] = jnp.zeros(p_low.shape[1:], jnp.bfloat16)
     for g, source in enumerate((p_own, p_on, p_off)):
         for i in range(rows):
             for k in range(slots):
                 at = (g * rows + i) * slots + k
                 p_high[at], p_low[at] = halves(source[i, k])
-    p_high[p_high.shape[0] - 1] = jnp.zeros(p_high.shape[1:], jnp.bfloat16)
-    p_low[p_low.shape[0] - 1] = jnp.zeros(p_low.shape[1:], jnp.bfloat16)
-
-    @pl.loop(0, rows)
-    def _(i):
+    for i in range(rows):
         total = gather_dot(index_ref, i, slots, slots, p_high, p_low, lhs_high, lhs_low,
-                           (left_high[i], left_low[i]), ((1,), (0,)))
+                           (l_high[i], l_low[i]), ((1,), (0,)))
         total = total.reshape(slots, depth, lanes)
         for j in range(slots // 2):
             own_ref[i, j], send_ref[i, j] = unzip_lanes(total[2 * j], total[2 * j + 1])
@@ -206,16 +292,21 @@
 
 def finish(chunks, z_ref, *refs):
     second = lax.axis_index("inner") == 1
-    own, oth, out_ref = refs[:chunks], refs[chunks : 2 * chunks], refs[-1]
+    own, oth, (out_ref, staged, sems) = refs[:chunks], refs[chunks : 2 * chunks], refs[2 * chunks :]
     rows, slots, half, lanes = z_ref.shape
+    copies = []
     for i in range(rows):
         for j in range(slots // 2):
             stack = jnp.concatenate([ref[i, j] for ref in own + oth], axis=0)
             turned = stack.T
             turned = jnp.where(second, swapped(turned), turned)
-            out_ref[i, 2 * j : 2 * j + 2] = (
+            staged[i, 2 * j : 2 * j + 2] = (
                 2.0 * z_ref[i, 2 * j : 2 * j + 2] - turned.reshape(2, half, lanes)
             )
+        copies.append(pltpu.make_async_copy(staged.at[i], out_ref.at[i], sems.at[i]))
+        copies[-1].start()
+    for copy in copies:
+        copy.wait()
 
 
 def half_shards(hardness_blocks, inverse_blocks, hardness_pattern, inverse_pattern):
@@ -228,6 +319,8 @@
     pack = f32((rows, pairs, half, lanes))
     smem = pl.BlockSpec(memory_space=pltpu.SMEM)
     vmem = pl.BlockSpec(memory_space=pltpu.VMEM)
+    hbm = pl.BlockSpec(memory_space=pltpu.HBM)
+    anywhere = pl.BlockSpec(memory_space=pl.ANY)
 
     def across(x):
         return lax.ppermute(x, "inner", [(0, 1), (1, 0)])
@@ -239,83 +332,89 @@
         inside = [(i, i + 1) for i in range(1, count - 1, 2)]
         return lax.ppermute(x, "rows", inside + [(b, a) for a, b in inside])
 
-    z_own, z_send = call(split_columns, (pack, pack), "split_columns", nbytes=8 << 18)(inverse_blocks)
+    z_send = call(functools.partial(split_columns, True), pack, "split_send", nbytes=6 << 18)(inverse_blocks)
+    z_own = call(
+        functools.partial(split_columns, False), pack, "split_own", specs=[vmem, anywhere], nbytes=6 << 18
+    )(inverse_blocks, z_send)
     z_oth = across(z_send)
     off_own = off_swap(z_own)
     on_own = on_swap(z_own)
-    later, on_own = lax.optimization_barrier((hardness_blocks, on_own))
-    j_oth = across(later)
     off_oth = off_swap(z_oth)
     on_oth = on_swap(z_oth)
-    later, on_oth = lax.optimization_barrier((z_own, on_oth))
+    later, z_oth = lax.optimization_barrier((z_own, z_oth))
     z_rest = across(later)
 
-    base, beside_all, own_pattern = patterns_beside(inverse_pattern, rows)
-    odd = lax.axis_index("rows") % 2
-
-    def flat_index(left_pattern):
-        local, slot, found = match_slots(left_pattern, own_pattern, beside_all, base)
-        offset = local - REACH
-        segment = jnp.where(offset < 0, 2 - odd, jnp.where(offset < rows, 0, 1 + odd))
-        flat = (segment * rows + jnp.where(offset < 0, offset + rows, offset % rows)) * slots + slot
-        return jnp.where(found, flat, 3 * rows * slots).astype(jnp.int32).reshape(-1)
-
-    flat_one = flat_index(hardness_pattern)
-    flat_two = flat_index(own_pattern)
+    inverse_pattern, z_oth = lax.optimization_barrier((inverse_pattern, z_oth))
+    flat_one, flat_two = call(
+        find_blocks,
+        (
+            jax.ShapeDtypeStruct((rows * left_slots * slots,), jnp.int32),
+            jax.ShapeDtypeStruct((rows * slots * slots,), jnp.int32),
+        ),
+        "find_blocks",
+        scratch=[pltpu.SMEM((3 * rows * (2 * REACH + 1),), jnp.int32)],
+        specs=[smem, smem],
+        out_specs=[smem, smem],
+    )(hardness_pattern, inverse_pattern)
+    later, z_own = lax.optimization_barrier((hardness_blocks, z_own))
+    j_oth = across(later)
+
+    later, off_own = lax.optimization_barrier((hardness_blocks, off_own))
+    j_own = call(
+        left_rows, (bf16((rows, half, left_slots * lanes)),) * 2, "left_rows", nbytes=4 << 18
+    )(later)
 
     left = call(
         left_blocks, (bf16((rows, slots * lanes, lanes)),) * 2, "left_blocks", nbytes=16 << 18
     )(z_own, z_send, z_oth, z_rest)
 
-    depth = half // CHUNKS
     blocks = 3 * rows * slots + 1
-
-    def first(c):
-        part = pl.BlockSpec((rows, pairs, depth, lanes), lambda g: (0, 0, c, 0))
-        return call(
-            first_product,
-            f32((rows, slots, depth, lanes)),
-            "first_product",
-            scratch=[
-                pltpu.VMEM((blocks, depth, lanes), jnp.bfloat16),
-                pltpu.VMEM((blocks, depth, lanes), jnp.bfloat16),
-                pltpu.VMEM((rows, lanes, left_slots * lanes), jnp.bfloat16),
-                pltpu.VMEM((rows, lanes, left_slots * lanes), jnp.bfloat16),
-                pltpu.VMEM((slots * depth, left_slots * lanes), jnp.bfloat16),
-                pltpu.VMEM((slots * depth, left_slots * lanes), jnp.bfloat16),
-            ],
-            specs=[smem] + [part] * 6 + [vmem] * 2,
-            flops=6 * rows * left_slots * slots * depth * lanes * lanes,
-            nbytes=16 << 18,
-        )(flat_one, z_own, z_oth, on_own, on_oth, off_own, off_oth, hardness_blocks, j_oth)
+    bf16_buffer = functools.partial(pltpu.VMEM, dtype=jnp.bfloat16)
+
+    near = call(
+        merge_near, (bf16((2 * rows * slots, half, lanes)),) * 2, "merge_near", nbytes=16 << 18
+    )(z_own, z_oth, on_own, on_oth)
+    products = call(
+        first_product,
+        tuple(f32((rows, slots, depth, lanes)) for depth in CHUNKS),
+        "first_product",
+        scratch=[pltpu.VMEM((rows, pairs, half, lanes), jnp.float32)]
+        + [bf16_buffer((blocks, half, lanes))] * 2
+        + [bf16_buffer((rows, lanes, left_slots * lanes))] * 2
+        + [bf16_buffer((slots * half, left_slots * lanes))] * 2
+        + [pltpu.SemaphoreType.DMA((5,))],
+        specs=[smem, hbm, hbm, hbm, vmem, hbm, hbm, vmem],
+        flops=6 * rows * left_slots * slots * half * lanes * lanes,
+        nbytes=16 << 18,
+    )(flat_one, *near, off_own, off_oth, *j_own, j_oth)
+    products = [(p, on_swap(p), off_swap(p)) for p in products]
 
     def second(p, p_on, p_off):
+        depth = p.shape[2]
         return call(
             second_product,
             (f32((rows, pairs, depth, lanes)),) * 2,
             "second_product",
-            scratch=[
-                pltpu.VMEM((blocks, depth, lanes), jnp.bfloat16),
-                pltpu.VMEM((blocks, depth, lanes), jnp.bfloat16),
-                pltpu.VMEM((slots * depth, slots * lanes), jnp.bfloat16),
-                pltpu.VMEM((slots * depth, slots * lanes), jnp.bfloat16),
-            ],
+            scratch=[bf16_buffer((blocks, depth, lanes))] * 2
+            + [bf16_buffer((slots * depth, slots * lanes))] * 2,
             specs=[smem] + [vmem] * 5,
             flops=6 * rows * slots * slots * depth * lanes * lanes,
             nbytes=16 << 18,
         )(flat_two, p, p_on, p_off, *left)
 
-    products = []
-    for c in range(CHUNKS):
-        p = first(c)
-        products.append((p, on_swap(p), off_swap(p)))
     own, oth = [], []
     for p, p_on, p_off in products:
         mine, send = second(p, p_on, p_off)
         own.append(mine)
         oth.append(across(send))
     return call(
-        functools.partial(finish, CHUNKS), f32(inverse_blocks.shape), "finish", nbytes=12 << 18
+        functools.partial(finish, len(CHUNKS)),
+        f32(inverse_blocks.shape),
+        "finish",
+        scratch=[pltpu.VMEM(inverse_blocks.shape, jnp.float32), pltpu.SemaphoreType.DMA((rows,))],
+        specs=[vmem] * (1 + 2 * len(CHUNKS)),
+        out_specs=anywhere,
+        nbytes=12 << 18,
     )(inverse_blocks, *own, *oth)
 
 

time: 77.2 us -> 72.2 us (0.935); the launches traced: 75.9 us -> 71.9 us
  local copies, waits for them, and re-layouts: 11.6 us -> 1.57 us
  waiting for transfers between devices: 25.6 us -> 35.5 us
  other arithmetic: 2.93 us -> 0 us
  starting transfers between devices: 18.1 us -> 16.2 us
  Pallas kernels: 17.5 us -> 18.4 us
    unnamed x29 -> x11, local copies, waits for them, and re-layouts: 9.05 us -> 1.47 us
    ppermute x4, waiting for transfers between devices: 13.2 us -> 18.7 us  [off_swap(): return lax.ppermute(x, 'rows', inside + [(b, a) for a, b in inside])]
    ppermute x5, waiting for transfers between devices: 12.1 us -> 16.8 us  [across(): return lax.ppermute(x, 'inner', [(0, 1), (1, 0)])]
    pallas_call x4 -> x7, Pallas kernels: 8.83 us -> 13.2 us  [the longest x1 4.66 us: half_shards(): call(first_product, tuple((f32((rows, slots, depth, lanes)) for depth in...]
    pallas_call x2, Pallas kernels: 7.02 us -> 4.68 us  [second(): call(second_product, (f32((rows, pairs, depth, lanes)),) * 2, 'second_pro...]
    ppermute x4, starting transfers between devices: 5.01 us -> 3.35 us  [on_swap(): return lax.ppermute(x, 'rows', [(i, i ^ 1) for i in range(count)])]
    reduce_or x2 -> x0, other arithmetic: 1.33 us -> none  [match_slots(): return (local[:, :, None], slot, jnp.any(equal, axis=3))]
    reduce_sum x2 -> x0, other arithmetic: 1.3 us -> none  [match_slots(): jnp.sum(jnp.where(equal, jnp.arange(width, dtype=jnp.int32), 0), axis=3)]
  transfers between devices with their start and end apart: 13 -> 13, of which waited for: 6 -> 8; matrix products, arithmetic and copies ran while one was open for 7% -> 0% of each run, Pallas kernels for 20% -> 23%
where the time goes in v3:
time: 72.2 us; the launch traced here: 71.9 us
  waiting for transfers between devices  35.5 us (49%)
  Pallas kernels  18.4 us (25%)
  starting transfers between devices  16.2 us (22%)
  local copies, waits for them, and re-layouts  1.57 us (2%)
    ppermute x4, waiting for transfers between devices, off_swap(): return lax.ppermute(x, 'rows', inside + [(b, a) for a, b in inside])  18.7 us
    ppermute x5, waiting for transfers between devices, across(): return lax.ppermute(x, 'inner', [(0, 1), (1, 0)])  16.8 us
    ppermute x4, starting transfers between devices, off_swap(): return lax.ppermute(x, 'rows', inside + [(b, a) for a, b in inside])  9.1 us
    pallas_call x2, Pallas kernels, second(): call(second_product, (f32((rows, pairs, depth, lanes)),) * 2, 'second_pro...  4.68 us
    pallas_call x1, Pallas kernels, half_shards(): call(first_product, tuple((f32((rows, slots, depth, lanes)) for depth in...  4.66 us
    pallas_call x1, Pallas kernels, half_shards(): call(find_blocks, (jax.ShapeDtypeStruct((rows * left_slots * slots,), jnp...  4.53 us
    ppermute x5, starting transfers between devices, across(): return lax.ppermute(x, 'inner', [(0, 1), (1, 0)])  3.79 us
    ppermute x4, starting transfers between devices, on_swap(): return lax.ppermute(x, 'rows', [(i, i ^ 1) for i in range(count)])  3.35 us
  transfers between devices with their start and end apart: 13, of which 8 were waited for; matrix products, arithmetic and copies ran while one was open for 0% of the time, Pallas kernels for 23%

profile of v3, /device:TPU:14, one launch (start us, length us, event | category | flops | bytes accessed | tf_op | source)
XLA Modules:
  0.0 71.9 jit_solution(1537664004212589651)
XLA Ops:
  0.0 1.2 %copy-done = f32[5,6,64,128]{3,2,1,0:T(8,128)S(1)} copy-done((f32[5,6,64,128]{3,2,1,0:T(8,128)S(1)}, f32[5,6,64,128]{3,2,1,0:T(8,128)}, u32[]{:S(2)}) %copy-start) | copy-done | bytes 983064
  1.6 0.6 collective-permute-start
  2.6 1.4 %collective-permute-start.5 = (f32[5,4,64,128]{3,2,1,0:T(8,128)S(1)}, f32[5,4,64,128]{3,2,1,0:T(8,128)S(1)}, u32[]{:S(2)}, u32[]{:S(2)}) collective-permute-start(f32[5,4,64,128]{3,2,1,0:T(8,128)S(1)} %copy-done.2), channel_id=1, source_target_pairs={{0,1},{1,0},{2,3},{3,2},{4,5},{5,4},{6,7},{7,6},{8,9},{9,8},{10,11... | collective-permute-start | bytes 1966088 | tf_op jit(solution)/shard_map/ppermute | solution.py:326
  4.1 1.9 %collective-permute-start.3 = (f32[5,3,64,128]{3,2,1,0:T(8,128)S(1)}, f32[5,3,64,128]{3,2,1,0:T(8,128)S(1)}, u32[]{:S(2)}, u32[]{:S(2)}) collective-permute-start(f32[5,3,64,128]{3,2,1,0:T(8,128)S(1)} %split_own.1.z_own), channel_id=1, source_target_pairs={{2,4},{6,8},{10,12},{14,16},{18,20},{22,24},{26,28},{4,2},{8,6},{1... | collective-permute-start | bytes 1474568 | tf_op jit(solution)/shard_map/ppermute | solution.py:333
  6.0 1.7 %collective-permute-start.1 = (f32[5,3,64,128]{3,2,1,0:T(8,128)S(1)}, f32[5,3,64,128]{3,2,1,0:T(8,128)}, u32[]{:S(2)}, u32[]{:S(2)}) collective-permute-start(f32[5,3,64,128]{3,2,1,0:T(8,128)S(1)} %split_own.1.z_own), channel_id=1, source_target_pairs={{0,2},{2,0},{4,6},{6,4},{8,10},{10,8},{12,14},{14,12},{16,18},{18,... | collective-permute-start | bytes 1474568 | tf_op jit(solution)/shard_map/ppermute | solution.py:329
  7.7 8.0 %collective-permute-done.z_oth = f32[5,3,64,128]{3,2,1,0:T(8,128)S(1)} collective-permute-done((f32[5,3,64,128]{3,2,1,0:T(8,128)S(1)}, f32[5,3,64,128]{3,2,1,0:T(8,128)S(1)}, u32[]{:S(2)}, u32[]{:S(2)}) %collective-permute-start) | collective-permute-done | bytes 491552 | tf_op jit(solution)/shard_map/ppermute | solution.py:326
  15.7 2.5 %collective-permute-start.4 = (f32[5,3,64,128]{3,2,1,0:T(8,128)S(1)}, f32[5,3,64,128]{3,2,1,0:T(8,128)}, u32[]{:S(2)}, u32[]{:S(2)}) collective-permute-start(f32[5,3,64,128]{3,2,1,0:T(8,128)S(1)} %collective-permute-done.z_oth), channel_id=1, source_target_pairs={{2,4},{6,8},{10,12},{14,16},{18,20},{22,24},{26,28},{4,2},{8,6},{1... | collective-permute-start | bytes 1474568 | tf_op jit(solution)/shard_map/ppermute | solution.py:333
  18.5 1.0 %collective-permute-done.3.off_own = f32[5,3,64,128]{3,2,1,0:T(8,128)S(1)} collective-permute-done((f32[5,3,64,128]{3,2,1,0:T(8,128)S(1)}, f32[5,3,64,128]{3,2,1,0:T(8,128)S(1)}, u32[]{:S(2)}, u32[]{:S(2)}) %collective-permute-start.3) | collective-permute-done | bytes 491552 | tf_op jit(solution)/shard_map/ppermute | solution.py:333
  19.7 0.6 collective-permute-start.8
  20.4 4.5 %find_blocks.1 = (s32[120]{0:T(128)S(1)}, s32[180]{0:T(256)S(1)}) custom-call(s32[5,4]{1,0:T(8,128)S(1)} %copy.5.left_ref, s32[80,6]{1,0:T(8,128)S(1)} %copy.6.pattern_ref), custom_call_target="tpu_custom_call" | custom-call | tf_op jit(solution)/shard_map/find_blocks/pallas_call | solution.py:348
  24.9 1.8 %merge_near.1 = (bf16[60,64,128]{2,1,0:T(8,128)(2,1)S(1)}, bf16[60,64,128]{2,1,0:T(8,128)(2,1)S(1)}) custom-call(f32[5,3,64,128]{3,2,1,0:T(8,128)S(1)} %split_own.1.z_own, f32[5,3,64,128]{3,2,1,0:T(8,128)S(1)} %collective-permute-done.z_oth, f32[5,3,64,128]{3,2,1,0:T(8,128)} %collective-permute-done.1.on_own, f32[5,3,64,128]{3,2,1,0:T(8,128)} %collective-permute-done.2.on_oth), custom_call_target="tpu_custom_call" | custom-call | bytes 4194304 | tf_op jit(solution)/shard_map/merge_near/pallas_call | solution.py:374
  26.7 3.1 %collective-permute-done.5.j_oth = f32[5,4,64,128]{3,2,1,0:T(8,128)S(1)} collective-permute-done((f32[5,4,64,128]{3,2,1,0:T(8,128)S(1)}, f32[5,4,64,128]{3,2,1,0:T(8,128)S(1)}, u32[]{:S(2)}, u32[]{:S(2)}) %collective-permute-start.5) | collective-permute-done | bytes 655392 | tf_op jit(solution)/shard_map/ppermute | solution.py:326
  29.8 1.5 %collective-permute-done.4.off_oth = f32[5,3,64,128]{3,2,1,0:T(8,128)} collective-permute-done((f32[5,3,64,128]{3,2,1,0:T(8,128)S(1)}, f32[5,3,64,128]{3,2,1,0:T(8,128)}, u32[]{:S(2)}, u32[]{:S(2)}) %collective-permute-start.4) | collective-permute-done | bytes 491552 | tf_op jit(solution)/shard_map/ppermute | solution.py:333
  31.3 4.7 %first_product.1 = (f32[5,6,32,128]{3,2,1,0:T(8,128)S(1)}, f32[5,6,32,128]{3,2,1,0:T(8,128)S(1)}) custom-call(s32[120]{0:T(128)S(1)} %get-tuple-element.30.index_ref, bf16[60,64,128]{2,1,0:T(8,128)(2,1)S(1)} %get-tuple-element.33.near_high, bf16[60,64,128]{2,1,0:T(8,128)(2,1)S(1)} %get-tuple-element.34.near_low, ...), custom_call_target="tpu_custom_call" | custom-call | flops 754974720 | bytes 4194304 | tf_op jit(solution)/shard_map/first_product/pallas_call | solution.py:377
  36.0 2.7 %collective-permute-start.7 = (f32[5,6,32,128]{3,2,1,0:T(8,128)S(1)}, f32[5,6,32,128]{3,2,1,0:T(8,128)S(1)}, u32[]{:S(2)}, u32[]{:S(2)}) collective-permute-start(f32[5,6,32,128]{3,2,1,0:T(8,128)S(1)} %get-tuple-element.40.p_own), channel_id=1, source_target_pairs={{2,4},{6,8},{10,12},{14,16},{18,20},{22,24},{26,28},{4,2},{8,6},{1... | collective-permute-start | bytes 1474568 | tf_op jit(solution)/shard_map/ppermute | solution.py:333
  38.7 1.6 %collective-permute-start.9 = (f32[5,6,32,128]{3,2,1,0:T(8,128)S(1)}, f32[5,6,32,128]{3,2,1,0:T(8,128)S(1)}, u32[]{:S(2)}, u32[]{:S(2)}) collective-permute-start(f32[5,6,32,128]{3,2,1,0:T(8,128)S(1)} %get-tuple-element.45.p_own), channel_id=1, source_target_pairs={{0,2},{2,0},{4,6},{6,4},{8,10},{10,8},{12,14},{14,12},{16,18},{18,... | collective-permute-start | bytes 1474568 | tf_op jit(solution)/shard_map/ppermute | solution.py:329
  40.3 1.9 %collective-permute-start.10 = (f32[5,6,32,128]{3,2,1,0:T(8,128)S(1)}, f32[5,6,32,128]{3,2,1,0:T(8,128)S(1)}, u32[]{:S(2)}, u32[]{:S(2)}) collective-permute-start(f32[5,6,32,128]{3,2,1,0:T(8,128)S(1)} %get-tuple-element.45.p_own), channel_id=1, source_target_pairs={{2,4},{6,8},{10,12},{14,16},{18,20},{22,24},{26,28},{4,2},{8,6},{1... | collective-permute-start | bytes 1474568 | tf_op jit(solution)/shard_map/ppermute | solution.py:333
  42.2 0.6 left_blocks.1
  42.8 13.9 %collective-permute-done.7.p_off = f32[5,6,32,128]{3,2,1,0:T(8,128)S(1)} collective-permute-done((f32[5,6,32,128]{3,2,1,0:T(8,128)S(1)}, f32[5,6,32,128]{3,2,1,0:T(8,128)S(1)}, u32[]{:S(2)}, u32[]{:S(2)}) %collective-permute-start.7) | collective-permute-done | bytes 491552 | tf_op jit(solution)/shard_map/ppermute | solution.py:333
  56.7 2.3 %second_product.2 = (f32[5,3,32,128]{3,2,1,0:T(8,128)S(1)}, f32[5,3,32,128]{3,2,1,0:T(8,128)S(1)}) custom-call(s32[180]{0:T(256)S(1)} %get-tuple-element.29.index_ref, f32[5,6,32,128]{3,2,1,0:T(8,128)S(1)} %get-tuple-element.40.p_own, f32[5,6,32,128]{3,2,1,0:T(8,128)S(1)} %collective-permute-done.6.p_on, f32[5,6,32,128]{3,2,1,0:T(8,128)S(1)} %collective-permute-done.7.p_off, ...), custom_call_target="tpu_custom_call" | custom-call | flops 566231040 | bytes 4194304 | tf_op jit(solution)/shard_map/second_product/pallas_call | solution.py:394
  59.6 2.3 %collective-permute-done.10.p_off = f32[5,6,32,128]{3,2,1,0:T(8,128)S(1)} collective-permute-done((f32[5,6,32,128]{3,2,1,0:T(8,128)S(1)}, f32[5,6,32,128]{3,2,1,0:T(8,128)S(1)}, u32[]{:S(2)}, u32[]{:S(2)}) %collective-permute-start.10) | collective-permute-done | bytes 491552 | tf_op jit(solution)/shard_map/ppermute | solution.py:333
  61.9 2.3 %second_product.3 = (f32[5,3,32,128]{3,2,1,0:T(8,128)S(1)}, f32[5,3,32,128]{3,2,1,0:T(8,128)S(1)}) custom-call(s32[180]{0:T(256)S(1)} %get-tuple-element.29.index_ref, f32[5,6,32,128]{3,2,1,0:T(8,128)S(1)} %get-tuple-element.45.p_own, f32[5,6,32,128]{3,2,1,0:T(8,128)S(1)} %collective-permute-done.9.p_on, ...), custom_call_target="tpu_custom_call" | custom-call | flops 566231040 | bytes 4194304 | tf_op jit(solution)/shard_map/second_product/pallas_call | solution.py:394
  65.3 5.3 %collective-permute-done.12.refs_3_ = f32[5,3,32,128]{3,2,1,0:T(8,128)S(1)} collective-permute-done((f32[5,3,32,128]{3,2,1,0:T(8,128)S(1)}, f32[5,3,32,128]{3,2,1,0:T(8,128)S(1)}, u32[]{:S(2)}, u32[]{:S(2)}) %collective-permute-start.12) | collective-permute-done | bytes 245792 | tf_op jit(solution)/shard_map/ppermute | solution.py:326
  70.5 1.4 %finish.1 = f32[5,6,64,128]{3,2,1,0:T(8,128)} custom-call(f32[5,6,64,128]{3,2,1,0:T(8,128)S(1)} %copy-done.1, f32[5,3,32,128]{3,2,1,0:T(8,128)S(1)} %get-tuple-element.44.refs_0_, f32[5,3,32,128]{3,2,1,0:T(8,128)S(1)} %get-tuple-element.46.refs_1_, f32[5,3,32,128]{3,2,1,0:T(8,128)S(1)} %collective-permute-done.11.refs_2_, ...), custom_call_target="tpu_custom_call" | custom-call | bytes 3145728 | tf_op jit(solution)/shard_map/finish/pallas_call | solution.py:410
  (24 shorter events, 2.9 us)
Async XLA Ops:
  0.0 1.2 %copy-start = (f32[5,6,64,128]{3,2,1,0:T(8,128)S(1)}, f32[5,6,64,128]{3,2,1,0:T(8,128)}, u32[]{:S(2)}) copy-start(f32[5,6,64,128]{3,2,1,0:T(8,128)} %z_ref.5) | copy-start | bytes 2949124
  1.5 1.1 %copy-start.2 = (f32[5,4,64,128]{3,2,1,0:T(8,128)S(1)}, f32[5,4,64,128]{3,2,1,0:T(8,128)}, u32[]{:S(2)}) copy-start(f32[5,4,64,128]{3,2,1,0:T(8,128)} %j_ref) | copy-start | bytes 1966084
  1.6 16.7 %copy-start.4 = (s32[5,4]{0,1:T(4,128)S(1)}, s32[5,4]{0,1:T(4,128)}, u32[]{:S(2)}) copy-start(s32[5,4]{0,1:T(4,128)} %param.6) | copy-start | bytes 244
  1.6 14.2 %collective-permute-start = (f32[5,3,64,128]{3,2,1,0:T(8,128)S(1)}, f32[5,3,64,128]{3,2,1,0:T(8,128)S(1)}, u32[]{:S(2)}, u32[]{:S(2)}) collective-permute-start(f32[5,3,64,128]{3,2,1,0:T(8,128)S(1)} %split_send.1.refs_0_.z_send), channel_id=1, source_target_pairs={{0,1},{1,0},{2,3},{3,2},{4,5},{5,4},{6,7},{7,6},{8,9},{9,8},{10,11... | collective-permute-start | bytes 1474568 | tf_op jit(solution)/shard_map/ppermute | solution.py:326
  2.6 15.8 %copy-start.3 = (s32[80,6]{0,1:T(8,128)S(1)}, s32[80,6]{0,1:T(8,128)}, u32[]{:S(2)}) copy-start(s32[80,6]{0,1:T(8,128)} %param.7) | copy-start | bytes 5764
  2.6 27.1 %collective-permute-start.5 = (f32[5,4,64,128]{3,2,1,0:T(8,128)S(1)}, f32[5,4,64,128]{3,2,1,0:T(8,128)S(1)}, u32[]{:S(2)}, u32[]{:S(2)}) collective-permute-start(f32[5,4,64,128]{3,2,1,0:T(8,128)S(1)} %copy-done.2), channel_id=1, source_target_pairs={{0,1},{1,0},{2,3},{3,2},{4,5},{5,4},{6,7},{7,6},{8,9},{9,8},{10,11... | collective-permute-start | bytes 1966088 | tf_op jit(solution)/shard_map/ppermute | solution.py:326
  4.1 15.4 %collective-permute-start.3 = (f32[5,3,64,128]{3,2,1,0:T(8,128)S(1)}, f32[5,3,64,128]{3,2,1,0:T(8,128)S(1)}, u32[]{:S(2)}, u32[]{:S(2)}) collective-permute-start(f32[5,3,64,128]{3,2,1,0:T(8,128)S(1)} %split_own.1.z_own), channel_id=1, source_target_pairs={{2,4},{6,8},{10,12},{14,16},{18,20},{22,24},{26,28},{4,2},{8,6},{1... | collective-permute-start | bytes 1474568 | tf_op jit(solution)/shard_map/ppermute | solution.py:333
  6.0 18.9 %collective-permute-start.1 = (f32[5,3,64,128]{3,2,1,0:T(8,128)S(1)}, f32[5,3,64,128]{3,2,1,0:T(8,128)}, u32[]{:S(2)}, u32[]{:S(2)}) collective-permute-start(f32[5,3,64,128]{3,2,1,0:T(8,128)S(1)} %split_own.1.z_own), channel_id=1, source_target_pairs={{0,2},{2,0},{4,6},{6,4},{8,10},{10,8},{12,14},{14,12},{16,18},{18,... | collective-permute-start | bytes 1474568 | tf_op jit(solution)/shard_map/ppermute | solution.py:329
  15.7 9.2 %collective-permute-start.2 = (f32[5,3,64,128]{3,2,1,0:T(8,128)S(1)}, f32[5,3,64,128]{3,2,1,0:T(8,128)}, u32[]{:S(2)}, u32[]{:S(2)}) collective-permute-start(f32[5,3,64,128]{3,2,1,0:T(8,128)S(1)} %collective-permute-done.z_oth), channel_id=1, source_target_pairs={{0,2},{2,0},{4,6},{6,4},{8,10},{10,8},{12,14},{14,12},{16,18},{18,... | collective-permute-start | bytes 1474568 | tf_op jit(solution)/shard_map/ppermute | solution.py:329
  15.7 15.5 %collective-permute-start.4 = (f32[5,3,64,128]{3,2,1,0:T(8,128)S(1)}, f32[5,3,64,128]{3,2,1,0:T(8,128)}, u32[]{:S(2)}, u32[]{:S(2)}) collective-permute-start(f32[5,3,64,128]{3,2,1,0:T(8,128)S(1)} %collective-permute-done.z_oth), channel_id=1, source_target_pairs={{2,4},{6,8},{10,12},{14,16},{18,20},{22,24},{26,28},{4,2},{8,6},{1... | collective-permute-start | bytes 1474568 | tf_op jit(solution)/shard_map/ppermute | solution.py:333
  19.7 22.5 %collective-permute-start.8 = (f32[5,3,64,128]{3,2,1,0:T(8,128)S(1)}, f32[5,3,64,128]{3,2,1,0:T(8,128)S(1)}, u32[]{:S(2)}, u32[]{:S(2)}) collective-permute-start(f32[5,3,64,128]{3,2,1,0:T(8,128)S(1)} %split_own.1.z_own), channel_id=1, source_target_pairs={{0,1},{1,0},{2,3},{3,2},{4,5},{5,4},{6,7},{7,6},{8,9},{9,8},{10,11... | collective-permute-start | bytes 1474568 | tf_op jit(solution)/shard_map/ppermute | solution.py:326
  35.9 6.9 %collective-permute-start.6 = (f32[5,6,32,128]{3,2,1,0:T(8,128)S(1)}, f32[5,6,32,128]{3,2,1,0:T(8,128)S(1)}, u32[]{:S(2)}, u32[]{:S(2)}) collective-permute-start(f32[5,6,32,128]{3,2,1,0:T(8,128)S(1)} %get-tuple-element.40.p_own), channel_id=1, source_target_pairs={{0,2},{2,0},{4,6},{6,4},{8,10},{10,8},{12,14},{14,12},{16,18},{18,... | collective-permute-start | bytes 1474568 | tf_op jit(solution)/shard_map/ppermute | solution.py:329
  36.0 20.7 %collective-permute-start.7 = (f32[5,6,32,128]{3,2,1,0:T(8,128)S(1)}, f32[5,6,32,128]{3,2,1,0:T(8,128)S(1)}, u32[]{:S(2)}, u32[]{:S(2)}) collective-permute-start(f32[5,6,32,128]{3,2,1,0:T(8,128)S(1)} %get-tuple-element.40.p_own), channel_id=1, source_target_pairs={{2,4},{6,8},{10,12},{14,16},{18,20},{22,24},{26,28},{4,2},{8,6},{1... | collective-permute-start | bytes 1474568 | tf_op jit(solution)/shard_map/ppermute | solution.py:333
  38.7 20.9 %collective-permute-start.9 = (f32[5,6,32,128]{3,2,1,0:T(8,128)S(1)}, f32[5,6,32,128]{3,2,1,0:T(8,128)S(1)}, u32[]{:S(2)}, u32[]{:S(2)}) collective-permute-start(f32[5,6,32,128]{3,2,1,0:T(8,128)S(1)} %get-tuple-element.45.p_own), channel_id=1, source_target_pairs={{0,2},{2,0},{4,6},{6,4},{8,10},{10,8},{12,14},{14,12},{16,18},{18,... | collective-permute-start | bytes 1474568 | tf_op jit(solution)/shard_map/ppermute | solution.py:329
  40.3 21.6 %collective-permute-start.10 = (f32[5,6,32,128]{3,2,1,0:T(8,128)S(1)}, f32[5,6,32,128]{3,2,1,0:T(8,128)S(1)}, u32[]{:S(2)}, u32[]{:S(2)}) collective-permute-start(f32[5,6,32,128]{3,2,1,0:T(8,128)S(1)} %get-tuple-element.45.p_own), channel_id=1, source_target_pairs={{2,4},{6,8},{10,12},{14,16},{18,20},{22,24},{26,28},{4,2},{8,6},{1... | collective-permute-start | bytes 1474568 | tf_op jit(solution)/shard_map/ppermute | solution.py:333
  59.0 11.5 %copy-start.1 = (f32[5,6,64,128]{3,2,1,0:T(8,128)S(1)}, f32[5,6,64,128]{3,2,1,0:T(8,128)}, u32[]{:S(2)}) copy-start(f32[5,6,64,128]{3,2,1,0:T(8,128)} %z_ref.5) | copy-start | bytes 2949124
  59.0 6.3 %collective-permute-start.11 = (f32[5,3,32,128]{3,2,1,0:T(8,128)S(1)}, f32[5,3,32,128]{3,2,1,0:T(8,128)S(1)}, u32[]{:S(2)}, u32[]{:S(2)}) collective-permute-start(f32[5,3,32,128]{3,2,1,0:T(8,128)S(1)} %get-tuple-element.47), channel_id=1, source_target_pairs={{0,1},{1,0},{2,3},{3,2},{4,5},{5,4},{6,7},{7,6},{8,9},{9,8},{10,11... | collective-permute-start | bytes 737288 | tf_op jit(solution)/shard_map/ppermute | solution.py:326
  64.3 6.3 %collective-permute-start.12 = (f32[5,3,32,128]{3,2,1,0:T(8,128)S(1)}, f32[5,3,32,128]{3,2,1,0:T(8,128)S(1)}, u32[]{:S(2)}, u32[]{:S(2)}) collective-permute-start(f32[5,3,32,128]{3,2,1,0:T(8,128)S(1)} %get-tuple-element.48), channel_id=1, source_target_pairs={{0,1},{1,0},{2,3},{3,2},{4,5},{5,4},{6,7},{7,6},{8,9},{9,8},{10,11... | collective-permute-start | bytes 737288 | tf_op jit(solution)/shard_map/ppermute | solution.py:326

commit v4 on v3

--- a/solution.py
+++ b/solution.py
@@ -128,52 +128,53 @@
     width = 2 * REACH + 1
     none = 3 * rows * slots
 
-    @pl.loop(0, table.shape[0])
+    @pl.loop(0, 3 * rows)
     def _(n):
-        table[n] = none
-
-    def segment(n):
-        return (2 - odd, 0, 1 + odd)[n]
-
-    for n in range(3):
-        base = segment(n) * rows
+        for shift in range(width):
+            table[n * width + shift] = none
+
+    for n, segment in enumerate((2 - odd, 0, 1 + odd)):
 
         @pl.loop(0, rows)
         def _(r):
-            local = (n - 1) * rows + r
-            row = jnp.clip(first + local, 0, last)
-            for k in range(slots):
-                shift = pattern_ref[row, k] - row + REACH
-                table[(local + rows) * width + shift] = (base + r) * slots + k
-
-    def look_up(i, row, k):
-        column = pattern_ref[first + i, k]
-        shift = column - row + REACH
-        inside = (shift >= 0) & (shift < width)
-        found = table[(row - first + rows) * width + jnp.clip(shift, 0, width - 1)]
-        return jnp.where(inside, found, none)
+            local = n * rows + r
+            row = jnp.clip(first + local - rows, 0, last)
+            shifts = [pattern_ref[row, k] - row + REACH for k in range(slots)]
+            for k, shift in enumerate(shifts):
+                table[local * width + shift] = (segment * rows + r) * slots + k
 
     @pl.loop(0, rows)
     def _(i):
-        for count, row_of, out_ref in (
-            (left_ref.shape[1], lambda s: left_ref[i, s], one_ref),
-            (slots, lambda m: pattern_ref[first + i, m], two_ref),
+        columns = [pattern_ref[first + i, k] for k in range(slots)]
+        for count, lefts, out_ref in (
+            (left_ref.shape[1], [left_ref[i, s] for s in range(left_ref.shape[1])], one_ref),
+            (slots, columns, two_ref),
         ):
-            for s in range(count):
-                row = row_of(s)
-                for k in range(slots):
-                    out_ref[(i * count + s) * slots + k] = look_up(i, row, k)
+            found = []
+            for row in lefts:
+                at = (row - first + rows) * width
+                for column in columns:
+                    shift = column - row + REACH
+                    inside = (shift >= 0) & (shift < width)
+                    found.append(jnp.where(inside, table[at + jnp.clip(shift, 0, width - 1)], none))
+            for n, value in enumerate(found):
+                out_ref[i * count * slots + n] = value
 
 
 def split_columns(send, z_ref, *refs):
-    out_ref = refs[-1]
+    out_refs = refs[0 if send else 1 :]
     second = lax.axis_index("inner") == 1
-    rows, pairs, half, lanes = out_ref.shape
-    for i in range(rows):
-        for j in range(pairs):
+    rows, slots, half, lanes = z_ref.shape
+    for i in range(rows):
+        for j in range(slots // 2):
             turned = z_ref[i, 2 * j : 2 * j + 2].reshape(2 * half, lanes).T
             top, bottom = turned[:half], turned[half:]
-            out_ref[i, j] = jnp.where(second, top, bottom) if send else jnp.where(second, bottom, top)
+            part = jnp.where(second, top, bottom) if send else jnp.where(second, bottom, top)
+            start = 0
+            for out_ref in out_refs:
+                depth = out_ref.shape[2]
+                out_ref[i, j] = part[start : start + depth]
+                start += depth
 
 
 def gather_dot(index_ref, i, right_slots, out_slots, high_ref, low_ref, lhs_high, lhs_low, right, dims):
@@ -206,26 +207,30 @@
             high_ref[place], low_ref[place] = halves(turn_lanes(j_ref[i, s]))
 
 
-def merge_near(z_own, z_oth, on_own, on_oth, high_ref, low_ref):
-    rows, pairs, half, lanes = z_own.shape
+def merge_near(start, z_own, z_oth, on_own, on_oth, high_ref, low_ref):
+    rows, pairs, depth, lanes = z_oth.shape
+    mine = pl.ds(start, depth)
     for g, (own, oth) in enumerate(((z_own, z_oth), (on_own, on_oth))):
         for i in range(rows):
             for j in range(pairs):
                 at = ((g * rows + i) * pairs + j) * 2
-                even, odd = unzip_lanes(own[i, j], oth[i, j])
+                even, odd = unzip_lanes(own[i, j, mine], oth[i, j])
                 high_ref[at], low_ref[at] = halves(even)
                 high_ref[at + 1], low_ref[at + 1] = halves(odd)
 
 
-def first_product(index_ref, near_high, near_low, off_own, off_oth, j_own_high, j_own_low, j_oth, *refs):
-    *p_refs, off_in, z_high, z_low, j_high, j_low, lhs_high, lhs_low, sems = refs
-    rows, pairs, half, lanes = off_oth.shape
+def first_product(start, index_ref, near_high, near_low, off_own, off_oth, j_own_high, j_own_low, j_oth, *refs):
+    p_ref, off_in, z_high, z_low, j_high, j_low, lhs_high, lhs_low, sems = refs
+    rows, pairs, _, lanes = off_oth.shape
+    depth = z_high.shape[1]
+    mine = pl.ds(start, depth)
+    half = j_oth.shape[2]
     slots = j_oth.shape[1]
     near = near_high.shape[0]
     copies = [
         pltpu.make_async_copy(src, dst, sems.at[n])
         for n, (src, dst) in enumerate((
-            (off_own, off_in),
+            (off_own.at[:, :, mine], off_in),
             (near_high, z_high.at[pl.ds(0, near)]),
             (near_low, z_low.at[pl.ds(0, near)]),
             (j_own_high, j_high.at[:, pl.ds(0, half)]),
@@ -253,22 +258,20 @@
     for i in range(rows):
         total = gather_dot(index_ref, i, slots, 2 * pairs, z_high, z_low, lhs_high, lhs_low,
                            (j_high[i], j_low[i]), ((1,), (1,)))
-        total = total.reshape(2 * pairs, half, lanes)
-        start = 0
-        for p_ref in p_refs:
-            depth = p_ref.shape[2]
-            p_ref[i] = total[:, start : start + depth]
-            start += depth
-
-
-def left_blocks(z_own, z_send, z_oth, z_rest, high_ref, low_ref):
+        p_ref[i] = total.reshape(2 * pairs, depth, lanes)
+
+
+def left_blocks(chunks, z_own, z_rest, *refs):
+    z_send, z_oth, (high_ref, low_ref) = refs[:chunks], refs[chunks : 2 * chunks], refs[2 * chunks :]
     rows, pairs, half, lanes = z_own.shape
     for i in range(rows):
         for j in range(pairs):
-            for part, (own, oth) in enumerate(((z_own, z_oth), (z_send, z_rest))):
-                for slot, x in enumerate(unzip_lanes(own[i, j], oth[i, j])):
+            oth = jnp.concatenate([ref[i, j] for ref in z_oth], axis=0)
+            send = jnp.concatenate([ref[i, j] for ref in z_send], axis=0)
+            for part, (x, y) in enumerate(((z_own[i, j], oth), (send, z_rest[i, j]))):
+                for slot, block in enumerate(unzip_lanes(x, y)):
                     place = (i, pl.ds((2 * j + slot) * lanes + part * half, half))
-                    high_ref[place], low_ref[place] = halves(x)
+                    high_ref[place], low_ref[place] = halves(block)
 
 
 def second_product(index_ref, p_own, p_on, p_off, l_high, l_low, own_ref, send_ref,
@@ -332,20 +335,7 @@
         inside = [(i, i + 1) for i in range(1, count - 1, 2)]
         return lax.ppermute(x, "rows", inside + [(b, a) for a, b in inside])
 
-    z_send = call(functools.partial(split_columns, True), pack, "split_send", nbytes=6 << 18)(inverse_blocks)
-    z_own = call(
-        functools.partial(split_columns, False), pack, "split_own", specs=[vmem, anywhere], nbytes=6 << 18
-    )(inverse_blocks, z_send)
-    z_oth = across(z_send)
-    off_own = off_swap(z_own)
-    on_own = on_swap(z_own)
-    off_oth = off_swap(z_oth)
-    on_oth = on_swap(z_oth)
-    later, z_oth = lax.optimization_barrier((z_own, z_oth))
-    z_rest = across(later)
-
-    inverse_pattern, z_oth = lax.optimization_barrier((inverse_pattern, z_oth))
-    flat_one, flat_two = call(
+    find = call(
         find_blocks,
         (
             jax.ShapeDtypeStruct((rows * left_slots * slots,), jnp.int32),
@@ -355,41 +345,62 @@
         scratch=[pltpu.SMEM((3 * rows * (2 * REACH + 1),), jnp.int32)],
         specs=[smem, smem],
         out_specs=[smem, smem],
-    )(hardness_pattern, inverse_pattern)
-    later, z_own = lax.optimization_barrier((hardness_blocks, z_own))
+    )
+    take_rows = call(left_rows, (bf16((rows, half, left_slots * lanes)),) * 2, "left_rows")
+    chunks = [f32((rows, pairs, depth, lanes)) for depth in CHUNKS]
+    z_send = call(functools.partial(split_columns, True), tuple(chunks), "split_send")(inverse_blocks)
+    z_own = call(functools.partial(split_columns, False), pack, "split_own", specs=[vmem, anywhere])(
+        inverse_blocks, z_send[0]
+    )
+    z_oth = [across(x) for x in z_send]
+    off_own = off_swap(z_own)
+    z_send = list(z_send)
+    on_own = on_swap(z_own)
+    after = lax.optimization_barrier
+    inverse_pattern, z_own = after((inverse_pattern, z_own))
+    flat_one, flat_two = find(hardness_pattern, inverse_pattern)
+    z_oth[1], flat_one = after((z_oth[1], flat_one))
+    later, flat_one = after((hardness_blocks, flat_one))
     j_oth = across(later)
-
-    later, off_own = lax.optimization_barrier((hardness_blocks, off_own))
-    j_own = call(
-        left_rows, (bf16((rows, half, left_slots * lanes)),) * 2, "left_rows", nbytes=4 << 18
-    )(later)
-
+    off_oth = [off_swap(x) for x in z_oth]
+    on_oth = [on_swap(x) for x in z_oth]
+    later, z_oth[1] = after((z_own, z_oth[1]))
+    z_rest = across(later)
+    later, off_own = after((hardness_blocks, off_own))
+    j_own = list(take_rows(later))
     left = call(
-        left_blocks, (bf16((rows, slots * lanes, lanes)),) * 2, "left_blocks", nbytes=16 << 18
-    )(z_own, z_send, z_oth, z_rest)
+        functools.partial(left_blocks, len(CHUNKS)), (bf16((rows, slots * lanes, lanes)),) * 2, "left_blocks"
+    )(z_own, z_rest, *z_send, *z_oth)
 
     blocks = 3 * rows * slots + 1
     bf16_buffer = functools.partial(pltpu.VMEM, dtype=jnp.bfloat16)
 
-    near = call(
-        merge_near, (bf16((2 * rows * slots, half, lanes)),) * 2, "merge_near", nbytes=16 << 18
-    )(z_own, z_oth, on_own, on_oth)
-    products = call(
-        first_product,
-        tuple(f32((rows, slots, depth, lanes)) for depth in CHUNKS),
-        "first_product",
-        scratch=[pltpu.VMEM((rows, pairs, half, lanes), jnp.float32)]
-        + [bf16_buffer((blocks, half, lanes))] * 2
-        + [bf16_buffer((rows, lanes, left_slots * lanes))] * 2
-        + [bf16_buffer((slots * half, left_slots * lanes))] * 2
-        + [pltpu.SemaphoreType.DMA((5,))],
-        specs=[smem, hbm, hbm, hbm, vmem, hbm, hbm, vmem],
-        flops=6 * rows * left_slots * slots * half * lanes * lanes,
-        nbytes=16 << 18,
-    )(flat_one, *near, off_own, off_oth, *j_own, j_oth)
-    products = [(p, on_swap(p), off_swap(p)) for p in products]
-
-    def second(p, p_on, p_off):
+    def first(start, depth, z_oth, off_oth, on_oth):
+        near = call(
+            functools.partial(merge_near, start), (bf16((2 * rows * slots, depth, lanes)),) * 2, "merge_near"
+        )(z_own, z_oth, on_own, on_oth)
+        return call(
+            functools.partial(first_product, start),
+            f32((rows, slots, depth, lanes)),
+            "first_product",
+            scratch=[pltpu.VMEM((rows, pairs, depth, lanes), jnp.float32)]
+            + [bf16_buffer((blocks, depth, lanes))] * 2
+            + [bf16_buffer((rows, lanes, left_slots * lanes))] * 2
+            + [bf16_buffer((slots * depth, left_slots * lanes))] * 2
+            + [pltpu.SemaphoreType.DMA((5,))],
+            specs=[smem, hbm, hbm, hbm, vmem, hbm, hbm, vmem],
+            flops=6 * rows * left_slots * slots * depth * lanes * lanes,
+            nbytes=16 << 18,
+        )(flat_one, *near, off_own, off_oth, *j_own, j_oth)
+
+    products = []
+    start = 0
+    for depth, *oth in zip(CHUNKS, z_oth, off_oth, on_oth):
+        p = first(start, depth, *oth)
+        products.append((p, off_swap(p), on_swap(p)))
+        start += depth
+
+    def second(p, p_off, p_on):
         depth = p.shape[2]
         return call(
             second_product,
@@ -403,8 +414,8 @@
         )(flat_two, p, p_on, p_off, *left)
 
     own, oth = [], []
-    for p, p_on, p_off in products:
-        mine, send = second(p, p_on, p_off)
+    for p, p_off, p_on in products:
+        mine, send = second(p, p_off, p_on)
         own.append(mine)
         oth.append(across(send))
     return call(

time: 72.2 us -> 67.8 us (0.939)
  waiting for transfers between devices: 35.5 us -> 27.6 us
  starting transfers between devices: 16.2 us -> 20.4 us
    ppermute x5 -> x6, waiting for transfers between devices: 16.8 us -> 9.84 us  [across(): return lax.ppermute(x, 'inner', [(0, 1), (1, 0)])]
    ppermute x4 -> x5, starting transfers between devices: 3.35 us -> 5.45 us  [on_swap(): return lax.ppermute(x, 'rows', [(i, i ^ 1) for i in range(count)])]
    ppermute x4 -> x5, starting transfers between devices: 9.1 us -> 10.7 us  [off_swap(): return lax.ppermute(x, 'rows', inside + [(b, a) for a, b in inside])]
    ppermute x4 -> x5, waiting for transfers between devices: 18.7 us -> 17.7 us  [off_swap(): return lax.ppermute(x, 'rows', inside + [(b, a) for a, b in inside])]
    pallas_call x6 -> x8, Pallas kernels: 12.1 us -> 11.5 us  [the longest x2 5.74 us: first(): call(functools.partial(first_product, start), f32((rows, slots, depth, la...]
    ppermute x5 -> x6, starting transfers between devices: 3.79 us -> 4.31 us  [across(): return lax.ppermute(x, 'inner', [(0, 1), (1, 0)])]
  transfers between devices with their start and end apart: 13 -> 16, of which waited for: 8 -> 9; matrix products, arithmetic and copies ran while one was open for 0% -> 0% of each run, Pallas kernels for 23% -> 24%
where the time goes in v4:
time: 67.8 us; the launch traced here: 67.5 us
  waiting for transfers between devices  27.6 us (41%)
  starting transfers between devices  20.4 us (30%)
  Pallas kernels  17.9 us (26%)
  local copies, waits for them, and re-layouts  1.41 us (2%)
    ppermute x5, waiting for transfers between devices, off_swap(): return lax.ppermute(x, 'rows', inside + [(b, a) for a, b in inside])  17.7 us
    ppermute x5, starting transfers between devices, off_swap(): return lax.ppermute(x, 'rows', inside + [(b, a) for a, b in inside])  10.7 us
    ppermute x6, waiting for transfers between devices, across(): return lax.ppermute(x, 'inner', [(0, 1), (1, 0)])  9.84 us
    pallas_call x2, Pallas kernels, first(): call(functools.partial(first_product, start), f32((rows, slots, depth, la...  5.74 us
    ppermute x5, starting transfers between devices, on_swap(): return lax.ppermute(x, 'rows', [(i, i ^ 1) for i in range(count)])  5.45 us
    pallas_call x2, Pallas kernels, second(): call(second_product, (f32((rows, pairs, depth, lanes)),) * 2, 'second_pro...  4.68 us
    ppermute x6, starting transfers between devices, across(): return lax.ppermute(x, 'inner', [(0, 1), (1, 0)])  4.31 us
    pallas_call x1, Pallas kernels, half_shards(): flat_one, flat_two = find(hardness_pattern, inverse_pattern)  3.98 us
  transfers between devices with their start and end apart: 16, of which 9 were waited for; matrix products, arithmetic and copies ran while one was open for 0% of the time, Pallas kernels for 24%

profile of v4, /device:TPU:14, one launch (start us, length us, event | category | flops | bytes accessed | tf_op | source)
XLA Modules:
  0.0 67.5 jit_solution(12467333496518738123)
XLA Ops:
  0.0 1.2 %copy-done = f32[5,6,64,128]{3,2,1,0:T(8,128)S(1)} copy-done((f32[5,6,64,128]{3,2,1,0:T(8,128)S(1)}, f32[5,6,64,128]{3,2,1,0:T(8,128)}, u32[]{:S(2)}) %copy-start) | copy-done | bytes 983064
  2.1 1.5 %collective-permute-start.1 = (f32[5,3,32,128]{3,2,1,0:T(8,128)S(1)}, f32[5,3,32,128]{3,2,1,0:T(8,128)S(1)}, u32[]{:S(2)}, u32[]{:S(2)}) collective-permute-start(f32[5,3,32,128]{3,2,1,0:T(8,128)S(1)} %get-tuple-element.31.refs_0_), channel_id=1, source_target_pairs={{0,1},{1,0},{2,3},{3,2},{4,5},{5,4},{6,7},{7,6},{8,9},{9,8},{10,11... | collective-permute-start | bytes 737288 | tf_op jit(solution)/shard_map/ppermute | solution.py:329
  4.0 1.9 %collective-permute-start.4 = (f32[5,3,64,128]{3,2,1,0:T(8,128)S(1)}, f32[5,3,64,128]{3,2,1,0:T(8,128)S(1)}, u32[]{:S(2)}, u32[]{:S(2)}) collective-permute-start(f32[5,3,64,128]{3,2,1,0:T(8,128)S(1)} %split_own.1.z_own), channel_id=1, source_target_pairs={{2,4},{6,8},{10,12},{14,16},{18,20},{22,24},{26,28},{4,2},{8,6},{1... | collective-permute-start | bytes 1474568 | tf_op jit(solution)/shard_map/ppermute | solution.py:336
  6.1 4.0 %find_blocks.1 = (s32[120]{0:T(128)S(1)}, s32[180]{0:T(256)S(1)}) custom-call(s32[5,4]{1,0:T(8,128)S(1)} %copy.5.left_ref, s32[80,6]{1,0:T(8,128)S(1)} %copy.6.pattern_ref), custom_call_target="tpu_custom_call" | custom-call | tf_op jit(solution)/shard_map/find_blocks/pallas_call | solution.py:361
  11.0 1.1 %collective-permute-start.2 = (f32[5,3,64,128]{3,2,1,0:T(8,128)S(1)}, f32[5,3,64,128]{3,2,1,0:T(8,128)S(1)}, u32[]{:S(2)}, u32[]{:S(2)}) collective-permute-start(f32[5,3,64,128]{3,2,1,0:T(8,128)S(1)} %split_own.1.z_own), channel_id=1, source_target_pairs={{0,2},{2,0},{4,6},{6,4},{8,10},{10,8},{12,14},{14,12},{16,18},{18,... | collective-permute-start | bytes 1474568 | tf_op jit(solution)/shard_map/ppermute | solution.py:332
  12.1 2.5 %collective-permute-done.1.z_oth.refs_2_ = f32[5,3,32,128]{3,2,1,0:T(8,128)S(1)} collective-permute-done((f32[5,3,32,128]{3,2,1,0:T(8,128)S(1)}, f32[5,3,32,128]{3,2,1,0:T(8,128)S(1)}, u32[]{:S(2)}, u32[]{:S(2)}) %collective-permute-start.1) | collective-permute-done | bytes 245792 | tf_op jit(solution)/shard_map/ppermute | solution.py:329
  14.6 2.6 %collective-permute-start.5 = (f32[5,3,32,128]{3,2,1,0:T(8,128)S(1)}, f32[5,3,32,128]{3,2,1,0:T(8,128)S(1)}, u32[]{:S(2)}, u32[]{:S(2)}) collective-permute-start(f32[5,3,32,128]{3,2,1,0:T(8,128)S(1)} %collective-permute-done.1.z_oth.refs_2_), channel_id=1, source_target_pairs={{2,4},{6,8},{10,12},{14,16},{18,20},{22,24},{26,28},{4,2},{8,6},{1... | collective-permute-start | bytes 737288 | tf_op jit(solution)/shard_map/ppermute | solution.py:336
  17.2 1.1 %collective-permute-start.10 = (f32[5,3,32,128]{3,2,1,0:T(8,128)S(1)}, f32[5,3,32,128]{3,2,1,0:T(8,128)S(1)}, u32[]{:S(2)}, u32[]{:S(2)}) collective-permute-start(f32[5,3,32,128]{3,2,1,0:T(8,128)S(1)} %collective-permute-done.refs_3_.z_oth), channel_id=1, source_target_pairs={{0,2},{2,0},{4,6},{6,4},{8,10},{10,8},{12,14},{14,12},{16,18},{18,... | collective-permute-start | bytes 737288 | tf_op jit(solution)/shard_map/ppermute | solution.py:332
  18.3 1.1 %collective-permute-done.4.off_own = f32[5,3,64,128]{3,2,1,0:T(8,128)S(1)} collective-permute-done((f32[5,3,64,128]{3,2,1,0:T(8,128)S(1)}, f32[5,3,64,128]{3,2,1,0:T(8,128)S(1)}, u32[]{:S(2)}, u32[]{:S(2)}) %collective-permute-start.4) | collective-permute-done | bytes 491552 | tf_op jit(solution)/shard_map/ppermute | solution.py:336
  19.4 2.2 %collective-permute-start.11 = (f32[5,3,32,128]{3,2,1,0:T(8,128)S(1)}, f32[5,3,32,128]{3,2,1,0:T(8,128)S(1)}, u32[]{:S(2)}, u32[]{:S(2)}) collective-permute-start(f32[5,3,32,128]{3,2,1,0:T(8,128)S(1)} %collective-permute-done.refs_3_.z_oth), channel_id=1, source_target_pairs={{2,4},{6,8},{10,12},{14,16},{18,20},{22,24},{26,28},{4,2},{8,6},{1... | collective-permute-start | bytes 737288 | tf_op jit(solution)/shard_map/ppermute | solution.py:336
  22.8 4.6 %collective-permute-done.5.off_oth = f32[5,3,32,128]{3,2,1,0:T(8,128)S(1)} collective-permute-done((f32[5,3,32,128]{3,2,1,0:T(8,128)S(1)}, f32[5,3,32,128]{3,2,1,0:T(8,128)S(1)}, u32[]{:S(2)}, u32[]{:S(2)}) %collective-permute-start.5) | collective-permute-done | bytes 245792 | tf_op jit(solution)/shard_map/ppermute | solution.py:336
  27.4 1.3 %collective-permute-done.6.j_oth = f32[5,4,64,128]{3,2,1,0:T(8,128)S(1)} collective-permute-done((f32[5,4,64,128]{3,2,1,0:T(8,128)S(1)}, f32[5,4,64,128]{3,2,1,0:T(8,128)S(1)}, u32[]{:S(2)}, u32[]{:S(2)}) %collective-permute-start.6) | collective-permute-done | bytes 655392 | tf_op jit(solution)/shard_map/ppermute | solution.py:329
  28.7 2.9 %first_product.2.p_own = f32[5,6,32,128]{3,2,1,0:T(8,128)S(1)} custom-call(s32[120]{0:T(128)S(1)} %get-tuple-element.37.index_ref, bf16[60,32,128]{2,1,0:T(8,128)(2,1)S(1)} %get-tuple-element.39.near_high, bf16[60,32,128]{2,1,0:T(8,128)(2,1)S(1)} %get-tuple-element.40.near_low, f32[5,3,64,128]{3,2,1,0:T(8,128)S(1)} %collective-permute-done.4.off_own, ...), custom_call_target="tpu_custom_call" | custom-call | flops 377487360 | bytes 4194304 | tf_op jit(solution)/shard_map/first_product/pallas_call | solution.py:382
  31.5 2.0 %collective-permute-start.8 = (f32[5,6,32,128]{3,2,1,0:T(8,128)S(1)}, f32[5,6,32,128]{3,2,1,0:T(8,128)S(1)}, u32[]{:S(2)}, u32[]{:S(2)}) collective-permute-start(f32[5,6,32,128]{3,2,1,0:T(8,128)S(1)} %first_product.2.p_own), channel_id=1, source_target_pairs={{2,4},{6,8},{10,12},{14,16},{18,20},{22,24},{26,28},{4,2},{8,6},{1... | collective-permute-start | bytes 1474568 | tf_op jit(solution)/shard_map/ppermute | solution.py:336
  33.5 1.7 %collective-permute-start.7 = (f32[5,6,32,128]{3,2,1,0:T(8,128)S(1)}, f32[5,6,32,128]{3,2,1,0:T(8,128)S(1)}, u32[]{:S(2)}, u32[]{:S(2)}) collective-permute-start(f32[5,6,32,128]{3,2,1,0:T(8,128)S(1)} %first_product.2.p_own), channel_id=1, source_target_pairs={{0,2},{2,0},{4,6},{6,4},{8,10},{10,8},{12,14},{14,12},{16,18},{18,... | collective-permute-start | bytes 1474568 | tf_op jit(solution)/shard_map/ppermute | solution.py:332
  35.6 2.9 %first_product.3.p_own = f32[5,6,32,128]{3,2,1,0:T(8,128)S(1)} custom-call(s32[120]{0:T(128)S(1)} %get-tuple-element.37.index_ref, bf16[60,32,128]{2,1,0:T(8,128)(2,1)S(1)} %get-tuple-element.52.near_high, bf16[60,32,128]{2,1,0:T(8,128)(2,1)S(1)} %get-tuple-element.53.near_low, f32[5,3,64,128]{3,2,1,0:T(8,128)S(1)} %collective-permute-done.4.off_own, ...), custom_call_target="tpu_custom_call" | custom-call | flops 377487360 | bytes 4194304 | tf_op jit(solution)/shard_map/first_product/pallas_call | solution.py:382
  38.4 2.0 %collective-permute-start.13 = (f32[5,6,32,128]{3,2,1,0:T(8,128)S(1)}, f32[5,6,32,128]{3,2,1,0:T(8,128)S(1)}, u32[]{:S(2)}, u32[]{:S(2)}) collective-permute-start(f32[5,6,32,128]{3,2,1,0:T(8,128)S(1)} %first_product.3.p_own), channel_id=1, source_target_pairs={{2,4},{6,8},{10,12},{14,16},{18,20},{22,24},{26,28},{4,2},{8,6},{1... | collective-permute-start | bytes 1474568 | tf_op jit(solution)/shard_map/ppermute | solution.py:336
  40.4 1.6 %collective-permute-start.12 = (f32[5,6,32,128]{3,2,1,0:T(8,128)S(1)}, f32[5,6,32,128]{3,2,1,0:T(8,128)S(1)}, u32[]{:S(2)}, u32[]{:S(2)}) collective-permute-start(f32[5,6,32,128]{3,2,1,0:T(8,128)S(1)} %first_product.3.p_own), channel_id=1, source_target_pairs={{0,2},{2,0},{4,6},{6,4},{8,10},{10,8},{12,14},{14,12},{16,18},{18,... | collective-permute-start | bytes 1474568 | tf_op jit(solution)/shard_map/ppermute | solution.py:332
  42.6 9.7 %collective-permute-done.8.p_off = f32[5,6,32,128]{3,2,1,0:T(8,128)S(1)} collective-permute-done((f32[5,6,32,128]{3,2,1,0:T(8,128)S(1)}, f32[5,6,32,128]{3,2,1,0:T(8,128)S(1)}, u32[]{:S(2)}, u32[]{:S(2)}) %collective-permute-start.8) | collective-permute-done | bytes 491552 | tf_op jit(solution)/shard_map/ppermute | solution.py:336
  52.2 2.3 %second_product.2 = (f32[5,3,32,128]{3,2,1,0:T(8,128)S(1)}, f32[5,3,32,128]{3,2,1,0:T(8,128)S(1)}) custom-call(s32[180]{0:T(256)S(1)} %get-tuple-element.33.index_ref, f32[5,6,32,128]{3,2,1,0:T(8,128)S(1)} %first_product.2.p_own, f32[5,6,32,128]{3,2,1,0:T(8,128)S(1)} %collective-permute-done.7.p_on, f32[5,6,32,128]{3,2,1,0:T(8,128)S(1)} %collective-permute-done.8.p_off, ...), custom_call_target="tpu_custom_call" | custom-call | flops 566231040 | bytes 4194304 | tf_op jit(solution)/shard_map/second_product/pallas_call | solution.py:405
  55.2 2.3 %collective-permute-done.13.p_off = f32[5,6,32,128]{3,2,1,0:T(8,128)S(1)} collective-permute-done((f32[5,6,32,128]{3,2,1,0:T(8,128)S(1)}, f32[5,6,32,128]{3,2,1,0:T(8,128)S(1)}, u32[]{:S(2)}, u32[]{:S(2)}) %collective-permute-start.13) | collective-permute-done | bytes 491552 | tf_op jit(solution)/shard_map/ppermute | solution.py:336
  57.5 2.3 %second_product.3 = (f32[5,3,32,128]{3,2,1,0:T(8,128)S(1)}, f32[5,3,32,128]{3,2,1,0:T(8,128)S(1)}) custom-call(s32[180]{0:T(256)S(1)} %get-tuple-element.33.index_ref, f32[5,6,32,128]{3,2,1,0:T(8,128)S(1)} %first_product.3.p_own, f32[5,6,32,128]{3,2,1,0:T(8,128)S(1)} %collective-permute-done.12.p_on, f32[5,6,32,128]{3,2,1,0:T(8,128)S(1)} %collective-permute-done.13.p_off, ...), custom_call_target="tpu_custom_call" | custom-call | flops 566231040 | bytes 4194304 | tf_op jit(solution)/shard_map/second_product/pallas_call | solution.py:405
  60.8 5.3 %collective-permute-done.15.refs_3_ = f32[5,3,32,128]{3,2,1,0:T(8,128)S(1)} collective-permute-done((f32[5,3,32,128]{3,2,1,0:T(8,128)S(1)}, f32[5,3,32,128]{3,2,1,0:T(8,128)S(1)}, u32[]{:S(2)}, u32[]{:S(2)}) %collective-permute-start.15) | collective-permute-done | bytes 245792 | tf_op jit(solution)/shard_map/ppermute | solution.py:329
  66.1 1.4 %finish.1 = f32[5,6,64,128]{3,2,1,0:T(8,128)} custom-call(f32[5,6,64,128]{3,2,1,0:T(8,128)S(1)} %copy-done.1, f32[5,3,32,128]{3,2,1,0:T(8,128)S(1)} %get-tuple-element.51.refs_0_, f32[5,3,32,128]{3,2,1,0:T(8,128)S(1)} %get-tuple-element.54.refs_1_, f32[5,3,32,128]{3,2,1,0:T(8,128)S(1)} %collective-permute-done.14.refs_2_, ...), custom_call_target="tpu_custom_call" | custom-call | bytes 3145728 | tf_op jit(solution)/shard_map/finish/pallas_call | solution.py:421
  (32 shorter events, 5.9 us)
Async XLA Ops:
  0.0 1.2 %copy-start = (f32[5,6,64,128]{3,2,1,0:T(8,128)S(1)}, f32[5,6,64,128]{3,2,1,0:T(8,128)}, u32[]{:S(2)}) copy-start(f32[5,6,64,128]{3,2,1,0:T(8,128)} %z_ref.5) | copy-start | bytes 2949124
  1.5 8.9 %collective-permute-start = (f32[5,3,32,128]{3,2,1,0:T(8,128)S(1)}, f32[5,3,32,128]{3,2,1,0:T(8,128)S(1)}, u32[]{:S(2)}, u32[]{:S(2)}) collective-permute-start(f32[5,3,32,128]{3,2,1,0:T(8,128)S(1)} %get-tuple-element.34.refs_1_), channel_id=1, source_target_pairs={{0,1},{1,0},{2,3},{3,2},{4,5},{5,4},{6,7},{7,6},{8,9},{9,8},{10,11... | collective-permute-start | bytes 737288 | tf_op jit(solution)/shard_map/ppermute | solution.py:329
  2.1 3.8 %copy-start.4 = (s32[5,4]{0,1:T(4,128)S(1)}, s32[5,4]{0,1:T(4,128)}, u32[]{:S(2)}) copy-start(s32[5,4]{0,1:T(4,128)} %param.6) | copy-start | bytes 244
  2.1 8.3 %copy-start.2 = (f32[5,4,64,128]{3,2,1,0:T(8,128)S(1)}, f32[5,4,64,128]{3,2,1,0:T(8,128)}, u32[]{:S(2)}) copy-start(f32[5,4,64,128]{3,2,1,0:T(8,128)} %j_ref) | copy-start | bytes 1966084
  2.1 12.5 %collective-permute-start.1 = (f32[5,3,32,128]{3,2,1,0:T(8,128)S(1)}, f32[5,3,32,128]{3,2,1,0:T(8,128)S(1)}, u32[]{:S(2)}, u32[]{:S(2)}) collective-permute-start(f32[5,3,32,128]{3,2,1,0:T(8,128)S(1)} %get-tuple-element.31.refs_0_), channel_id=1, source_target_pairs={{0,1},{1,0},{2,3},{3,2},{4,5},{5,4},{6,7},{7,6},{8,9},{9,8},{10,11... | collective-permute-start | bytes 737288 | tf_op jit(solution)/shard_map/ppermute | solution.py:329
  4.0 2.0 %copy-start.3 = (s32[80,6]{0,1:T(8,128)S(1)}, s32[80,6]{0,1:T(8,128)}, u32[]{:S(2)}) copy-start(s32[80,6]{0,1:T(8,128)} %param.7) | copy-start | bytes 5764
  4.0 15.4 %collective-permute-start.4 = (f32[5,3,64,128]{3,2,1,0:T(8,128)S(1)}, f32[5,3,64,128]{3,2,1,0:T(8,128)S(1)}, u32[]{:S(2)}, u32[]{:S(2)}) collective-permute-start(f32[5,3,64,128]{3,2,1,0:T(8,128)S(1)} %split_own.1.z_own), channel_id=1, source_target_pairs={{2,4},{6,8},{10,12},{14,16},{18,20},{22,24},{26,28},{4,2},{8,6},{1... | collective-permute-start | bytes 1474568 | tf_op jit(solution)/shard_map/ppermute | solution.py:336
  10.4 18.2 %collective-permute-start.6 = (f32[5,4,64,128]{3,2,1,0:T(8,128)S(1)}, f32[5,4,64,128]{3,2,1,0:T(8,128)S(1)}, u32[]{:S(2)}, u32[]{:S(2)}) collective-permute-start(f32[5,4,64,128]{3,2,1,0:T(8,128)S(1)} %copy-done.2), channel_id=1, source_target_pairs={{0,1},{1,0},{2,3},{3,2},{4,5},{5,4},{6,7},{7,6},{8,9},{9,8},{10,11... | collective-permute-start | bytes 1966088 | tf_op jit(solution)/shard_map/ppermute | solution.py:329
  11.0 10.9 %collective-permute-start.2 = (f32[5,3,64,128]{3,2,1,0:T(8,128)S(1)}, f32[5,3,64,128]{3,2,1,0:T(8,128)S(1)}, u32[]{:S(2)}, u32[]{:S(2)}) collective-permute-start(f32[5,3,64,128]{3,2,1,0:T(8,128)S(1)} %split_own.1.z_own), channel_id=1, source_target_pairs={{0,2},{2,0},{4,6},{6,4},{8,10},{10,8},{12,14},{14,12},{16,18},{18,... | collective-permute-start | bytes 1474568 | tf_op jit(solution)/shard_map/ppermute | solution.py:332
  14.6 2.6 %collective-permute-start.3 = (f32[5,3,32,128]{3,2,1,0:T(8,128)S(1)}, f32[5,3,32,128]{3,2,1,0:T(8,128)S(1)}, u32[]{:S(2)}, u32[]{:S(2)}) collective-permute-start(f32[5,3,32,128]{3,2,1,0:T(8,128)S(1)} %collective-permute-done.1.z_oth.refs_2_), channel_id=1, source_target_pairs={{0,2},{2,0},{4,6},{6,4},{8,10},{10,8},{12,14},{14,12},{16,18},{18,... | collective-permute-start | bytes 737288 | tf_op jit(solution)/shard_map/ppermute | solution.py:332
  14.6 12.8 %collective-permute-start.5 = (f32[5,3,32,128]{3,2,1,0:T(8,128)S(1)}, f32[5,3,32,128]{3,2,1,0:T(8,128)S(1)}, u32[]{:S(2)}, u32[]{:S(2)}) collective-permute-start(f32[5,3,32,128]{3,2,1,0:T(8,128)S(1)} %collective-permute-done.1.z_oth.refs_2_), channel_id=1, source_target_pairs={{2,4},{6,8},{10,12},{14,16},{18,20},{22,24},{26,28},{4,2},{8,6},{1... | collective-permute-start | bytes 737288 | tf_op jit(solution)/shard_map/ppermute | solution.py:336
  17.2 18.0 %collective-permute-start.10 = (f32[5,3,32,128]{3,2,1,0:T(8,128)S(1)}, f32[5,3,32,128]{3,2,1,0:T(8,128)S(1)}, u32[]{:S(2)}, u32[]{:S(2)}) collective-permute-start(f32[5,3,32,128]{3,2,1,0:T(8,128)S(1)} %collective-permute-done.refs_3_.z_oth), channel_id=1, source_target_pairs={{0,2},{2,0},{4,6},{6,4},{8,10},{10,8},{12,14},{14,12},{16,18},{18,... | collective-permute-start | bytes 737288 | tf_op jit(solution)/shard_map/ppermute | solution.py:332
  19.4 16.2 %collective-permute-start.11 = (f32[5,3,32,128]{3,2,1,0:T(8,128)S(1)}, f32[5,3,32,128]{3,2,1,0:T(8,128)S(1)}, u32[]{:S(2)}, u32[]{:S(2)}) collective-permute-start(f32[5,3,32,128]{3,2,1,0:T(8,128)S(1)} %collective-permute-done.refs_3_.z_oth), channel_id=1, source_target_pairs={{2,4},{6,8},{10,12},{14,16},{18,20},{22,24},{26,28},{4,2},{8,6},{1... | collective-permute-start | bytes 737288 | tf_op jit(solution)/shard_map/ppermute | solution.py:336
  21.9 20.1 %collective-permute-start.9 = (f32[5,3,64,128]{3,2,1,0:T(8,128)S(1)}, f32[5,3,64,128]{3,2,1,0:T(8,128)S(1)}, u32[]{:S(2)}, u32[]{:S(2)}) collective-permute-start(f32[5,3,64,128]{3,2,1,0:T(8,128)S(1)} %split_own.1.z_own), channel_id=1, source_target_pairs={{0,1},{1,0},{2,3},{3,2},{4,5},{5,4},{6,7},{7,6},{8,9},{9,8},{10,11... | collective-permute-start | bytes 1474568 | tf_op jit(solution)/shard_map/ppermute | solution.py:329
  31.5 20.7 %collective-permute-start.8 = (f32[5,6,32,128]{3,2,1,0:T(8,128)S(1)}, f32[5,6,32,128]{3,2,1,0:T(8,128)S(1)}, u32[]{:S(2)}, u32[]{:S(2)}) collective-permute-start(f32[5,6,32,128]{3,2,1,0:T(8,128)S(1)} %first_product.2.p_own), channel_id=1, source_target_pairs={{2,4},{6,8},{10,12},{14,16},{18,20},{22,24},{26,28},{4,2},{8,6},{1... | collective-permute-start | bytes 1474568 | tf_op jit(solution)/shard_map/ppermute | solution.py:336
  33.5 18.7 %collective-permute-start.7 = (f32[5,6,32,128]{3,2,1,0:T(8,128)S(1)}, f32[5,6,32,128]{3,2,1,0:T(8,128)S(1)}, u32[]{:S(2)}, u32[]{:S(2)}) collective-permute-start(f32[5,6,32,128]{3,2,1,0:T(8,128)S(1)} %first_product.2.p_own), channel_id=1, source_target_pairs={{0,2},{2,0},{4,6},{6,4},{8,10},{10,8},{12,14},{14,12},{16,18},{18,... | collective-permute-start | bytes 1474568 | tf_op jit(solution)/shard_map/ppermute | solution.py:332
  38.4 19.0 %collective-permute-start.13 = (f32[5,6,32,128]{3,2,1,0:T(8,128)S(1)}, f32[5,6,32,128]{3,2,1,0:T(8,128)S(1)}, u32[]{:S(2)}, u32[]{:S(2)}) collective-permute-start(f32[5,6,32,128]{3,2,1,0:T(8,128)S(1)} %first_product.3.p_own), channel_id=1, source_target_pairs={{2,4},{6,8},{10,12},{14,16},{18,20},{22,24},{26,28},{4,2},{8,6},{1... | collective-permute-start | bytes 1474568 | tf_op jit(solution)/shard_map/ppermute | solution.py:336
  40.4 17.1 %collective-permute-start.12 = (f32[5,6,32,128]{3,2,1,0:T(8,128)S(1)}, f32[5,6,32,128]{3,2,1,0:T(8,128)S(1)}, u32[]{:S(2)}, u32[]{:S(2)}) collective-permute-start(f32[5,6,32,128]{3,2,1,0:T(8,128)S(1)} %first_product.3.p_own), channel_id=1, source_target_pairs={{0,2},{2,0},{4,6},{6,4},{8,10},{10,8},{12,14},{14,12},{16,18},{18,... | collective-permute-start | bytes 1474568 | tf_op jit(solution)/shard_map/ppermute | solution.py:332
  54.6 11.5 %copy-start.1 = (f32[5,6,64,128]{3,2,1,0:T(8,128)S(1)}, f32[5,6,64,128]{3,2,1,0:T(8,128)}, u32[]{:S(2)}) copy-start(f32[5,6,64,128]{3,2,1,0:T(8,128)} %z_ref.5) | copy-start | bytes 2949124
  54.6 6.3 %collective-permute-start.14 = (f32[5,3,32,128]{3,2,1,0:T(8,128)S(1)}, f32[5,3,32,128]{3,2,1,0:T(8,128)S(1)}, u32[]{:S(2)}, u32[]{:S(2)}) collective-permute-start(f32[5,3,32,128]{3,2,1,0:T(8,128)S(1)} %get-tuple-element.55), channel_id=1, source_target_pairs={{0,1},{1,0},{2,3},{3,2},{4,5},{5,4},{6,7},{7,6},{8,9},{9,8},{10,11... | collective-permute-start | bytes 737288 | tf_op jit(solution)/shard_map/ppermute | solution.py:329
  59.8 6.3 %collective-permute-start.15 = (f32[5,3,32,128]{3,2,1,0:T(8,128)S(1)}, f32[5,3,32,128]{3,2,1,0:T(8,128)S(1)}, u32[]{:S(2)}, u32[]{:S(2)}) collective-permute-start(f32[5,3,32,128]{3,2,1,0:T(8,128)S(1)} %get-tuple-element.56), channel_id=1, source_target_pairs={{0,1},{1,0},{2,3},{3,2},{4,5},{5,4},{6,7},{7,6},{8,9},{9,8},{10,11... | collective-permute-start | bytes 737288 | tf_op jit(solution)/shard_map/ppermute | solution.py:329

commit v5 on v4

--- a/solution.py
+++ b/solution.py
@@ -8,7 +8,8 @@
 from jax.sharding import PartitionSpec as P
 
 REACH = 5
-CHUNKS = (32, 32)
+PARTS = ((32,), (32,))
+CHUNKS = tuple(sum(parts) for parts in PARTS)
 VMEM_BYTES = 14 * 1024 * 1024
 
 
@@ -188,12 +189,10 @@
     dot = functools.partial(
         lax.dot_general, dimension_numbers=(dims, ((), ())), preferred_element_type=jnp.float32
     )
-    right_high, right_low = right
-    return (
-        dot(lhs_high[...], right_low)
-        + dot(lhs_low[...], right_high)
-        + dot(lhs_high[...], right_high)
-    )
+    both, high = right
+    total = dot(lhs_high[...], both)
+    count = total.shape[1] // 2
+    return total[:, :count] + (total[:, count:] + dot(lhs_low[...], high))
 
 
 def turn_lanes(x):
@@ -220,49 +219,44 @@
 
 
 def first_product(start, index_ref, near_high, near_low, off_own, off_oth, j_own_high, j_own_low, j_oth, *refs):
-    p_ref, off_in, z_high, z_low, j_high, j_low, lhs_high, lhs_low, sems = refs
+    *p_refs, off_in, z_high, z_low, j_both, lhs_high, lhs_low, sems = refs
     rows, pairs, _, lanes = off_oth.shape
     depth = z_high.shape[1]
     mine = pl.ds(start, depth)
     half = j_oth.shape[2]
     slots = j_oth.shape[1]
     near = near_high.shape[0]
-    copies = [
-        pltpu.make_async_copy(src, dst, sems.at[n])
-        for n, (src, dst) in enumerate((
-            (off_own.at[:, :, mine], off_in),
-            (near_high, z_high.at[pl.ds(0, near)]),
-            (near_low, z_low.at[pl.ds(0, near)]),
-            (j_own_high, j_high.at[:, pl.ds(0, half)]),
-            (j_own_low, j_low.at[:, pl.ds(0, half)]),
-        ))
-    ]
-    for copy in copies:
-        copy.start()
+    copy = pltpu.make_async_copy(off_own.at[:, :, mine], off_in, sems.at[0])
+    copy.start()
+    z_high[:near], z_low[:near] = near_high[...], near_low[...]
+    j_both[:, :half], j_both[:, 2 * half : 3 * half] = j_own_high[...], j_own_low[...]
     blank = z_high.shape[0] - 1
     z_high[blank] = jnp.zeros(z_high.shape[1:], jnp.bfloat16)
     z_low[blank] = jnp.zeros(z_low.shape[1:], jnp.bfloat16)
     for i in range(rows):
         for s in range(slots):
-            place = (i, pl.ds(half, half), pl.ds(s * 128, 128))
-            j_high[place], j_low[place] = halves(turn_lanes(j_oth[i, s]))
-    copies[0].wait()
+            place = pl.ds(s * 128, 128)
+            j_both[i, half : 2 * half, place], j_both[i, 3 * half :, place] = halves(turn_lanes(j_oth[i, s]))
+    copy.wait()
     for i in range(rows):
         for j in range(pairs):
             even, odd = unzip_lanes(off_in[i, j], off_oth[i, j])
             at = near + (i * pairs + j) * 2
             z_high[at], z_low[at] = halves(even)
             z_high[at + 1], z_low[at + 1] = halves(odd)
-    for copy in copies[1:]:
-        copy.wait()
     for i in range(rows):
         total = gather_dot(index_ref, i, slots, 2 * pairs, z_high, z_low, lhs_high, lhs_low,
-                           (j_high[i], j_low[i]), ((1,), (1,)))
-        p_ref[i] = total.reshape(2 * pairs, depth, lanes)
+                           (j_both[i], j_both[i, : 2 * half]), ((1,), (1,)))
+        total = total.reshape(2 * pairs, depth, lanes)
+        at = 0
+        for p_ref in p_refs:
+            count = p_ref.shape[2]
+            p_ref[i] = total[:, at : at + count]
+            at += count
 
 
 def left_blocks(chunks, z_own, z_rest, *refs):
-    z_send, z_oth, (high_ref, low_ref) = refs[:chunks], refs[chunks : 2 * chunks], refs[2 * chunks :]
+    z_send, z_oth, both_ref = refs[:chunks], refs[chunks : 2 * chunks], refs[-1]
     rows, pairs, half, lanes = z_own.shape
     for i in range(rows):
         for j in range(pairs):
@@ -270,11 +264,11 @@
             send = jnp.concatenate([ref[i, j] for ref in z_send], axis=0)
             for part, (x, y) in enumerate(((z_own[i, j], oth), (send, z_rest[i, j]))):
                 for slot, block in enumerate(unzip_lanes(x, y)):
-                    place = (i, pl.ds((2 * j + slot) * lanes + part * half, half))
-                    high_ref[place], low_ref[place] = halves(block)
-
-
-def second_product(index_ref, p_own, p_on, p_off, l_high, l_low, own_ref, send_ref,
+                    place = pl.ds((2 * j + slot) * lanes + part * half, half)
+                    both_ref[i, place, :lanes], both_ref[i, place, lanes:] = halves(block)
+
+
+def second_product(index_ref, p_own, p_on, p_off, l_both, own_ref, send_ref,
                    p_high, p_low, lhs_high, lhs_low):
     rows, slots, depth, lanes = p_own.shape
     blank = p_high.shape[0] - 1
@@ -287,7 +281,7 @@
                 p_high[at], p_low[at] = halves(source[i, k])
     for i in range(rows):
         total = gather_dot(index_ref, i, slots, slots, p_high, p_low, lhs_high, lhs_low,
-                           (l_high[i], l_low[i]), ((1,), (0,)))
+                           (l_both[i], l_both[i, :, :128]), ((1,), (0,)))
         total = total.reshape(slots, depth, lanes)
         for j in range(slots // 2):
             own_ref[i, j], send_ref[i, j] = unzip_lanes(total[2 * j], total[2 * j + 1])
@@ -369,36 +363,36 @@
     later, off_own = after((hardness_blocks, off_own))
     j_own = list(take_rows(later))
     left = call(
-        functools.partial(left_blocks, len(CHUNKS)), (bf16((rows, slots * lanes, lanes)),) * 2, "left_blocks"
+        functools.partial(left_blocks, len(CHUNKS)), bf16((rows, slots * lanes, 2 * lanes)), "left_blocks"
     )(z_own, z_rest, *z_send, *z_oth)
 
     blocks = 3 * rows * slots + 1
     bf16_buffer = functools.partial(pltpu.VMEM, dtype=jnp.bfloat16)
 
-    def first(start, depth, z_oth, off_oth, on_oth):
+    def first(start, parts, z_oth, off_oth, on_oth):
+        depth = sum(parts)
         near = call(
             functools.partial(merge_near, start), (bf16((2 * rows * slots, depth, lanes)),) * 2, "merge_near"
         )(z_own, z_oth, on_own, on_oth)
         return call(
             functools.partial(first_product, start),
-            f32((rows, slots, depth, lanes)),
+            tuple(f32((rows, slots, part, lanes)) for part in parts),
             "first_product",
             scratch=[pltpu.VMEM((rows, pairs, depth, lanes), jnp.float32)]
             + [bf16_buffer((blocks, depth, lanes))] * 2
-            + [bf16_buffer((rows, lanes, left_slots * lanes))] * 2
+            + [bf16_buffer((rows, 2 * lanes, left_slots * lanes))]
             + [bf16_buffer((slots * depth, left_slots * lanes))] * 2
-            + [pltpu.SemaphoreType.DMA((5,))],
-            specs=[smem, hbm, hbm, hbm, vmem, hbm, hbm, vmem],
+            + [pltpu.SemaphoreType.DMA((1,))],
+            specs=[smem, vmem, vmem, hbm, vmem, vmem, vmem, vmem],
             flops=6 * rows * left_slots * slots * depth * lanes * lanes,
             nbytes=16 << 18,
         )(flat_one, *near, off_own, off_oth, *j_own, j_oth)
 
     products = []
     start = 0
-    for depth, *oth in zip(CHUNKS, z_oth, off_oth, on_oth):
-        p = first(start, depth, *oth)
-        products.append((p, off_swap(p), on_swap(p)))
-        start += depth
+    for parts, *oth in zip(PARTS, z_oth, off_oth, on_oth):
+        products += [(p, off_swap(p), on_swap(p)) for p in first(start, parts, *oth)]
+        start += sum(parts)
 
     def second(p, p_off, p_on):
         depth = p.shape[2]
@@ -408,10 +402,10 @@
             "second_product",
             scratch=[bf16_buffer((blocks, depth, lanes))] * 2
             + [bf16_buffer((slots * depth, slots * lanes))] * 2,
-            specs=[smem] + [vmem] * 5,
+            specs=[smem] + [vmem] * 4,
             flops=6 * rows * slots * slots * depth * lanes * lanes,
             nbytes=16 << 18,
-        )(flat_two, p, p_on, p_off, *left)
+        )(flat_two, p, p_on, p_off, left)
 
     own, oth = [], []
     for p, p_off, p_on in products:
@@ -419,11 +413,11 @@
         own.append(mine)
         oth.append(across(send))
     return call(
-        functools.partial(finish, len(CHUNKS)),
+        functools.partial(finish, len(products)),
         f32(inverse_blocks.shape),
         "finish",
         scratch=[pltpu.VMEM(inverse_blocks.shape, jnp.float32), pltpu.SemaphoreType.DMA((rows,))],
-        specs=[vmem] * (1 + 2 * len(CHUNKS)),
+        specs=[vmem] * (1 + 2 * len(products)),
         out_specs=anywhere,
         nbytes=12 << 18,
     )(inverse_blocks, *own, *oth)

time: 67.8 us -> 66.6 us (0.982)
  Pallas kernels: 17.9 us -> 15.6 us
  waiting for transfers between devices: 27.6 us -> 28.7 us
    pallas_call x4, Pallas kernels: 7.67 us -> 6.07 us  [the longest x2 4.13 us: first(): call(functools.partial(first_product, start), tuple((f32((rows, slots, pa...]
    ppermute x5, waiting for transfers between devices: 17.7 us -> 18.8 us  [off_swap(): return lax.ppermute(x, 'rows', inside + [(b, a) for a, b in inside])]
    pallas_call x2, Pallas kernels: 4.68 us -> 3.98 us  [second(): call(second_product, (f32((rows, pairs, depth, lanes)),) * 2, 'second_pro...]
  transfers between devices with their start and end apart: 16 -> 16, of which waited for: 9 -> 9; matrix products, arithmetic and copies ran while one was open for 0% -> 0% of each run, Pallas kernels for 24% -> 21%
where the time goes in v5:
time: 66.6 us; the launch traced here: 66.3 us
  waiting for transfers between devices  28.7 us (43%)
  starting transfers between devices  20.4 us (31%)
  Pallas kernels  15.6 us (23%)
  local copies, waits for them, and re-layouts  1.41 us (2%)
    ppermute x5, waiting for transfers between devices, off_swap(): return lax.ppermute(x, 'rows', inside + [(b, a) for a, b in inside])  18.8 us
    ppermute x5, starting transfers between devices, off_swap(): return lax.ppermute(x, 'rows', inside + [(b, a) for a, b in inside])  10.6 us
    ppermute x6, waiting for transfers between devices, across(): return lax.ppermute(x, 'inner', [(0, 1), (1, 0)])  9.89 us
    ppermute x5, starting transfers between devices, on_swap(): return lax.ppermute(x, 'rows', [(i, i ^ 1) for i in range(count)])  5.49 us
    ppermute x6, starting transfers between devices, across(): return lax.ppermute(x, 'inner', [(0, 1), (1, 0)])  4.31 us
    pallas_call x2, Pallas kernels, first(): call(functools.partial(first_product, start), tuple((f32((rows, slots, pa...  4.13 us
    pallas_call x1, Pallas kernels, half_shards(): flat_one, flat_two = find(hardness_pattern, inverse_pattern)  3.98 us
    pallas_call x2, Pallas kernels, second(): call(second_product, (f32((rows, pairs, depth, lanes)),) * 2, 'second_pro...  3.98 us
  transfers between devices with their start and end apart: 16, of which 9 were waited for; matrix products, arithmetic and copies ran while one was open for 0% of the time, Pallas kernels for 21%

profile of v5, /device:TPU:14, one launch (start us, length us, event | category | flops | bytes accessed | tf_op | source)
XLA Modules:
  0.0 66.3 jit_solution(6961217090603783596)
XLA Ops:
  0.0 1.2 %copy-done = f32[5,6,64,128]{3,2,1,0:T(8,128)S(1)} copy-done((f32[5,6,64,128]{3,2,1,0:T(8,128)S(1)}, f32[5,6,64,128]{3,2,1,0:T(8,128)}, u32[]{:S(2)}) %copy-start) | copy-done | bytes 983064
  2.1 1.5 %collective-permute-start.1 = (f32[5,3,32,128]{3,2,1,0:T(8,128)S(1)}, f32[5,3,32,128]{3,2,1,0:T(8,128)S(1)}, u32[]{:S(2)}, u32[]{:S(2)}) collective-permute-start(f32[5,3,32,128]{3,2,1,0:T(8,128)S(1)} %get-tuple-element.29.refs_0_), channel_id=1, source_target_pairs={{0,1},{1,0},{2,3},{3,2},{4,5},{5,4},{6,7},{7,6},{8,9},{9,8},{10,11... | collective-permute-start | bytes 737288 | tf_op jit(solution)/shard_map/ppermute | solution.py:323
  4.0 1.9 %collective-permute-start.4 = (f32[5,3,64,128]{3,2,1,0:T(8,128)S(1)}, f32[5,3,64,128]{3,2,1,0:T(8,128)S(1)}, u32[]{:S(2)}, u32[]{:S(2)}) collective-permute-start(f32[5,3,64,128]{3,2,1,0:T(8,128)S(1)} %split_own.1.z_own), channel_id=1, source_target_pairs={{2,4},{6,8},{10,12},{14,16},{18,20},{22,24},{26,28},{4,2},{8,6},{1... | collective-permute-start | bytes 1474568 | tf_op jit(solution)/shard_map/ppermute | solution.py:330
  6.1 4.0 %find_blocks.1 = (s32[120]{0:T(128)S(1)}, s32[180]{0:T(256)S(1)}) custom-call(s32[5,4]{1,0:T(8,128)S(1)} %copy.5.left_ref, s32[80,6]{1,0:T(8,128)S(1)} %copy.6.pattern_ref), custom_call_target="tpu_custom_call" | custom-call | tf_op jit(solution)/shard_map/find_blocks/pallas_call | solution.py:355
  11.0 1.1 %collective-permute-start.2 = (f32[5,3,64,128]{3,2,1,0:T(8,128)S(1)}, f32[5,3,64,128]{3,2,1,0:T(8,128)S(1)}, u32[]{:S(2)}, u32[]{:S(2)}) collective-permute-start(f32[5,3,64,128]{3,2,1,0:T(8,128)S(1)} %split_own.1.z_own), channel_id=1, source_target_pairs={{0,2},{2,0},{4,6},{6,4},{8,10},{10,8},{12,14},{14,12},{16,18},{18,... | collective-permute-start | bytes 1474568 | tf_op jit(solution)/shard_map/ppermute | solution.py:326
  12.1 2.6 %collective-permute-done.1.z_oth.refs_2_ = f32[5,3,32,128]{3,2,1,0:T(8,128)S(1)} collective-permute-done((f32[5,3,32,128]{3,2,1,0:T(8,128)S(1)}, f32[5,3,32,128]{3,2,1,0:T(8,128)S(1)}, u32[]{:S(2)}, u32[]{:S(2)}) %collective-permute-start.1) | collective-permute-done | bytes 245792 | tf_op jit(solution)/shard_map/ppermute | solution.py:323
  14.6 2.6 %collective-permute-start.5 = (f32[5,3,32,128]{3,2,1,0:T(8,128)S(1)}, f32[5,3,32,128]{3,2,1,0:T(8,128)S(1)}, u32[]{:S(2)}, u32[]{:S(2)}) collective-permute-start(f32[5,3,32,128]{3,2,1,0:T(8,128)S(1)} %collective-permute-done.1.z_oth.refs_2_), channel_id=1, source_target_pairs={{2,4},{6,8},{10,12},{14,16},{18,20},{22,24},{26,28},{4,2},{8,6},{1... | collective-permute-start | bytes 737288 | tf_op jit(solution)/shard_map/ppermute | solution.py:330
  17.3 1.1 %collective-permute-start.10 = (f32[5,3,32,128]{3,2,1,0:T(8,128)S(1)}, f32[5,3,32,128]{3,2,1,0:T(8,128)S(1)}, u32[]{:S(2)}, u32[]{:S(2)}) collective-permute-start(f32[5,3,32,128]{3,2,1,0:T(8,128)S(1)} %collective-permute-done.refs_3_.z_oth), channel_id=1, source_target_pairs={{0,2},{2,0},{4,6},{6,4},{8,10},{10,8},{12,14},{14,12},{16,18},{18,... | collective-permute-start | bytes 737288 | tf_op jit(solution)/shard_map/ppermute | solution.py:326
  18.3 1.0 %collective-permute-done.4.off_own = f32[5,3,64,128]{3,2,1,0:T(8,128)S(1)} collective-permute-done((f32[5,3,64,128]{3,2,1,0:T(8,128)S(1)}, f32[5,3,64,128]{3,2,1,0:T(8,128)S(1)}, u32[]{:S(2)}, u32[]{:S(2)}) %collective-permute-start.4) | collective-permute-done | bytes 491552 | tf_op jit(solution)/shard_map/ppermute | solution.py:330
  19.4 2.2 %collective-permute-start.11 = (f32[5,3,32,128]{3,2,1,0:T(8,128)S(1)}, f32[5,3,32,128]{3,2,1,0:T(8,128)S(1)}, u32[]{:S(2)}, u32[]{:S(2)}) collective-permute-start(f32[5,3,32,128]{3,2,1,0:T(8,128)S(1)} %collective-permute-done.refs_3_.z_oth), channel_id=1, source_target_pairs={{2,4},{6,8},{10,12},{14,16},{18,20},{22,24},{26,28},{4,2},{8,6},{1... | collective-permute-start | bytes 737288 | tf_op jit(solution)/shard_map/ppermute | solution.py:330
  22.8 4.7 %collective-permute-done.5.off_oth = f32[5,3,32,128]{3,2,1,0:T(8,128)S(1)} collective-permute-done((f32[5,3,32,128]{3,2,1,0:T(8,128)S(1)}, f32[5,3,32,128]{3,2,1,0:T(8,128)S(1)}, u32[]{:S(2)}, u32[]{:S(2)}) %collective-permute-start.5) | collective-permute-done | bytes 245792 | tf_op jit(solution)/shard_map/ppermute | solution.py:330
  27.4 1.3 %collective-permute-done.6.j_oth = f32[5,4,64,128]{3,2,1,0:T(8,128)S(1)} collective-permute-done((f32[5,4,64,128]{3,2,1,0:T(8,128)S(1)}, f32[5,4,64,128]{3,2,1,0:T(8,128)S(1)}, u32[]{:S(2)}, u32[]{:S(2)}) %collective-permute-start.6) | collective-permute-done | bytes 655392 | tf_op jit(solution)/shard_map/ppermute | solution.py:323
  28.7 2.1 %first_product.2.p_own = f32[5,6,32,128]{3,2,1,0:T(8,128)S(1)} custom-call(s32[120]{0:T(128)S(1)} %get-tuple-element.35.index_ref, bf16[60,32,128]{2,1,0:T(8,128)(2,1)S(1)} %get-tuple-element.37.near_high, bf16[60,32,128]{2,1,0:T(8,128)(2,1)S(1)} %get-tuple-element.38.near_low, f32[5,3,64,128]{3,2,1,0:T(8,128)S(1)} %collective-permute-done.4.off_own, ...), custom_call_target="tpu_custom_call" | custom-call | flops 377487360 | bytes 4194304 | tf_op jit(solution)/shard_map/first_product/pallas_call | solution.py:377
  30.8 2.0 %collective-permute-start.8 = (f32[5,6,32,128]{3,2,1,0:T(8,128)S(1)}, f32[5,6,32,128]{3,2,1,0:T(8,128)S(1)}, u32[]{:S(2)}, u32[]{:S(2)}) collective-permute-start(f32[5,6,32,128]{3,2,1,0:T(8,128)S(1)} %first_product.2.p_own), channel_id=1, source_target_pairs={{2,4},{6,8},{10,12},{14,16},{18,20},{22,24},{26,28},{4,2},{8,6},{1... | collective-permute-start | bytes 1474568 | tf_op jit(solution)/shard_map/ppermute | solution.py:330
  32.7 1.7 %collective-permute-start.7 = (f32[5,6,32,128]{3,2,1,0:T(8,128)S(1)}, f32[5,6,32,128]{3,2,1,0:T(8,128)S(1)}, u32[]{:S(2)}, u32[]{:S(2)}) collective-permute-start(f32[5,6,32,128]{3,2,1,0:T(8,128)S(1)} %first_product.2.p_own), channel_id=1, source_target_pairs={{0,2},{2,0},{4,6},{6,4},{8,10},{10,8},{12,14},{14,12},{16,18},{18,... | collective-permute-start | bytes 1474568 | tf_op jit(solution)/shard_map/ppermute | solution.py:326
  34.8 2.1 %first_product.3.p_own = f32[5,6,32,128]{3,2,1,0:T(8,128)S(1)} custom-call(s32[120]{0:T(128)S(1)} %get-tuple-element.35.index_ref, bf16[60,32,128]{2,1,0:T(8,128)(2,1)S(1)} %get-tuple-element.48.near_high, bf16[60,32,128]{2,1,0:T(8,128)(2,1)S(1)} %get-tuple-element.49.near_low, f32[5,3,64,128]{3,2,1,0:T(8,128)S(1)} %collective-permute-done.4.off_own, ...), custom_call_target="tpu_custom_call" | custom-call | flops 377487360 | bytes 4194304 | tf_op jit(solution)/shard_map/first_product/pallas_call | solution.py:377
  36.9 2.0 %collective-permute-start.13 = (f32[5,6,32,128]{3,2,1,0:T(8,128)S(1)}, f32[5,6,32,128]{3,2,1,0:T(8,128)S(1)}, u32[]{:S(2)}, u32[]{:S(2)}) collective-permute-start(f32[5,6,32,128]{3,2,1,0:T(8,128)S(1)} %first_product.3.p_own), channel_id=1, source_target_pairs={{2,4},{6,8},{10,12},{14,16},{18,20},{22,24},{26,28},{4,2},{8,6},{1... | collective-permute-start | bytes 1474568 | tf_op jit(solution)/shard_map/ppermute | solution.py:330
  38.8 1.6 %collective-permute-start.12 = (f32[5,6,32,128]{3,2,1,0:T(8,128)S(1)}, f32[5,6,32,128]{3,2,1,0:T(8,128)S(1)}, u32[]{:S(2)}, u32[]{:S(2)}) collective-permute-start(f32[5,6,32,128]{3,2,1,0:T(8,128)S(1)} %first_product.3.p_own), channel_id=1, source_target_pairs={{0,2},{2,0},{4,6},{6,4},{8,10},{10,8},{12,14},{14,12},{16,18},{18,... | collective-permute-start | bytes 1474568 | tf_op jit(solution)/shard_map/ppermute | solution.py:326
  41.0 10.4 %collective-permute-done.8.p_off = f32[5,6,32,128]{3,2,1,0:T(8,128)S(1)} collective-permute-done((f32[5,6,32,128]{3,2,1,0:T(8,128)S(1)}, f32[5,6,32,128]{3,2,1,0:T(8,128)S(1)}, u32[]{:S(2)}, u32[]{:S(2)}) %collective-permute-start.8) | collective-permute-done | bytes 491552 | tf_op jit(solution)/shard_map/ppermute | solution.py:330
  51.4 2.0 %second_product.2 = (f32[5,3,32,128]{3,2,1,0:T(8,128)S(1)}, f32[5,3,32,128]{3,2,1,0:T(8,128)S(1)}) custom-call(s32[180]{0:T(256)S(1)} %get-tuple-element.31.index_ref, f32[5,6,32,128]{3,2,1,0:T(8,128)S(1)} %first_product.2.p_own, f32[5,6,32,128]{3,2,1,0:T(8,128)S(1)} %collective-permute-done.7.p_on, f32[5,6,32,128]{3,2,1,0:T(8,128)S(1)} %collective-permute-done.8.p_off, ...), custom_call_target="tpu_custom_call" | custom-call | flops 566231040 | bytes 4194304 | tf_op jit(solution)/shard_map/second_product/pallas_call | solution.py:399
  54.0 2.7 %collective-permute-done.13.p_off = f32[5,6,32,128]{3,2,1,0:T(8,128)S(1)} collective-permute-done((f32[5,6,32,128]{3,2,1,0:T(8,128)S(1)}, f32[5,6,32,128]{3,2,1,0:T(8,128)S(1)}, u32[]{:S(2)}, u32[]{:S(2)}) %collective-permute-start.13) | collective-permute-done | bytes 491552 | tf_op jit(solution)/shard_map/ppermute | solution.py:330
  56.7 2.0 %second_product.3 = (f32[5,3,32,128]{3,2,1,0:T(8,128)S(1)}, f32[5,3,32,128]{3,2,1,0:T(8,128)S(1)}) custom-call(s32[180]{0:T(256)S(1)} %get-tuple-element.31.index_ref, f32[5,6,32,128]{3,2,1,0:T(8,128)S(1)} %first_product.3.p_own, f32[5,6,32,128]{3,2,1,0:T(8,128)S(1)} %collective-permute-done.12.p_on, f32[5,6,32,128]{3,2,1,0:T(8,128)S(1)} %collective-permute-done.13.p_off, ...), custom_call_target="tpu_custom_call" | custom-call | flops 566231040 | bytes 4194304 | tf_op jit(solution)/shard_map/second_product/pallas_call | solution.py:399
  59.7 5.3 %collective-permute-done.15.refs_3_ = f32[5,3,32,128]{3,2,1,0:T(8,128)S(1)} collective-permute-done((f32[5,3,32,128]{3,2,1,0:T(8,128)S(1)}, f32[5,3,32,128]{3,2,1,0:T(8,128)S(1)}, u32[]{:S(2)}, u32[]{:S(2)}) %collective-permute-start.15) | collective-permute-done | bytes 245792 | tf_op jit(solution)/shard_map/ppermute | solution.py:323
  65.0 1.4 %finish.1 = f32[5,6,64,128]{3,2,1,0:T(8,128)} custom-call(f32[5,6,64,128]{3,2,1,0:T(8,128)S(1)} %copy-done.1, f32[5,3,32,128]{3,2,1,0:T(8,128)S(1)} %get-tuple-element.47.refs_0_, f32[5,3,32,128]{3,2,1,0:T(8,128)S(1)} %get-tuple-element.50.refs_1_, f32[5,3,32,128]{3,2,1,0:T(8,128)S(1)} %collective-permute-done.14.refs_2_, ...), custom_call_target="tpu_custom_call" | custom-call | bytes 3145728 | tf_op jit(solution)/shard_map/finish/pallas_call | solution.py:415
  (32 shorter events, 5.9 us)
Async XLA Ops:
  0.0 1.2 %copy-start = (f32[5,6,64,128]{3,2,1,0:T(8,128)S(1)}, f32[5,6,64,128]{3,2,1,0:T(8,128)}, u32[]{:S(2)}) copy-start(f32[5,6,64,128]{3,2,1,0:T(8,128)} %z_ref.5) | copy-start | bytes 2949124
  1.2 4.7 %copy-start.4 = (s32[5,4]{0,1:T(4,128)S(1)}, s32[5,4]{0,1:T(4,128)}, u32[]{:S(2)}) copy-start(s32[5,4]{0,1:T(4,128)} %param.6) | copy-start | bytes 244
  1.2 4.8 %copy-start.3 = (s32[80,6]{0,1:T(8,128)S(1)}, s32[80,6]{0,1:T(8,128)}, u32[]{:S(2)}) copy-start(s32[80,6]{0,1:T(8,128)} %param.7) | copy-start | bytes 5764
  1.2 9.2 %copy-start.2 = (f32[5,4,64,128]{3,2,1,0:T(8,128)S(1)}, f32[5,4,64,128]{3,2,1,0:T(8,128)}, u32[]{:S(2)}) copy-start(f32[5,4,64,128]{3,2,1,0:T(8,128)} %j_ref) | copy-start | bytes 1966084
  1.5 8.9 %collective-permute-start = (f32[5,3,32,128]{3,2,1,0:T(8,128)S(1)}, f32[5,3,32,128]{3,2,1,0:T(8,128)S(1)}, u32[]{:S(2)}, u32[]{:S(2)}) collective-permute-start(f32[5,3,32,128]{3,2,1,0:T(8,128)S(1)} %get-tuple-element.32.refs_1_), channel_id=1, source_target_pairs={{0,1},{1,0},{2,3},{3,2},{4,5},{5,4},{6,7},{7,6},{8,9},{9,8},{10,11... | collective-permute-start | bytes 737288 | tf_op jit(solution)/shard_map/ppermute | solution.py:323
  2.1 12.5 %collective-permute-start.1 = (f32[5,3,32,128]{3,2,1,0:T(8,128)S(1)}, f32[5,3,32,128]{3,2,1,0:T(8,128)S(1)}, u32[]{:S(2)}, u32[]{:S(2)}) collective-permute-start(f32[5,3,32,128]{3,2,1,0:T(8,128)S(1)} %get-tuple-element.29.refs_0_), channel_id=1, source_target_pairs={{0,1},{1,0},{2,3},{3,2},{4,5},{5,4},{6,7},{7,6},{8,9},{9,8},{10,11... | collective-permute-start | bytes 737288 | tf_op jit(solution)/shard_map/ppermute | solution.py:323
  4.0 15.4 %collective-permute-start.4 = (f32[5,3,64,128]{3,2,1,0:T(8,128)S(1)}, f32[5,3,64,128]{3,2,1,0:T(8,128)S(1)}, u32[]{:S(2)}, u32[]{:S(2)}) collective-permute-start(f32[5,3,64,128]{3,2,1,0:T(8,128)S(1)} %split_own.1.z_own), channel_id=1, source_target_pairs={{2,4},{6,8},{10,12},{14,16},{18,20},{22,24},{26,28},{4,2},{8,6},{1... | collective-permute-start | bytes 1474568 | tf_op jit(solution)/shard_map/ppermute | solution.py:330
  10.5 18.2 %collective-permute-start.6 = (f32[5,4,64,128]{3,2,1,0:T(8,128)S(1)}, f32[5,4,64,128]{3,2,1,0:T(8,128)S(1)}, u32[]{:S(2)}, u32[]{:S(2)}) collective-permute-start(f32[5,4,64,128]{3,2,1,0:T(8,128)S(1)} %copy-done.2), channel_id=1, source_target_pairs={{0,1},{1,0},{2,3},{3,2},{4,5},{5,4},{6,7},{7,6},{8,9},{9,8},{10,11... | collective-permute-start | bytes 1966088 | tf_op jit(solution)/shard_map/ppermute | solution.py:323
  11.0 10.9 %collective-permute-start.2 = (f32[5,3,64,128]{3,2,1,0:T(8,128)S(1)}, f32[5,3,64,128]{3,2,1,0:T(8,128)S(1)}, u32[]{:S(2)}, u32[]{:S(2)}) collective-permute-start(f32[5,3,64,128]{3,2,1,0:T(8,128)S(1)} %split_own.1.z_own), channel_id=1, source_target_pairs={{0,2},{2,0},{4,6},{6,4},{8,10},{10,8},{12,14},{14,12},{16,18},{18,... | collective-permute-start | bytes 1474568 | tf_op jit(solution)/shard_map/ppermute | solution.py:326
  14.6 2.6 %collective-permute-start.3 = (f32[5,3,32,128]{3,2,1,0:T(8,128)S(1)}, f32[5,3,32,128]{3,2,1,0:T(8,128)S(1)}, u32[]{:S(2)}, u32[]{:S(2)}) collective-permute-start(f32[5,3,32,128]{3,2,1,0:T(8,128)S(1)} %collective-permute-done.1.z_oth.refs_2_), channel_id=1, source_target_pairs={{0,2},{2,0},{4,6},{6,4},{8,10},{10,8},{12,14},{14,12},{16,18},{18,... | collective-permute-start | bytes 737288 | tf_op jit(solution)/shard_map/ppermute | solution.py:326
  14.6 12.8 %collective-permute-start.5 = (f32[5,3,32,128]{3,2,1,0:T(8,128)S(1)}, f32[5,3,32,128]{3,2,1,0:T(8,128)S(1)}, u32[]{:S(2)}, u32[]{:S(2)}) collective-permute-start(f32[5,3,32,128]{3,2,1,0:T(8,128)S(1)} %collective-permute-done.1.z_oth.refs_2_), channel_id=1, source_target_pairs={{2,4},{6,8},{10,12},{14,16},{18,20},{22,24},{26,28},{4,2},{8,6},{1... | collective-permute-start | bytes 737288 | tf_op jit(solution)/shard_map/ppermute | solution.py:330
  17.3 17.2 %collective-permute-start.10 = (f32[5,3,32,128]{3,2,1,0:T(8,128)S(1)}, f32[5,3,32,128]{3,2,1,0:T(8,128)S(1)}, u32[]{:S(2)}, u32[]{:S(2)}) collective-permute-start(f32[5,3,32,128]{3,2,1,0:T(8,128)S(1)} %collective-permute-done.refs_3_.z_oth), channel_id=1, source_target_pairs={{0,2},{2,0},{4,6},{6,4},{8,10},{10,8},{12,14},{14,12},{16,18},{18,... | collective-permute-start | bytes 737288 | tf_op jit(solution)/shard_map/ppermute | solution.py:326
  19.4 15.4 %collective-permute-start.11 = (f32[5,3,32,128]{3,2,1,0:T(8,128)S(1)}, f32[5,3,32,128]{3,2,1,0:T(8,128)S(1)}, u32[]{:S(2)}, u32[]{:S(2)}) collective-permute-start(f32[5,3,32,128]{3,2,1,0:T(8,128)S(1)} %collective-permute-done.refs_3_.z_oth), channel_id=1, source_target_pairs={{2,4},{6,8},{10,12},{14,16},{18,20},{22,24},{26,28},{4,2},{8,6},{1... | collective-permute-start | bytes 737288 | tf_op jit(solution)/shard_map/ppermute | solution.py:330
  21.9 18.5 %collective-permute-start.9 = (f32[5,3,64,128]{3,2,1,0:T(8,128)S(1)}, f32[5,3,64,128]{3,2,1,0:T(8,128)S(1)}, u32[]{:S(2)}, u32[]{:S(2)}) collective-permute-start(f32[5,3,64,128]{3,2,1,0:T(8,128)S(1)} %split_own.1.z_own), channel_id=1, source_target_pairs={{0,1},{1,0},{2,3},{3,2},{4,5},{5,4},{6,7},{7,6},{8,9},{9,8},{10,11... | collective-permute-start | bytes 1474568 | tf_op jit(solution)/shard_map/ppermute | solution.py:323
  30.8 20.7 %collective-permute-start.8 = (f32[5,6,32,128]{3,2,1,0:T(8,128)S(1)}, f32[5,6,32,128]{3,2,1,0:T(8,128)S(1)}, u32[]{:S(2)}, u32[]{:S(2)}) collective-permute-start(f32[5,6,32,128]{3,2,1,0:T(8,128)S(1)} %first_product.2.p_own), channel_id=1, source_target_pairs={{2,4},{6,8},{10,12},{14,16},{18,20},{22,24},{26,28},{4,2},{8,6},{1... | collective-permute-start | bytes 1474568 | tf_op jit(solution)/shard_map/ppermute | solution.py:330
  32.7 18.7 %collective-permute-start.7 = (f32[5,6,32,128]{3,2,1,0:T(8,128)S(1)}, f32[5,6,32,128]{3,2,1,0:T(8,128)S(1)}, u32[]{:S(2)}, u32[]{:S(2)}) collective-permute-start(f32[5,6,32,128]{3,2,1,0:T(8,128)S(1)} %first_product.2.p_own), channel_id=1, source_target_pairs={{0,2},{2,0},{4,6},{6,4},{8,10},{10,8},{12,14},{14,12},{16,18},{18,... | collective-permute-start | bytes 1474568 | tf_op jit(solution)/shard_map/ppermute | solution.py:326
  36.9 19.8 %collective-permute-start.13 = (f32[5,6,32,128]{3,2,1,0:T(8,128)S(1)}, f32[5,6,32,128]{3,2,1,0:T(8,128)S(1)}, u32[]{:S(2)}, u32[]{:S(2)}) collective-permute-start(f32[5,6,32,128]{3,2,1,0:T(8,128)S(1)} %first_product.3.p_own), channel_id=1, source_target_pairs={{2,4},{6,8},{10,12},{14,16},{18,20},{22,24},{26,28},{4,2},{8,6},{1... | collective-permute-start | bytes 1474568 | tf_op jit(solution)/shard_map/ppermute | solution.py:330
  38.8 17.9 %collective-permute-start.12 = (f32[5,6,32,128]{3,2,1,0:T(8,128)S(1)}, f32[5,6,32,128]{3,2,1,0:T(8,128)S(1)}, u32[]{:S(2)}, u32[]{:S(2)}) collective-permute-start(f32[5,6,32,128]{3,2,1,0:T(8,128)S(1)} %first_product.3.p_own), channel_id=1, source_target_pairs={{0,2},{2,0},{4,6},{6,4},{8,10},{10,8},{12,14},{14,12},{16,18},{18,... | collective-permute-start | bytes 1474568 | tf_op jit(solution)/shard_map/ppermute | solution.py:326
  53.4 11.5 %copy-start.1 = (f32[5,6,64,128]{3,2,1,0:T(8,128)S(1)}, f32[5,6,64,128]{3,2,1,0:T(8,128)}, u32[]{:S(2)}) copy-start(f32[5,6,64,128]{3,2,1,0:T(8,128)} %z_ref.5) | copy-start | bytes 2949124
  53.5 6.3 %collective-permute-start.14 = (f32[5,3,32,128]{3,2,1,0:T(8,128)S(1)}, f32[5,3,32,128]{3,2,1,0:T(8,128)S(1)}, u32[]{:S(2)}, u32[]{:S(2)}) collective-permute-start(f32[5,3,32,128]{3,2,1,0:T(8,128)S(1)} %get-tuple-element.51), channel_id=1, source_target_pairs={{0,1},{1,0},{2,3},{3,2},{4,5},{5,4},{6,7},{7,6},{8,9},{9,8},{10,11... | collective-permute-start | bytes 737288 | tf_op jit(solution)/shard_map/ppermute | solution.py:323
  58.7 6.3 %collective-permute-start.15 = (f32[5,3,32,128]{3,2,1,0:T(8,128)S(1)}, f32[5,3,32,128]{3,2,1,0:T(8,128)S(1)}, u32[]{:S(2)}, u32[]{:S(2)}) collective-permute-start(f32[5,3,32,128]{3,2,1,0:T(8,128)S(1)} %get-tuple-element.52), channel_id=1, source_target_pairs={{0,1},{1,0},{2,3},{3,2},{4,5},{5,4},{6,7},{7,6},{8,9},{9,8},{10,11... | collective-permute-start | bytes 737288 | tf_op jit(solution)/shard_map/ppermute | solution.py:323

commit v6 on v5

--- a/solution.py
+++ b/solution.py
@@ -8,8 +8,7 @@
 from jax.sharding import PartitionSpec as P
 
 REACH = 5
-PARTS = ((32,), (32,))
-CHUNKS = tuple(sum(parts) for parts in PARTS)
+CHUNKS = (32, 32)
 VMEM_BYTES = 14 * 1024 * 1024
 
 
@@ -218,25 +217,15 @@
                 high_ref[at + 1], low_ref[at + 1] = halves(odd)
 
 
-def first_product(start, index_ref, near_high, near_low, off_own, off_oth, j_own_high, j_own_low, j_oth, *refs):
-    *p_refs, off_in, z_high, z_low, j_both, lhs_high, lhs_low, sems = refs
-    rows, pairs, _, lanes = off_oth.shape
-    depth = z_high.shape[1]
-    mine = pl.ds(start, depth)
-    half = j_oth.shape[2]
-    slots = j_oth.shape[1]
+def take_blocks(start, near_high, near_low, off_own, off_oth, off_in, z_high, z_low, sem):
+    rows, pairs, depth, lanes = off_oth.shape
     near = near_high.shape[0]
-    copy = pltpu.make_async_copy(off_own.at[:, :, mine], off_in, sems.at[0])
+    copy = pltpu.make_async_copy(off_own.at[:, :, pl.ds(start, depth)], off_in, sem)
     copy.start()
     z_high[:near], z_low[:near] = near_high[...], near_low[...]
-    j_both[:, :half], j_both[:, 2 * half : 3 * half] = j_own_high[...], j_own_low[...]
     blank = z_high.shape[0] - 1
     z_high[blank] = jnp.zeros(z_high.shape[1:], jnp.bfloat16)
     z_low[blank] = jnp.zeros(z_low.shape[1:], jnp.bfloat16)
-    for i in range(rows):
-        for s in range(slots):
-            place = pl.ds(s * 128, 128)
-            j_both[i, half : 2 * half, place], j_both[i, 3 * half :, place] = halves(turn_lanes(j_oth[i, s]))
     copy.wait()
     for i in range(rows):
         for j in range(pairs):
@@ -244,15 +233,36 @@
             at = near + (i * pairs + j) * 2
             z_high[at], z_low[at] = halves(even)
             z_high[at + 1], z_low[at + 1] = halves(odd)
+
+
+def first_product(start, index_ref, near_high, near_low, off_own, off_oth, j_own_high, j_own_low,
+                  j_oth_high, j_oth_low, p_ref, p_rest_ref, off_in, z_high, z_low, j_both, lhs_high, lhs_low,
+                  sems):
+    rows, pairs, depth, lanes = off_oth.shape
+    half, slots = j_own_high.shape[1], j_own_high.shape[2] // 128
+    for n, part in enumerate((j_own_high, j_oth_high, j_own_low, j_oth_low)):
+        j_both[:, n * half : (n + 1) * half] = part[...]
+    take_blocks(start, near_high, near_low, off_own, off_oth, off_in, z_high, z_low, sems.at[0])
     for i in range(rows):
         total = gather_dot(index_ref, i, slots, 2 * pairs, z_high, z_low, lhs_high, lhs_low,
                            (j_both[i], j_both[i, : 2 * half]), ((1,), (1,)))
         total = total.reshape(2 * pairs, depth, lanes)
-        at = 0
-        for p_ref in p_refs:
-            count = p_ref.shape[2]
-            p_ref[i] = total[:, at : at + count]
-            at += count
+        p_ref[i], p_rest_ref[i] = total[:pairs], total[pairs:]
+
+
+def first_half_product(start, index_ref, near_high, near_low, off_own, off_oth, rows_high, rows_low,
+                       p_ref, off_in, z_high, z_low, j_both, lhs_high, lhs_low, sems):
+    rows, pairs, depth, lanes = off_oth.shape
+    half, slots = rows_high.shape[1], rows_high.shape[2] // 128
+    for n, part in enumerate((rows_high, rows_high, rows_low, rows_low)):
+        j_both[:, n * half : (n + 1) * half] = part[...]
+    take_blocks(start, near_high, near_low, off_own, off_oth, off_in, z_high, z_low, sems.at[0])
+    for i in range(rows):
+        total = gather_dot(index_ref, i, slots, 2 * pairs, z_high, z_low, lhs_high, lhs_low,
+                           (j_both[i], j_both[i, : 2 * half]), ((1,), (1,)))
+        total = total.reshape(2 * pairs, depth, lanes)
+        for j in range(pairs):
+            p_ref[i, j] = jnp.where(is_low((depth, lanes)), total[2 * j], total[2 * j + 1])
 
 
 def left_blocks(chunks, z_own, z_rest, *refs):
@@ -268,22 +278,29 @@
                     both_ref[i, place, :lanes], both_ref[i, place, lanes:] = halves(block)
 
 
-def second_product(index_ref, p_own, p_on, p_off, l_both, own_ref, send_ref,
-                   p_high, p_low, lhs_high, lhs_low):
-    rows, slots, depth, lanes = p_own.shape
+def second_product(packed, index_ref, *refs):
+    sources, (l_both, own_ref, send_ref, p_high, p_low, lhs_high, lhs_low) = refs[:6], refs[6:]
+    rows, pairs, depth, lanes = own_ref.shape
+    slots = 2 * pairs
     blank = p_high.shape[0] - 1
     p_high[blank] = jnp.zeros(p_high.shape[1:], jnp.bfloat16)
     p_low[blank] = jnp.zeros(p_low.shape[1:], jnp.bfloat16)
-    for g, source in enumerate((p_own, p_on, p_off)):
+    for g in range(3):
         for i in range(rows):
-            for k in range(slots):
-                at = (g * rows + i) * slots + k
-                p_high[at], p_low[at] = halves(source[i, k])
+            for j in range(pairs):
+                blocks = sources[g][i, j], sources[3 + g][i, j]
+                places = j, pairs + j
+                if packed:
+                    blocks = unzip_lanes(*blocks)
+                    places = 2 * j, 2 * j + 1
+                for slot, block in zip(places, blocks):
+                    at = (g * rows + i) * slots + slot
+                    p_high[at], p_low[at] = halves(block)
     for i in range(rows):
         total = gather_dot(index_ref, i, slots, slots, p_high, p_low, lhs_high, lhs_low,
                            (l_both[i], l_both[i, :, :128]), ((1,), (0,)))
         total = total.reshape(slots, depth, lanes)
-        for j in range(slots // 2):
+        for j in range(pairs):
             own_ref[i, j], send_ref[i, j] = unzip_lanes(total[2 * j], total[2 * j + 1])
 
 
@@ -369,55 +386,59 @@
     blocks = 3 * rows * slots + 1
     bf16_buffer = functools.partial(pltpu.VMEM, dtype=jnp.bfloat16)
 
-    def first(start, parts, z_oth, off_oth, on_oth):
-        depth = sum(parts)
-        near = call(
+    def beside(start, depth, z_oth, on_oth):
+        return call(
             functools.partial(merge_near, start), (bf16((2 * rows * slots, depth, lanes)),) * 2, "merge_near"
         )(z_own, z_oth, on_own, on_oth)
+
+    def first(body, name, count, start, depth, near, off_oth, j_rows):
         return call(
-            functools.partial(first_product, start),
-            tuple(f32((rows, slots, part, lanes)) for part in parts),
-            "first_product",
+            functools.partial(body, start),
+            (f32((rows, pairs, depth, lanes)),) * count,
+            name,
             scratch=[pltpu.VMEM((rows, pairs, depth, lanes), jnp.float32)]
             + [bf16_buffer((blocks, depth, lanes))] * 2
             + [bf16_buffer((rows, 2 * lanes, left_slots * lanes))]
             + [bf16_buffer((slots * depth, left_slots * lanes))] * 2
             + [pltpu.SemaphoreType.DMA((1,))],
-            specs=[smem, vmem, vmem, hbm, vmem, vmem, vmem, vmem],
-            flops=6 * rows * left_slots * slots * depth * lanes * lanes,
-            nbytes=16 << 18,
-        )(flat_one, *near, off_own, off_oth, *j_own, j_oth)
-
-    products = []
-    start = 0
-    for parts, *oth in zip(PARTS, z_oth, off_oth, on_oth):
-        products += [(p, off_swap(p), on_swap(p)) for p in first(start, parts, *oth)]
-        start += sum(parts)
-
-    def second(p, p_off, p_on):
-        depth = p.shape[2]
+            specs=[smem, vmem, vmem, hbm, vmem] + [vmem] * len(j_rows),
+        )(flat_one, *near, off_own, off_oth, *j_rows)
+
+    def second(packed, depth, products):
         return call(
-            second_product,
+            functools.partial(second_product, packed),
             (f32((rows, pairs, depth, lanes)),) * 2,
             "second_product",
             scratch=[bf16_buffer((blocks, depth, lanes))] * 2
             + [bf16_buffer((slots * depth, slots * lanes))] * 2,
-            specs=[smem] + [vmem] * 4,
-            flops=6 * rows * slots * slots * depth * lanes * lanes,
-            nbytes=16 << 18,
-        )(flat_two, p, p_on, p_off, left)
+            specs=[smem] + [vmem] * 7,
+        )(flat_two, *products, left)
+
+    depth_one, depth_two = CHUNKS
+    near = beside(0, depth_one, z_oth[0], on_oth[0])
+    (one,) = first(first_half_product, "first_half_product", 1, 0, depth_one, near, off_oth[0], j_own)
+    one_on, one_off = on_swap(one), off_swap(one)
+    j_other = take_rows(j_oth)
+    (two,) = first(first_half_product, "first_half_product", 1, 0, depth_one, near, off_oth[0], j_other)
+    two_on, two_off = on_swap(two), off_swap(two)
+    near = beside(depth_one, depth_two, z_oth[1], on_oth[1])
+    three = first(first_product, "first_product", 2, depth_one, depth_two, near, off_oth[1], (*j_own, *j_other))
+    three_on, three_off = [on_swap(x) for x in three], [off_swap(x) for x in three]
 
     own, oth = [], []
-    for p, p_off, p_on in products:
-        mine, send = second(p, p_off, p_on)
+    for packed, depth, products in (
+        (True, depth_one, (one, one_on, one_off, two, two_on, two_off)),
+        (False, depth_two, tuple(x[h] for h in range(2) for x in (three, three_on, three_off))),
+    ):
+        mine, send = second(packed, depth, products)
         own.append(mine)
         oth.append(across(send))
     return call(
-        functools.partial(finish, len(products)),
+        functools.partial(finish, len(CHUNKS)),
         f32(inverse_blocks.shape),
         "finish",
         scratch=[pltpu.VMEM(inverse_blocks.shape, jnp.float32), pltpu.SemaphoreType.DMA((rows,))],
-        specs=[vmem] * (1 + 2 * len(products)),
+        specs=[vmem] * (1 + 2 * len(CHUNKS)),
         out_specs=anywhere,
         nbytes=12 << 18,
     )(inverse_blocks, *own, *oth)

time: 66.6 us -> 65.8 us (0.988)
  waiting for transfers between devices: 28.7 us -> 18.5 us
  starting transfers between devices: 20.4 us -> 27.4 us
  Pallas kernels: 15.6 us -> 17.6 us
    ppermute x5 -> x7, waiting for transfers between devices: 18.8 us -> 8.04 us  [off_swap(): return lax.ppermute(x, 'rows', inside + [(b, a) for a, b in inside])]
    ppermute x5 -> x7, starting transfers between devices: 10.6 us -> 16.3 us  [off_swap(): return lax.ppermute(x, 'rows', inside + [(b, a) for a, b in inside])]
    pallas_call x7 -> x9, Pallas kernels: 10.1 us -> 12.2 us  [the longest x3 5.68 us: first(): call(functools.partial(body, start), (f32((rows, pairs, depth, lanes)),)...]
    ppermute x5 -> x7, starting transfers between devices: 5.49 us -> 7.23 us  [on_swap(): return lax.ppermute(x, 'rows', [(i, i ^ 1) for i in range(count)])]
  transfers between devices with their start and end apart: 16 -> 20, of which waited for: 9 -> 9; matrix products, arithmetic and copies ran while one was open for 0% -> 0% of each run, Pallas kernels for 21% -> 24%
where the time goes in v6:
time: 65.8 us; the launch traced here: 65.2 us
  starting transfers between devices  27.4 us (42%)
  waiting for transfers between devices  18.5 us (28%)
  Pallas kernels  17.6 us (27%)
  local copies, waits for them, and re-layouts  1.41 us (2%)
    ppermute x7, starting transfers between devices, off_swap(): return lax.ppermute(x, 'rows', inside + [(b, a) for a, b in inside])  16.3 us
    ppermute x6, waiting for transfers between devices, across(): return lax.ppermute(x, 'inner', [(0, 1), (1, 0)])  10.4 us
    ppermute x7, waiting for transfers between devices, off_swap(): return lax.ppermute(x, 'rows', inside + [(b, a) for a, b in inside])  8.04 us
    ppermute x7, starting transfers between devices, on_swap(): return lax.ppermute(x, 'rows', [(i, i ^ 1) for i in range(count)])  7.23 us
    pallas_call x3, Pallas kernels, first(): call(functools.partial(body, start), (f32((rows, pairs, depth, lanes)),)...  5.68 us
    pallas_call x2, Pallas kernels, second(): call(functools.partial(second_product, packed), (f32((rows, pairs, depth,...  4.27 us
    pallas_call x1, Pallas kernels, half_shards(): flat_one, flat_two = find(hardness_pattern, inverse_pattern)  3.98 us
    ppermute x6, starting transfers between devices, across(): return lax.ppermute(x, 'inner', [(0, 1), (1, 0)])  3.81 us
  transfers between devices with their start and end apart: 20, of which 9 were waited for; matrix products, arithmetic and copies ran while one was open for 0% of the time, Pallas kernels for 24%

profile of v6, /device:TPU:14, one launch (start us, length us, event | category | flops | bytes accessed | tf_op | source)
XLA Modules:
  0.0 65.2 jit_solution(5630685398343571138)
XLA Ops:
  2.1 1.5 %collective-permute-start.1 = (f32[5,3,32,128]{3,2,1,0:T(8,128)S(1)}, f32[5,3,32,128]{3,2,1,0:T(8,128)S(1)}, u32[]{:S(2)}, u32[]{:S(2)}) collective-permute-start(f32[5,3,32,128]{3,2,1,0:T(8,128)S(1)} %get-tuple-element.33.refs_0_), channel_id=1, source_target_pairs={{0,1},{1,0},{2,3},{3,2},{4,5},{5,4},{6,7},{7,6},{8,9},{9,8},{10,11... | collective-permute-start | bytes 737288 | tf_op jit(solution)/shard_map/ppermute | solution.py:340
  4.0 1.9 %collective-permute-start.4 = (f32[5,3,64,128]{3,2,1,0:T(8,128)S(1)}, f32[5,3,64,128]{3,2,1,0:T(8,128)S(1)}, u32[]{:S(2)}, u32[]{:S(2)}) collective-permute-start(f32[5,3,64,128]{3,2,1,0:T(8,128)S(1)} %split_own.1.z_own), channel_id=1, source_target_pairs={{2,4},{6,8},{10,12},{14,16},{18,20},{22,24},{26,28},{4,2},{8,6},{1... | collective-permute-start | bytes 1474568 | tf_op jit(solution)/shard_map/ppermute | solution.py:347
  6.1 4.0 %find_blocks.1 = (s32[120]{0:T(128)S(1)}, s32[180]{0:T(256)S(1)}) custom-call(s32[5,4]{1,0:T(8,128)S(1)} %copy.5.left_ref, s32[80,6]{1,0:T(8,128)S(1)} %copy.6.pattern_ref), custom_call_target="tpu_custom_call" | custom-call | tf_op jit(solution)/shard_map/find_blocks/pallas_call | solution.py:372
  12.1 2.6 %collective-permute-done.1.z_oth.refs_2_ = f32[5,3,32,128]{3,2,1,0:T(8,128)S(1)} collective-permute-done((f32[5,3,32,128]{3,2,1,0:T(8,128)S(1)}, f32[5,3,32,128]{3,2,1,0:T(8,128)S(1)}, u32[]{:S(2)}, u32[]{:S(2)}) %collective-permute-start.1) | collective-permute-done | bytes 245792 | tf_op jit(solution)/shard_map/ppermute | solution.py:340
  14.6 2.6 %collective-permute-start.5 = (f32[5,3,32,128]{3,2,1,0:T(8,128)S(1)}, f32[5,3,32,128]{3,2,1,0:T(8,128)S(1)}, u32[]{:S(2)}, u32[]{:S(2)}) collective-permute-start(f32[5,3,32,128]{3,2,1,0:T(8,128)S(1)} %collective-permute-done.1.z_oth.refs_2_), channel_id=1, source_target_pairs={{2,4},{6,8},{10,12},{14,16},{18,20},{22,24},{26,28},{4,2},{8,6},{1... | collective-permute-start | bytes 737288 | tf_op jit(solution)/shard_map/ppermute | solution.py:347
  17.8 1.6 %collective-permute-done.4.off_own = f32[5,3,64,128]{3,2,1,0:T(8,128)S(1)} collective-permute-done((f32[5,3,64,128]{3,2,1,0:T(8,128)S(1)}, f32[5,3,64,128]{3,2,1,0:T(8,128)S(1)}, u32[]{:S(2)}, u32[]{:S(2)}) %collective-permute-start.4) | collective-permute-done | bytes 491552 | tf_op jit(solution)/shard_map/ppermute | solution.py:347
  19.6 2.2 %collective-permute-start.13 = (f32[5,3,32,128]{3,2,1,0:T(8,128)S(1)}, f32[5,3,32,128]{3,2,1,0:T(8,128)S(1)}, u32[]{:S(2)}, u32[]{:S(2)}) collective-permute-start(f32[5,3,32,128]{3,2,1,0:T(8,128)S(1)} %collective-permute-done.refs_3_.z_oth), channel_id=1, source_target_pairs={{2,4},{6,8},{10,12},{14,16},{18,20},{22,24},{26,28},{4,2},{8,6},{1... | collective-permute-start | bytes 737288 | tf_op jit(solution)/shard_map/ppermute | solution.py:347
  22.2 2.6 %collective-permute-done.5.off_oth = f32[5,3,32,128]{3,2,1,0:T(8,128)S(1)} collective-permute-done((f32[5,3,32,128]{3,2,1,0:T(8,128)S(1)}, f32[5,3,32,128]{3,2,1,0:T(8,128)S(1)}, u32[]{:S(2)}, u32[]{:S(2)}) %collective-permute-start.5) | collective-permute-done | bytes 245792 | tf_op jit(solution)/shard_map/ppermute | solution.py:347
  24.8 1.9 %first_half_product.2.refs_0_ = f32[5,3,32,128]{3,2,1,0:T(8,128)S(1)} custom-call(s32[120]{0:T(128)S(1)} %get-tuple-element.39.index_ref, bf16[60,32,128]{2,1,0:T(8,128)(2,1)S(1)} %get-tuple-element.41.near_high, bf16[60,32,128]{2,1,0:T(8,128)(2,1)S(1)} %get-tuple-element.42.near_low, f32[5,3,64,128]{3,2,1,0:T(8,128)S(1)} %collective-permute-done.4.off_own, ...), custom_call_target="tpu_custom_call" | custom-call | tf_op jit(solution)/shard_map/first_half_product/pallas_call | solution.py:395
  26.7 2.9 %collective-permute-start.7 = (f32[5,3,32,128]{3,2,1,0:T(8,128)S(1)}, f32[5,3,32,128]{3,2,1,0:T(8,128)S(1)}, u32[]{:S(2)}, u32[]{:S(2)}) collective-permute-start(f32[5,3,32,128]{3,2,1,0:T(8,128)S(1)} %first_half_product.2.refs_0_), channel_id=1, source_target_pairs={{2,4},{6,8},{10,12},{14,16},{18,20},{22,24},{26,28},{4,2},{8,6},{1... | collective-permute-start | bytes 737288 | tf_op jit(solution)/shard_map/ppermute | solution.py:347
  29.9 1.9 %first_half_product.3.refs_3_ = f32[5,3,32,128]{3,2,1,0:T(8,128)S(1)} custom-call(s32[120]{0:T(128)S(1)} %get-tuple-element.39.index_ref, bf16[60,32,128]{2,1,0:T(8,128)(2,1)S(1)} %get-tuple-element.41.near_high, bf16[60,32,128]{2,1,0:T(8,128)(2,1)S(1)} %get-tuple-element.42.near_low, f32[5,3,64,128]{3,2,1,0:T(8,128)S(1)} %collective-permute-done.4.off_own, ...), custom_call_target="tpu_custom_call" | custom-call | tf_op jit(solution)/shard_map/first_half_product/pallas_call | solution.py:395
  31.8 2.7 %collective-permute-start.10 = (f32[5,3,32,128]{3,2,1,0:T(8,128)S(1)}, f32[5,3,32,128]{3,2,1,0:T(8,128)S(1)}, u32[]{:S(2)}, u32[]{:S(2)}) collective-permute-start(f32[5,3,32,128]{3,2,1,0:T(8,128)S(1)} %first_half_product.3.refs_3_), channel_id=1, source_target_pairs={{2,4},{6,8},{10,12},{14,16},{18,20},{22,24},{26,28},{4,2},{8,6},{1... | collective-permute-start | bytes 737288 | tf_op jit(solution)/shard_map/ppermute | solution.py:347
  34.8 1.6 %collective-permute-start.9 = (f32[5,3,32,128]{3,2,1,0:T(8,128)S(1)}, f32[5,3,32,128]{3,2,1,0:T(8,128)S(1)}, u32[]{:S(2)}, u32[]{:S(2)}) collective-permute-start(f32[5,3,32,128]{3,2,1,0:T(8,128)S(1)} %first_half_product.3.refs_3_), channel_id=1, source_target_pairs={{0,2},{2,0},{4,6},{6,4},{8,10},{10,8},{12,14},{14,12},{16,18},{18,... | collective-permute-start | bytes 737288 | tf_op jit(solution)/shard_map/ppermute | solution.py:343
  36.4 1.9 %first_product.1 = (f32[5,3,32,128]{3,2,1,0:T(8,128)S(1)}, f32[5,3,32,128]{3,2,1,0:T(8,128)S(1)}) custom-call(s32[120]{0:T(128)S(1)} %get-tuple-element.39.index_ref, bf16[60,32,128]{2,1,0:T(8,128)(2,1)S(1)} %get-tuple-element.54.near_high, bf16[60,32,128]{2,1,0:T(8,128)(2,1)S(1)} %get-tuple-element.55.near_low, ...), custom_call_target="tpu_custom_call" | custom-call | tf_op jit(solution)/shard_map/first_product/pallas_call | solution.py:395
  39.2 2.0 %collective-permute-start.15 = (f32[5,3,32,128]{3,2,1,0:T(8,128)S(1)}, f32[5,3,32,128]{3,2,1,0:T(8,128)S(1)}, u32[]{:S(2)}, u32[]{:S(2)}) collective-permute-start(f32[5,3,32,128]{3,2,1,0:T(8,128)S(1)} %get-tuple-element.56.refs_0_), channel_id=1, source_target_pairs={{2,4},{6,8},{10,12},{14,16},{18,20},{22,24},{26,28},{4,2},{8,6},{1... | collective-permute-start | bytes 737288 | tf_op jit(solution)/shard_map/ppermute | solution.py:347
  41.2 1.6 %collective-permute-start.14 = (f32[5,3,32,128]{3,2,1,0:T(8,128)S(1)}, f32[5,3,32,128]{3,2,1,0:T(8,128)S(1)}, u32[]{:S(2)}, u32[]{:S(2)}) collective-permute-start(f32[5,3,32,128]{3,2,1,0:T(8,128)S(1)} %get-tuple-element.56.refs_0_), channel_id=1, source_target_pairs={{0,2},{2,0},{4,6},{6,4},{8,10},{10,8},{12,14},{14,12},{16,18},{18,... | collective-permute-start | bytes 737288 | tf_op jit(solution)/shard_map/ppermute | solution.py:343
  42.8 2.0 %collective-permute-start.17 = (f32[5,3,32,128]{3,2,1,0:T(8,128)S(1)}, f32[5,3,32,128]{3,2,1,0:T(8,128)S(1)}, u32[]{:S(2)}, u32[]{:S(2)}) collective-permute-start(f32[5,3,32,128]{3,2,1,0:T(8,128)S(1)} %get-tuple-element.57.refs_3_), channel_id=1, source_target_pairs={{2,4},{6,8},{10,12},{14,16},{18,20},{22,24},{26,28},{4,2},{8,6},{1... | collective-permute-start | bytes 737288 | tf_op jit(solution)/shard_map/ppermute | solution.py:347
  44.8 2.9 %collective-permute-start.16 = (f32[5,3,32,128]{3,2,1,0:T(8,128)S(1)}, f32[5,3,32,128]{3,2,1,0:T(8,128)S(1)}, u32[]{:S(2)}, u32[]{:S(2)}) collective-permute-start(f32[5,3,32,128]{3,2,1,0:T(8,128)S(1)} %get-tuple-element.57.refs_3_), channel_id=1, source_target_pairs={{0,2},{2,0},{4,6},{6,4},{8,10},{10,8},{12,14},{14,12},{16,18},{18,... | collective-permute-start | bytes 737288 | tf_op jit(solution)/shard_map/ppermute | solution.py:343
  48.3 2.3 %second_product.2 = (f32[5,3,32,128]{3,2,1,0:T(8,128)S(1)}, f32[5,3,32,128]{3,2,1,0:T(8,128)S(1)}) custom-call(s32[180]{0:T(256)S(1)} %get-tuple-element.35.index_ref, f32[5,3,32,128]{3,2,1,0:T(8,128)S(1)} %first_half_product.2.refs_0_, f32[5,3,32,128]{3,2,1,0:T(8,128)S(1)} %collective-permute-done.6.refs_1_, ...), custom_call_target="tpu_custom_call" | custom-call | tf_op jit(solution)/shard_map/second_product/pallas_call | solution.py:408
  51.9 2.6 %collective-permute-done.17.refs_5_ = f32[5,3,32,128]{3,2,1,0:T(8,128)S(1)} collective-permute-done((f32[5,3,32,128]{3,2,1,0:T(8,128)S(1)}, f32[5,3,32,128]{3,2,1,0:T(8,128)S(1)}, u32[]{:S(2)}, u32[]{:S(2)}) %collective-permute-start.17) | collective-permute-done | bytes 245792 | tf_op jit(solution)/shard_map/ppermute | solution.py:347
  54.6 2.0 %second_product.3 = (f32[5,3,32,128]{3,2,1,0:T(8,128)S(1)}, f32[5,3,32,128]{3,2,1,0:T(8,128)S(1)}) custom-call(s32[180]{0:T(256)S(1)} %get-tuple-element.35.index_ref, f32[5,3,32,128]{3,2,1,0:T(8,128)S(1)} %get-tuple-element.56.refs_0_, f32[5,3,32,128]{3,2,1,0:T(8,128)S(1)} %collective-permute-done.14.refs_1_, ...), custom_call_target="tpu_custom_call" | custom-call | tf_op jit(solution)/shard_map/second_product/pallas_call | solution.py:408
  57.1 2.3 %collective-permute-done.18.refs_2_ = f32[5,3,32,128]{3,2,1,0:T(8,128)S(1)} collective-permute-done((f32[5,3,32,128]{3,2,1,0:T(8,128)S(1)}, f32[5,3,32,128]{3,2,1,0:T(8,128)S(1)}, u32[]{:S(2)}, u32[]{:S(2)}) %collective-permute-start.18) | collective-permute-done | bytes 245792 | tf_op jit(solution)/shard_map/ppermute | solution.py:340
  59.5 4.3 %collective-permute-done.19.refs_3_ = f32[5,3,32,128]{3,2,1,0:T(8,128)S(1)} collective-permute-done((f32[5,3,32,128]{3,2,1,0:T(8,128)S(1)}, f32[5,3,32,128]{3,2,1,0:T(8,128)S(1)}, u32[]{:S(2)}, u32[]{:S(2)}) %collective-permute-start.19) | collective-permute-done | bytes 245792 | tf_op jit(solution)/shard_map/ppermute | solution.py:340
  63.8 1.4 %finish.1 = f32[5,6,64,128]{3,2,1,0:T(8,128)} custom-call(f32[5,6,64,128]{3,2,1,0:T(8,128)S(1)} %copy-done.1, f32[5,3,32,128]{3,2,1,0:T(8,128)S(1)} %get-tuple-element.53.refs_0_, f32[5,3,32,128]{3,2,1,0:T(8,128)S(1)} %get-tuple-element.58.refs_1_, f32[5,3,32,128]{3,2,1,0:T(8,128)S(1)} %collective-permute-done.18.refs_2_, ...), custom_call_target="tpu_custom_call" | custom-call | bytes 3145728 | tf_op jit(solution)/shard_map/finish/pallas_call | solution.py:436
  (42 shorter events, 9.7 us)
Async XLA Ops:
  1.2 4.7 %copy-start.4 = (s32[5,4]{0,1:T(4,128)S(1)}, s32[5,4]{0,1:T(4,128)}, u32[]{:S(2)}) copy-start(s32[5,4]{0,1:T(4,128)} %param.6) | copy-start | bytes 244
  1.2 4.8 %copy-start.3 = (s32[80,6]{0,1:T(8,128)S(1)}, s32[80,6]{0,1:T(8,128)}, u32[]{:S(2)}) copy-start(s32[80,6]{0,1:T(8,128)} %param.7) | copy-start | bytes 5764
  1.2 9.2 %copy-start.2 = (f32[5,4,64,128]{3,2,1,0:T(8,128)S(1)}, f32[5,4,64,128]{3,2,1,0:T(8,128)}, u32[]{:S(2)}) copy-start(f32[5,4,64,128]{3,2,1,0:T(8,128)} %j_ref) | copy-start | bytes 1966084
  1.5 8.9 %collective-permute-start = (f32[5,3,32,128]{3,2,1,0:T(8,128)S(1)}, f32[5,3,32,128]{3,2,1,0:T(8,128)S(1)}, u32[]{:S(2)}, u32[]{:S(2)}) collective-permute-start(f32[5,3,32,128]{3,2,1,0:T(8,128)S(1)} %get-tuple-element.36.refs_1_), channel_id=1, source_target_pairs={{0,1},{1,0},{2,3},{3,2},{4,5},{5,4},{6,7},{7,6},{8,9},{9,8},{10,11... | collective-permute-start | bytes 737288 | tf_op jit(solution)/shard_map/ppermute | solution.py:340
  2.1 12.5 %collective-permute-start.1 = (f32[5,3,32,128]{3,2,1,0:T(8,128)S(1)}, f32[5,3,32,128]{3,2,1,0:T(8,128)S(1)}, u32[]{:S(2)}, u32[]{:S(2)}) collective-permute-start(f32[5,3,32,128]{3,2,1,0:T(8,128)S(1)} %get-tuple-element.33.refs_0_), channel_id=1, source_target_pairs={{0,1},{1,0},{2,3},{3,2},{4,5},{5,4},{6,7},{7,6},{8,9},{9,8},{10,11... | collective-permute-start | bytes 737288 | tf_op jit(solution)/shard_map/ppermute | solution.py:340
  4.0 15.4 %collective-permute-start.4 = (f32[5,3,64,128]{3,2,1,0:T(8,128)S(1)}, f32[5,3,64,128]{3,2,1,0:T(8,128)S(1)}, u32[]{:S(2)}, u32[]{:S(2)}) collective-permute-start(f32[5,3,64,128]{3,2,1,0:T(8,128)S(1)} %split_own.1.z_own), channel_id=1, source_target_pairs={{2,4},{6,8},{10,12},{14,16},{18,20},{22,24},{26,28},{4,2},{8,6},{1... | collective-permute-start | bytes 1474568 | tf_op jit(solution)/shard_map/ppermute | solution.py:347
  10.5 19.1 %collective-permute-start.8 = (f32[5,4,64,128]{3,2,1,0:T(8,128)S(1)}, f32[5,4,64,128]{3,2,1,0:T(8,128)S(1)}, u32[]{:S(2)}, u32[]{:S(2)}) collective-permute-start(f32[5,4,64,128]{3,2,1,0:T(8,128)S(1)} %copy-done.2), channel_id=1, source_target_pairs={{0,1},{1,0},{2,3},{3,2},{4,5},{5,4},{6,7},{7,6},{8,9},{9,8},{10,11... | collective-permute-start | bytes 1966088 | tf_op jit(solution)/shard_map/ppermute | solution.py:340
  11.0 8.7 %collective-permute-start.2 = (f32[5,3,64,128]{3,2,1,0:T(8,128)S(1)}, f32[5,3,64,128]{3,2,1,0:T(8,128)S(1)}, u32[]{:S(2)}, u32[]{:S(2)}) collective-permute-start(f32[5,3,64,128]{3,2,1,0:T(8,128)S(1)} %split_own.1.z_own), channel_id=1, source_target_pairs={{0,2},{2,0},{4,6},{6,4},{8,10},{10,8},{12,14},{14,12},{16,18},{18,... | collective-permute-start | bytes 1474568 | tf_op jit(solution)/shard_map/ppermute | solution.py:343
  14.6 2.6 %collective-permute-start.3 = (f32[5,3,32,128]{3,2,1,0:T(8,128)S(1)}, f32[5,3,32,128]{3,2,1,0:T(8,128)S(1)}, u32[]{:S(2)}, u32[]{:S(2)}) collective-permute-start(f32[5,3,32,128]{3,2,1,0:T(8,128)S(1)} %collective-permute-done.1.z_oth.refs_2_), channel_id=1, source_target_pairs={{0,2},{2,0},{4,6},{6,4},{8,10},{10,8},{12,14},{14,12},{16,18},{18,... | collective-permute-start | bytes 737288 | tf_op jit(solution)/shard_map/ppermute | solution.py:343
  14.6 10.1 %collective-permute-start.5 = (f32[5,3,32,128]{3,2,1,0:T(8,128)S(1)}, f32[5,3,32,128]{3,2,1,0:T(8,128)S(1)}, u32[]{:S(2)}, u32[]{:S(2)}) collective-permute-start(f32[5,3,32,128]{3,2,1,0:T(8,128)S(1)} %collective-permute-done.1.z_oth.refs_2_), channel_id=1, source_target_pairs={{2,4},{6,8},{10,12},{14,16},{18,20},{22,24},{26,28},{4,2},{8,6},{1... | collective-permute-start | bytes 737288 | tf_op jit(solution)/shard_map/ppermute | solution.py:347
  17.3 21.9 %collective-permute-start.11 = (f32[5,3,64,128]{3,2,1,0:T(8,128)S(1)}, f32[5,3,64,128]{3,2,1,0:T(8,128)S(1)}, u32[]{:S(2)}, u32[]{:S(2)}) collective-permute-start(f32[5,3,64,128]{3,2,1,0:T(8,128)S(1)} %split_own.1.z_own), channel_id=1, source_target_pairs={{0,1},{1,0},{2,3},{3,2},{4,5},{5,4},{6,7},{7,6},{8,9},{9,8},{10,11... | collective-permute-start | bytes 1474568 | tf_op jit(solution)/shard_map/ppermute | solution.py:340
  19.4 12.4 %collective-permute-start.12 = (f32[5,3,32,128]{3,2,1,0:T(8,128)S(1)}, f32[5,3,32,128]{3,2,1,0:T(8,128)S(1)}, u32[]{:S(2)}, u32[]{:S(2)}) collective-permute-start(f32[5,3,32,128]{3,2,1,0:T(8,128)S(1)} %collective-permute-done.refs_3_.z_oth), channel_id=1, source_target_pairs={{0,2},{2,0},{4,6},{6,4},{8,10},{10,8},{12,14},{14,12},{16,18},{18,... | collective-permute-start | bytes 737288 | tf_op jit(solution)/shard_map/ppermute | solution.py:343
  19.6 15.2 %collective-permute-start.13 = (f32[5,3,32,128]{3,2,1,0:T(8,128)S(1)}, f32[5,3,32,128]{3,2,1,0:T(8,128)S(1)}, u32[]{:S(2)}, u32[]{:S(2)}) collective-permute-start(f32[5,3,32,128]{3,2,1,0:T(8,128)S(1)} %collective-permute-done.refs_3_.z_oth), channel_id=1, source_target_pairs={{2,4},{6,8},{10,12},{14,16},{18,20},{22,24},{26,28},{4,2},{8,6},{1... | collective-permute-start | bytes 737288 | tf_op jit(solution)/shard_map/ppermute | solution.py:347
  26.7 14.5 %collective-permute-start.7 = (f32[5,3,32,128]{3,2,1,0:T(8,128)S(1)}, f32[5,3,32,128]{3,2,1,0:T(8,128)S(1)}, u32[]{:S(2)}, u32[]{:S(2)}) collective-permute-start(f32[5,3,32,128]{3,2,1,0:T(8,128)S(1)} %first_half_product.2.refs_0_), channel_id=1, source_target_pairs={{2,4},{6,8},{10,12},{14,16},{18,20},{22,24},{26,28},{4,2},{8,6},{1... | collective-permute-start | bytes 737288 | tf_op jit(solution)/shard_map/ppermute | solution.py:347
  29.6 13.2 %collective-permute-start.6 = (f32[5,3,32,128]{3,2,1,0:T(8,128)S(1)}, f32[5,3,32,128]{3,2,1,0:T(8,128)S(1)}, u32[]{:S(2)}, u32[]{:S(2)}) collective-permute-start(f32[5,3,32,128]{3,2,1,0:T(8,128)S(1)} %first_half_product.2.refs_0_), channel_id=1, source_target_pairs={{0,2},{2,0},{4,6},{6,4},{8,10},{10,8},{12,14},{14,12},{16,18},{18,... | collective-permute-start | bytes 737288 | tf_op jit(solution)/shard_map/ppermute | solution.py:343
  31.8 13.0 %collective-permute-start.10 = (f32[5,3,32,128]{3,2,1,0:T(8,128)S(1)}, f32[5,3,32,128]{3,2,1,0:T(8,128)S(1)}, u32[]{:S(2)}, u32[]{:S(2)}) collective-permute-start(f32[5,3,32,128]{3,2,1,0:T(8,128)S(1)} %first_half_product.3.refs_3_), channel_id=1, source_target_pairs={{2,4},{6,8},{10,12},{14,16},{18,20},{22,24},{26,28},{4,2},{8,6},{1... | collective-permute-start | bytes 737288 | tf_op jit(solution)/shard_map/ppermute | solution.py:347
  34.8 13.4 %collective-permute-start.9 = (f32[5,3,32,128]{3,2,1,0:T(8,128)S(1)}, f32[5,3,32,128]{3,2,1,0:T(8,128)S(1)}, u32[]{:S(2)}, u32[]{:S(2)}) collective-permute-start(f32[5,3,32,128]{3,2,1,0:T(8,128)S(1)} %first_half_product.3.refs_3_), channel_id=1, source_target_pairs={{0,2},{2,0},{4,6},{6,4},{8,10},{10,8},{12,14},{14,12},{16,18},{18,... | collective-permute-start | bytes 737288 | tf_op jit(solution)/shard_map/ppermute | solution.py:343
  39.2 12.8 %collective-permute-start.15 = (f32[5,3,32,128]{3,2,1,0:T(8,128)S(1)}, f32[5,3,32,128]{3,2,1,0:T(8,128)S(1)}, u32[]{:S(2)}, u32[]{:S(2)}) collective-permute-start(f32[5,3,32,128]{3,2,1,0:T(8,128)S(1)} %get-tuple-element.56.refs_0_), channel_id=1, source_target_pairs={{2,4},{6,8},{10,12},{14,16},{18,20},{22,24},{26,28},{4,2},{8,6},{1... | collective-permute-start | bytes 737288 | tf_op jit(solution)/shard_map/ppermute | solution.py:347
  41.2 10.7 %collective-permute-start.14 = (f32[5,3,32,128]{3,2,1,0:T(8,128)S(1)}, f32[5,3,32,128]{3,2,1,0:T(8,128)S(1)}, u32[]{:S(2)}, u32[]{:S(2)}) collective-permute-start(f32[5,3,32,128]{3,2,1,0:T(8,128)S(1)} %get-tuple-element.56.refs_0_), channel_id=1, source_target_pairs={{0,2},{2,0},{4,6},{6,4},{8,10},{10,8},{12,14},{14,12},{16,18},{18,... | collective-permute-start | bytes 737288 | tf_op jit(solution)/shard_map/ppermute | solution.py:343
  42.8 11.8 %collective-permute-start.17 = (f32[5,3,32,128]{3,2,1,0:T(8,128)S(1)}, f32[5,3,32,128]{3,2,1,0:T(8,128)S(1)}, u32[]{:S(2)}, u32[]{:S(2)}) collective-permute-start(f32[5,3,32,128]{3,2,1,0:T(8,128)S(1)} %get-tuple-element.57.refs_3_), channel_id=1, source_target_pairs={{2,4},{6,8},{10,12},{14,16},{18,20},{22,24},{26,28},{4,2},{8,6},{1... | collective-permute-start | bytes 737288 | tf_op jit(solution)/shard_map/ppermute | solution.py:347
  44.8 9.7 %collective-permute-start.16 = (f32[5,3,32,128]{3,2,1,0:T(8,128)S(1)}, f32[5,3,32,128]{3,2,1,0:T(8,128)S(1)}, u32[]{:S(2)}, u32[]{:S(2)}) collective-permute-start(f32[5,3,32,128]{3,2,1,0:T(8,128)S(1)} %get-tuple-element.57.refs_3_), channel_id=1, source_target_pairs={{0,2},{2,0},{4,6},{6,4},{8,10},{10,8},{12,14},{14,12},{16,18},{18,... | collective-permute-start | bytes 737288 | tf_op jit(solution)/shard_map/ppermute | solution.py:343
  50.6 13.2 %copy-start.1 = (f32[5,6,64,128]{3,2,1,0:T(8,128)S(1)}, f32[5,6,64,128]{3,2,1,0:T(8,128)}, u32[]{:S(2)}) copy-start(f32[5,6,64,128]{3,2,1,0:T(8,128)} %z_ref.5) | copy-start | bytes 2949124
  50.6 8.9 %collective-permute-start.18 = (f32[5,3,32,128]{3,2,1,0:T(8,128)S(1)}, f32[5,3,32,128]{3,2,1,0:T(8,128)S(1)}, u32[]{:S(2)}, u32[]{:S(2)}) collective-permute-start(f32[5,3,32,128]{3,2,1,0:T(8,128)S(1)} %get-tuple-element.59), channel_id=1, source_target_pairs={{0,1},{1,0},{2,3},{3,2},{4,5},{5,4},{6,7},{7,6},{8,9},{9,8},{10,11... | collective-permute-start | bytes 737288 | tf_op jit(solution)/shard_map/ppermute | solution.py:340
  56.6 7.2 %collective-permute-start.19 = (f32[5,3,32,128]{3,2,1,0:T(8,128)S(1)}, f32[5,3,32,128]{3,2,1,0:T(8,128)S(1)}, u32[]{:S(2)}, u32[]{:S(2)}) collective-permute-start(f32[5,3,32,128]{3,2,1,0:T(8,128)S(1)} %get-tuple-element.60), channel_id=1, source_target_pairs={{0,1},{1,0},{2,3},{3,2},{4,5},{5,4},{6,7},{7,6},{8,9},{9,8},{10,11... | collective-permute-start | bytes 737288 | tf_op jit(solution)/shard_map/ppermute | solution.py:340
  (1 other events, 1.2 us)

commit v7 on v6

--- a/solution.py
+++ b/solution.py
@@ -304,19 +304,40 @@
             own_ref[i, j], send_ref[i, j] = unzip_lanes(total[2 * j], total[2 * j + 1])
 
 
-def finish(chunks, z_ref, *refs):
-    second = lax.axis_index("inner") == 1
-    own, oth, (out_ref, staged, sems) = refs[:chunks], refs[chunks : 2 * chunks], refs[2 * chunks :]
+def left_and_second_product(index_ref, *refs):
+    sources, left, rest = refs[:6], refs[6:12], refs[12:]
+    own_ref, send_ref, l_both, *scratch = rest
+    left_blocks(2, *left, l_both)
+    second_product(True, index_ref, *sources, l_both, own_ref, send_ref, *scratch)
+
+
+def turned_back(start, half, own, oth):
+    depth, lanes = own.shape
+    parts = []
+    for part in (own, oth):
+        parts += [jnp.zeros((start, lanes), part.dtype), part]
+        parts += [jnp.zeros((half - start - depth, lanes), part.dtype)]
+    turned = jnp.concatenate([part for part in parts if part.shape[0]], axis=0).T
+    return jnp.where(lax.axis_index("inner") == 1, swapped(turned), turned)
+
+
+def begin_finish(z_ref, own_ref, oth_ref, out_ref):
     rows, slots, half, lanes = z_ref.shape
+    for i in range(rows):
+        for j in range(slots // 2):
+            turned = turned_back(0, half, own_ref[i, j], oth_ref[i, j])
+            pair = slice(2 * j, 2 * j + 2)
+            out_ref[i, pair] = 2.0 * z_ref[i, pair] - turned.reshape(2, half, lanes)
+
+
+def finish(begun_ref, own_ref, oth_ref, out_ref, staged, sems):
+    rows, slots, half, lanes = begun_ref.shape
     copies = []
     for i in range(rows):
         for j in range(slots // 2):
-            stack = jnp.concatenate([ref[i, j] for ref in own + oth], axis=0)
-            turned = stack.T
-            turned = jnp.where(second, swapped(turned), turned)
-            staged[i, 2 * j : 2 * j + 2] = (
-                2.0 * z_ref[i, 2 * j : 2 * j + 2] - turned.reshape(2, half, lanes)
-            )
+            turned = turned_back(half - own_ref.shape[2], half, own_ref[i, j], oth_ref[i, j])
+            pair = slice(2 * j, 2 * j + 2)
+            staged[i, pair] = begun_ref[i, pair] - turned.reshape(2, half, lanes)
         copies.append(pltpu.make_async_copy(staged.at[i], out_ref.at[i], sems.at[i]))
         copies[-1].start()
     for copy in copies:
@@ -375,14 +396,8 @@
     j_oth = across(later)
     off_oth = [off_swap(x) for x in z_oth]
     on_oth = [on_swap(x) for x in z_oth]
-    later, z_oth[1] = after((z_own, z_oth[1]))
-    z_rest = across(later)
     later, off_own = after((hardness_blocks, off_own))
     j_own = list(take_rows(later))
-    left = call(
-        functools.partial(left_blocks, len(CHUNKS)), bf16((rows, slots * lanes, 2 * lanes)), "left_blocks"
-    )(z_own, z_rest, *z_send, *z_oth)
-
     blocks = 3 * rows * slots + 1
     bf16_buffer = functools.partial(pltpu.VMEM, dtype=jnp.bfloat16)
 
@@ -404,18 +419,21 @@
             specs=[smem, vmem, vmem, hbm, vmem] + [vmem] * len(j_rows),
         )(flat_one, *near, off_own, off_oth, *j_rows)
 
-    def second(packed, depth, products):
+    def second(body, name, depth, operands, *more):
         return call(
-            functools.partial(second_product, packed),
-            (f32((rows, pairs, depth, lanes)),) * 2,
-            "second_product",
+            body,
+            (f32((rows, pairs, depth, lanes)),) * 2 + more,
+            name,
             scratch=[bf16_buffer((blocks, depth, lanes))] * 2
             + [bf16_buffer((slots * depth, slots * lanes))] * 2,
-            specs=[smem] + [vmem] * 7,
-        )(flat_two, *products, left)
+            specs=[smem] + [vmem] * len(operands),
+        )(flat_two, *operands)
 
     depth_one, depth_two = CHUNKS
-    near = beside(0, depth_one, z_oth[0], on_oth[0])
+    z_near, j_own[0] = after((z_oth[0], j_own[0]))
+    near = beside(0, depth_one, z_near, on_oth[0])
+    later, *near = after((z_own, *near))
+    z_rest = across(later)
     (one,) = first(first_half_product, "first_half_product", 1, 0, depth_one, near, off_oth[0], j_own)
     one_on, one_off = on_swap(one), off_swap(one)
     j_other = take_rows(j_oth)
@@ -425,23 +443,30 @@
     three = first(first_product, "first_product", 2, depth_one, depth_two, near, off_oth[1], (*j_own, *j_other))
     three_on, three_off = [on_swap(x) for x in three], [off_swap(x) for x in three]
 
-    own, oth = [], []
-    for packed, depth, products in (
-        (True, depth_one, (one, one_on, one_off, two, two_on, two_off)),
-        (False, depth_two, tuple(x[h] for h in range(2) for x in (three, three_on, three_off))),
-    ):
-        mine, send = second(packed, depth, products)
-        own.append(mine)
-        oth.append(across(send))
+    mine_one, send_one, left = second(
+        left_and_second_product,
+        "left_and_second_product",
+        depth_one,
+        (one, one_on, one_off, two, two_on, two_off, z_own, z_rest, *z_send, *z_oth),
+        bf16((rows, slots * lanes, 2 * lanes)),
+    )
+    mine_two, send_two = second(
+        functools.partial(second_product, False),
+        "second_product",
+        depth_two,
+        (*(x[h] for h in range(2) for x in (three, three_on, three_off)), left),
+    )
+    begun = call(begin_finish, f32(inverse_blocks.shape), "begin_finish", specs=[vmem] * 3)(
+        inverse_blocks, mine_one, across(send_one)
+    )
     return call(
-        functools.partial(finish, len(CHUNKS)),
+        finish,
         f32(inverse_blocks.shape),
         "finish",
         scratch=[pltpu.VMEM(inverse_blocks.shape, jnp.float32), pltpu.SemaphoreType.DMA((rows,))],
-        specs=[vmem] * (1 + 2 * len(CHUNKS)),
+        specs=[vmem] * 3,
         out_specs=anywhere,
-        nbytes=12 << 18,
-    )(inverse_blocks, *own, *oth)
+    )(begun, mine_two, across(send_two))
 
 
 def solution(mesh):

time: 65.8 us -> 63.9 us (0.971)
  waiting for transfers between devices: 18.5 us -> 17 us
    ppermute x6, waiting for transfers between devices: 10.4 us -> 8 us  [across(): return lax.ppermute(x, 'inner', [(0, 1), (1, 0)])]
    ppermute x7, starting transfers between devices: 7.23 us -> 5.1 us  [on_swap(): return lax.ppermute(x, 'rows', [(i, i ^ 1) for i in range(count)])]
    ppermute x6, starting transfers between devices: 3.81 us -> 5.22 us  [across(): return lax.ppermute(x, 'inner', [(0, 1), (1, 0)])]
    ppermute x7, waiting for transfers between devices: 8.04 us -> 8.99 us  [off_swap(): return lax.ppermute(x, 'rows', inside + [(b, a) for a, b in inside])]
  transfers between devices with their start and end apart: 20 -> 20, of which waited for: 9 -> 7; matrix products, arithmetic and copies ran while one was open for 0% -> 0% of each run, Pallas kernels for 24% -> 26%
where the time goes in v7:
time: 63.9 us; the launch traced here: 63.6 us
  starting transfers between devices  26.9 us (42%)
  Pallas kernels  18.1 us (28%)
  waiting for transfers between devices  17 us (27%)
  local copies, waits for them, and re-layouts  1.41 us (2%)
    ppermute x7, starting transfers between devices, off_swap(): return lax.ppermute(x, 'rows', inside + [(b, a) for a, b in inside])  16.6 us
    ppermute x7, waiting for transfers between devices, off_swap(): return lax.ppermute(x, 'rows', inside + [(b, a) for a, b in inside])  8.99 us
    ppermute x6, waiting for transfers between devices, across(): return lax.ppermute(x, 'inner', [(0, 1), (1, 0)])  8 us
    pallas_call x3, Pallas kernels, first(): call(functools.partial(body, start), (f32((rows, pairs, depth, lanes)),)...  5.7 us
    ppermute x6, starting transfers between devices, across(): return lax.ppermute(x, 'inner', [(0, 1), (1, 0)])  5.22 us
    ppermute x7, starting transfers between devices, on_swap(): return lax.ppermute(x, 'rows', [(i, i ^ 1) for i in range(count)])  5.1 us
    pallas_call x2, Pallas kernels, second(): call(body, (f32((rows, pairs, depth, lanes)),) * 2 + more, name, scratch=...  4.62 us
    pallas_call x1, Pallas kernels, half_shards(): flat_one, flat_two = find(hardness_pattern, inverse_pattern)  3.98 us
  transfers between devices with their start and end apart: 20, of which 7 were waited for; matrix products, arithmetic and copies ran while one was open for 0% of the time, Pallas kernels for 26%

profile of v7, /device:TPU:14, one launch (start us, length us, event | category | flops | bytes accessed | tf_op | source)
XLA Modules:
  0.0 63.6 jit_solution(11505237771291128176)
XLA Ops:
  0.0 1.2 %copy-done = f32[5,6,64,128]{3,2,1,0:T(8,128)S(1)} copy-done((f32[5,6,64,128]{3,2,1,0:T(8,128)S(1)}, f32[5,6,64,128]{3,2,1,0:T(8,128)}, u32[]{:S(2)}) %copy-start) | copy-done | bytes 983064
  2.5 1.9 %collective-permute-start.2 = (f32[5,3,64,128]{3,2,1,0:T(8,128)S(1)}, f32[5,3,64,128]{3,2,1,0:T(8,128)S(1)}, u32[]{:S(2)}, u32[]{:S(2)}) collective-permute-start(f32[5,3,64,128]{3,2,1,0:T(8,128)S(1)} %split_own.1.z_own.refs_6_), channel_id=1, source_target_pairs={{2,4},{6,8},{10,12},{14,16},{18,20},{22,24},{26,28},{4,2},{8,6},{1... | collective-permute-start | bytes 1474568 | tf_op jit(solution)/shard_map/ppermute | solution.py:368
  4.4 1.6 %collective-permute-start.1 = (f32[5,3,32,128]{3,2,1,0:T(8,128)S(1)}, f32[5,3,32,128]{3,2,1,0:T(8,128)S(1)}, u32[]{:S(2)}, u32[]{:S(2)}) collective-permute-start(f32[5,3,32,128]{3,2,1,0:T(8,128)S(1)} %get-tuple-element.37.refs_0_.refs_8_), channel_id=1, source_target_pairs={{0,1},{1,0},{2,3},{3,2},{4,5},{5,4},{6,7},{7,6},{8,9},{9,8},{10,11... | collective-permute-start | bytes 737288 | tf_op jit(solution)/shard_map/ppermute | solution.py:361
  6.0 1.4 %collective-permute-start.3 = (f32[5,3,64,128]{3,2,1,0:T(8,128)S(1)}, f32[5,3,64,128]{3,2,1,0:T(8,128)S(1)}, u32[]{:S(2)}, u32[]{:S(2)}) collective-permute-start(f32[5,3,64,128]{3,2,1,0:T(8,128)S(1)} %split_own.1.z_own.refs_6_), channel_id=1, source_target_pairs={{0,2},{2,0},{4,6},{6,4},{8,10},{10,8},{12,14},{14,12},{16,18},{18,... | collective-permute-start | bytes 1474568 | tf_op jit(solution)/shard_map/ppermute | solution.py:364
  7.5 4.0 %find_blocks.1 = (s32[120]{0:T(128)S(1)}, s32[180]{0:T(256)S(1)}) custom-call(s32[5,4]{1,0:T(8,128)S(1)} %copy.5.left_ref, s32[80,6]{1,0:T(8,128)S(1)} %copy.6.pattern_ref), custom_call_target="tpu_custom_call" | custom-call | tf_op jit(solution)/shard_map/find_blocks/pallas_call | solution.py:393
  12.1 2.7 %collective-permute-done.1.z_oth.refs_10_ = f32[5,3,32,128]{3,2,1,0:T(8,128)S(1)} collective-permute-done((f32[5,3,32,128]{3,2,1,0:T(8,128)S(1)}, f32[5,3,32,128]{3,2,1,0:T(8,128)S(1)}, u32[]{:S(2)}, u32[]{:S(2)}) %collective-permute-start.1) | collective-permute-done | bytes 245792 | tf_op jit(solution)/shard_map/ppermute | solution.py:361
  14.9 2.6 %collective-permute-start.5 = (f32[5,3,32,128]{3,2,1,0:T(8,128)S(1)}, f32[5,3,32,128]{3,2,1,0:T(8,128)S(1)}, u32[]{:S(2)}, u32[]{:S(2)}) collective-permute-start(f32[5,3,32,128]{3,2,1,0:T(8,128)S(1)} %collective-permute-done.1.z_oth.refs_10_), channel_id=1, source_target_pairs={{2,4},{6,8},{10,12},{14,16},{18,20},{22,24},{26,28},{4,2},{8,6},{1... | collective-permute-start | bytes 737288 | tf_op jit(solution)/shard_map/ppermute | solution.py:368
  18.5 1.6 %collective-permute-start.11 = (f32[5,3,64,128]{3,2,1,0:T(8,128)S(1)}, f32[5,3,64,128]{3,2,1,0:T(8,128)S(1)}, u32[]{:S(2)}, u32[]{:S(2)}) collective-permute-start(f32[5,3,64,128]{3,2,1,0:T(8,128)S(1)} %split_own.1.z_own.refs_6_), channel_id=1, source_target_pairs={{0,1},{1,0},{2,3},{3,2},{4,5},{5,4},{6,7},{7,6},{8,9},{9,8},{10,11... | collective-permute-start | bytes 1474568 | tf_op jit(solution)/shard_map/ppermute | solution.py:361
  20.1 1.9 %collective-permute-start.14 = (f32[5,3,32,128]{3,2,1,0:T(8,128)S(1)}, f32[5,3,32,128]{3,2,1,0:T(8,128)S(1)}, u32[]{:S(2)}, u32[]{:S(2)}) collective-permute-start(f32[5,3,32,128]{3,2,1,0:T(8,128)S(1)} %collective-permute-done.refs_11_.z_oth), channel_id=1, source_target_pairs={{2,4},{6,8},{10,12},{14,16},{18,20},{22,24},{26,28},{4,2},{8,6},{1... | collective-permute-start | bytes 737288 | tf_op jit(solution)/shard_map/ppermute | solution.py:368
  22.0 3.0 %collective-permute-done.5.off_oth = f32[5,3,32,128]{3,2,1,0:T(8,128)S(1)} collective-permute-done((f32[5,3,32,128]{3,2,1,0:T(8,128)S(1)}, f32[5,3,32,128]{3,2,1,0:T(8,128)S(1)}, u32[]{:S(2)}, u32[]{:S(2)}) %collective-permute-start.5) | collective-permute-done | bytes 245792 | tf_op jit(solution)/shard_map/ppermute | solution.py:368
  25.0 1.9 %first_half_product.2.refs_0_ = f32[5,3,32,128]{3,2,1,0:T(8,128)S(1)} custom-call(s32[120]{0:T(128)S(1)} %get-tuple-element.43.index_ref, bf16[60,32,128]{2,1,0:T(8,128)(2,1)S(1)} %get-tuple-element.50.near_high, bf16[60,32,128]{2,1,0:T(8,128)(2,1)S(1)} %get-tuple-element.51.near_low, f32[5,3,64,128]{3,2,1,0:T(8,128)S(1)} %collective-permute-done.2.off_own, ...), custom_call_target="tpu_custom_call" | custom-call | tf_op jit(solution)/shard_map/first_half_product/pallas_call | solution.py:410
  26.9 2.9 %collective-permute-start.7 = (f32[5,3,32,128]{3,2,1,0:T(8,128)S(1)}, f32[5,3,32,128]{3,2,1,0:T(8,128)S(1)}, u32[]{:S(2)}, u32[]{:S(2)}) collective-permute-start(f32[5,3,32,128]{3,2,1,0:T(8,128)S(1)} %first_half_product.2.refs_0_), channel_id=1, source_target_pairs={{2,4},{6,8},{10,12},{14,16},{18,20},{22,24},{26,28},{4,2},{8,6},{1... | collective-permute-start | bytes 737288 | tf_op jit(solution)/shard_map/ppermute | solution.py:368
  30.2 1.9 %first_half_product.3.refs_3_ = f32[5,3,32,128]{3,2,1,0:T(8,128)S(1)} custom-call(s32[120]{0:T(128)S(1)} %get-tuple-element.43.index_ref, bf16[60,32,128]{2,1,0:T(8,128)(2,1)S(1)} %get-tuple-element.50.near_high, bf16[60,32,128]{2,1,0:T(8,128)(2,1)S(1)} %get-tuple-element.51.near_low, f32[5,3,64,128]{3,2,1,0:T(8,128)S(1)} %collective-permute-done.2.off_own, ...), custom_call_target="tpu_custom_call" | custom-call | tf_op jit(solution)/shard_map/first_half_product/pallas_call | solution.py:410
  32.1 2.6 %collective-permute-start.10 = (f32[5,3,32,128]{3,2,1,0:T(8,128)S(1)}, f32[5,3,32,128]{3,2,1,0:T(8,128)S(1)}, u32[]{:S(2)}, u32[]{:S(2)}) collective-permute-start(f32[5,3,32,128]{3,2,1,0:T(8,128)S(1)} %first_half_product.3.refs_3_), channel_id=1, source_target_pairs={{2,4},{6,8},{10,12},{14,16},{18,20},{22,24},{26,28},{4,2},{8,6},{1... | collective-permute-start | bytes 737288 | tf_op jit(solution)/shard_map/ppermute | solution.py:368
  35.1 1.6 %collective-permute-start.9 = (f32[5,3,32,128]{3,2,1,0:T(8,128)S(1)}, f32[5,3,32,128]{3,2,1,0:T(8,128)S(1)}, u32[]{:S(2)}, u32[]{:S(2)}) collective-permute-start(f32[5,3,32,128]{3,2,1,0:T(8,128)S(1)} %first_half_product.3.refs_3_), channel_id=1, source_target_pairs={{0,2},{2,0},{4,6},{6,4},{8,10},{10,8},{12,14},{14,12},{16,18},{18,... | collective-permute-start | bytes 737288 | tf_op jit(solution)/shard_map/ppermute | solution.py:364
  36.7 1.9 %first_product.1 = (f32[5,3,32,128]{3,2,1,0:T(8,128)S(1)}, f32[5,3,32,128]{3,2,1,0:T(8,128)S(1)}) custom-call(s32[120]{0:T(128)S(1)} %get-tuple-element.43.index_ref, bf16[60,32,128]{2,1,0:T(8,128)(2,1)S(1)} %get-tuple-element.62.near_high, bf16[60,32,128]{2,1,0:T(8,128)(2,1)S(1)} %get-tuple-element.63.near_low, ...), custom_call_target="tpu_custom_call" | custom-call | tf_op jit(solution)/shard_map/first_product/pallas_call | solution.py:410
  38.6 1.9 %collective-permute-start.16 = (f32[5,3,32,128]{3,2,1,0:T(8,128)S(1)}, f32[5,3,32,128]{3,2,1,0:T(8,128)S(1)}, u32[]{:S(2)}, u32[]{:S(2)}) collective-permute-start(f32[5,3,32,128]{3,2,1,0:T(8,128)S(1)} %get-tuple-element.64.refs_0_), channel_id=1, source_target_pairs={{2,4},{6,8},{10,12},{14,16},{18,20},{22,24},{26,28},{4,2},{8,6},{1... | collective-permute-start | bytes 737288 | tf_op jit(solution)/shard_map/ppermute | solution.py:368
  41.6 2.7 %collective-permute-start.18 = (f32[5,3,32,128]{3,2,1,0:T(8,128)S(1)}, f32[5,3,32,128]{3,2,1,0:T(8,128)S(1)}, u32[]{:S(2)}, u32[]{:S(2)}) collective-permute-start(f32[5,3,32,128]{3,2,1,0:T(8,128)S(1)} %get-tuple-element.65.refs_3_), channel_id=1, source_target_pairs={{2,4},{6,8},{10,12},{14,16},{18,20},{22,24},{26,28},{4,2},{8,6},{1... | collective-permute-start | bytes 737288 | tf_op jit(solution)/shard_map/ppermute | solution.py:368
  45.3 2.6 %left_and_second_product.1 = (f32[5,3,32,128]{3,2,1,0:T(8,128)S(1)}, f32[5,3,32,128]{3,2,1,0:T(8,128)S(1)}, bf16[5,768,256]{2,1,0:T(8,128)(2,1)S(1)}) custom-call(s32[180]{0:T(256)S(1)} %get-tuple-element.39.index_ref, f32[5,3,32,128]{3,2,1,0:T(8,128)S(1)} %first_half_product.2.refs_0_, f32[5,3,32,128]{3,2,1,0:T(8,128)S(1)} %collective-permute-done.6.refs_1_, ...), custom_call_target="tpu_custom_call" | custom-call | tf_op jit(solution)/shard_map/left_and_second_product/pallas_call | solution.py:423
  48.4 2.9 %collective-permute-done.16.refs_2_ = f32[5,3,32,128]{3,2,1,0:T(8,128)S(1)} collective-permute-done((f32[5,3,32,128]{3,2,1,0:T(8,128)S(1)}, f32[5,3,32,128]{3,2,1,0:T(8,128)S(1)}, u32[]{:S(2)}, u32[]{:S(2)}) %collective-permute-start.16) | collective-permute-done | bytes 245792 | tf_op jit(solution)/shard_map/ppermute | solution.py:368
  51.4 2.6 %collective-permute-done.18.refs_5_ = f32[5,3,32,128]{3,2,1,0:T(8,128)S(1)} collective-permute-done((f32[5,3,32,128]{3,2,1,0:T(8,128)S(1)}, f32[5,3,32,128]{3,2,1,0:T(8,128)S(1)}, u32[]{:S(2)}, u32[]{:S(2)}) %collective-permute-start.18) | collective-permute-done | bytes 245792 | tf_op jit(solution)/shard_map/ppermute | solution.py:368
  54.0 2.0 %second_product.1 = (f32[5,3,32,128]{3,2,1,0:T(8,128)S(1)}, f32[5,3,32,128]{3,2,1,0:T(8,128)S(1)}) custom-call(s32[180]{0:T(256)S(1)} %get-tuple-element.39.index_ref, f32[5,3,32,128]{3,2,1,0:T(8,128)S(1)} %get-tuple-element.64.refs_0_, f32[5,3,32,128]{3,2,1,0:T(8,128)S(1)} %collective-permute-done.15.refs_1_, ...), custom_call_target="tpu_custom_call" | custom-call | tf_op jit(solution)/shard_map/second_product/pallas_call | solution.py:423
  57.4 4.8 %collective-permute-done.19.oth_ref = f32[5,3,32,128]{3,2,1,0:T(8,128)S(1)} collective-permute-done((f32[5,3,32,128]{3,2,1,0:T(8,128)S(1)}, f32[5,3,32,128]{3,2,1,0:T(8,128)S(1)}, u32[]{:S(2)}, u32[]{:S(2)}) %collective-permute-start.19) | collective-permute-done | bytes 245792 | tf_op jit(solution)/shard_map/ppermute | solution.py:361
  62.3 1.4 %finish.1 = f32[5,6,64,128]{3,2,1,0:T(8,128)} custom-call(f32[5,6,64,128]{3,2,1,0:T(8,128)S(1)} %begin_finish.1.begun_ref, f32[5,3,32,128]{3,2,1,0:T(8,128)S(1)} %get-tuple-element.67.own_ref, f32[5,3,32,128]{3,2,1,0:T(8,128)S(1)} %collective-permute-done.19.oth_ref), custom_call_target="tpu_custom_call" | custom-call | tf_op jit(solution)/shard_map/finish/pallas_call | solution.py:462
  (42 shorter events, 7.6 us)
Async XLA Ops:
  1.2 6.1 %copy-start.4 = (s32[5,4]{0,1:T(4,128)S(1)}, s32[5,4]{0,1:T(4,128)}, u32[]{:S(2)}) copy-start(s32[5,4]{0,1:T(4,128)} %param.6) | copy-start | bytes 244
  1.2 6.2 %copy-start.3 = (s32[80,6]{0,1:T(8,128)S(1)}, s32[80,6]{0,1:T(8,128)}, u32[]{:S(2)}) copy-start(s32[80,6]{0,1:T(8,128)} %param.7) | copy-start | bytes 5764
  1.2 10.3 %copy-start.2 = (f32[5,4,64,128]{3,2,1,0:T(8,128)S(1)}, f32[5,4,64,128]{3,2,1,0:T(8,128)}, u32[]{:S(2)}) copy-start(f32[5,4,64,128]{3,2,1,0:T(8,128)} %j_ref) | copy-start | bytes 1966084
  1.5 10.0 %collective-permute-start = (f32[5,3,32,128]{3,2,1,0:T(8,128)S(1)}, f32[5,3,32,128]{3,2,1,0:T(8,128)S(1)}, u32[]{:S(2)}, u32[]{:S(2)}) collective-permute-start(f32[5,3,32,128]{3,2,1,0:T(8,128)S(1)} %get-tuple-element.40.refs_9_), channel_id=1, source_target_pairs={{0,1},{1,0},{2,3},{3,2},{4,5},{5,4},{6,7},{7,6},{8,9},{9,8},{10,11... | collective-permute-start | bytes 737288 | tf_op jit(solution)/shard_map/ppermute | solution.py:361
  2.5 15.4 %collective-permute-start.2 = (f32[5,3,64,128]{3,2,1,0:T(8,128)S(1)}, f32[5,3,64,128]{3,2,1,0:T(8,128)S(1)}, u32[]{:S(2)}, u32[]{:S(2)}) collective-permute-start(f32[5,3,64,128]{3,2,1,0:T(8,128)S(1)} %split_own.1.z_own.refs_6_), channel_id=1, source_target_pairs={{2,4},{6,8},{10,12},{14,16},{18,20},{22,24},{26,28},{4,2},{8,6},{1... | collective-permute-start | bytes 1474568 | tf_op jit(solution)/shard_map/ppermute | solution.py:368
  4.4 10.5 %collective-permute-start.1 = (f32[5,3,32,128]{3,2,1,0:T(8,128)S(1)}, f32[5,3,32,128]{3,2,1,0:T(8,128)S(1)}, u32[]{:S(2)}, u32[]{:S(2)}) collective-permute-start(f32[5,3,32,128]{3,2,1,0:T(8,128)S(1)} %get-tuple-element.37.refs_0_.refs_8_), channel_id=1, source_target_pairs={{0,1},{1,0},{2,3},{3,2},{4,5},{5,4},{6,7},{7,6},{8,9},{9,8},{10,11... | collective-permute-start | bytes 737288 | tf_op jit(solution)/shard_map/ppermute | solution.py:361
  6.0 12.2 %collective-permute-start.3 = (f32[5,3,64,128]{3,2,1,0:T(8,128)S(1)}, f32[5,3,64,128]{3,2,1,0:T(8,128)S(1)}, u32[]{:S(2)}, u32[]{:S(2)}) collective-permute-start(f32[5,3,64,128]{3,2,1,0:T(8,128)S(1)} %split_own.1.z_own.refs_6_), channel_id=1, source_target_pairs={{0,2},{2,0},{4,6},{6,4},{8,10},{10,8},{12,14},{14,12},{16,18},{18,... | collective-permute-start | bytes 1474568 | tf_op jit(solution)/shard_map/ppermute | solution.py:364
  11.6 18.3 %collective-permute-start.8 = (f32[5,4,64,128]{3,2,1,0:T(8,128)S(1)}, f32[5,4,64,128]{3,2,1,0:T(8,128)S(1)}, u32[]{:S(2)}, u32[]{:S(2)}) collective-permute-start(f32[5,4,64,128]{3,2,1,0:T(8,128)S(1)} %copy-done.2), channel_id=1, source_target_pairs={{0,1},{1,0},{2,3},{3,2},{4,5},{5,4},{6,7},{7,6},{8,9},{9,8},{10,11... | collective-permute-start | bytes 1966088 | tf_op jit(solution)/shard_map/ppermute | solution.py:361
  14.9 3.3 %collective-permute-start.4 = (f32[5,3,32,128]{3,2,1,0:T(8,128)S(1)}, f32[5,3,32,128]{3,2,1,0:T(8,128)S(1)}, u32[]{:S(2)}, u32[]{:S(2)}) collective-permute-start(f32[5,3,32,128]{3,2,1,0:T(8,128)S(1)} %collective-permute-done.1.z_oth.refs_10_), channel_id=1, source_target_pairs={{0,2},{2,0},{4,6},{6,4},{8,10},{10,8},{12,14},{14,12},{16,18},{18,... | collective-permute-start | bytes 737288 | tf_op jit(solution)/shard_map/ppermute | solution.py:364
  14.9 10.1 %collective-permute-start.5 = (f32[5,3,32,128]{3,2,1,0:T(8,128)S(1)}, f32[5,3,32,128]{3,2,1,0:T(8,128)S(1)}, u32[]{:S(2)}, u32[]{:S(2)}) collective-permute-start(f32[5,3,32,128]{3,2,1,0:T(8,128)S(1)} %collective-permute-done.1.z_oth.refs_10_), channel_id=1, source_target_pairs={{2,4},{6,8},{10,12},{14,16},{18,20},{22,24},{26,28},{4,2},{8,6},{1... | collective-permute-start | bytes 737288 | tf_op jit(solution)/shard_map/ppermute | solution.py:368
  18.5 23.1 %collective-permute-start.11 = (f32[5,3,64,128]{3,2,1,0:T(8,128)S(1)}, f32[5,3,64,128]{3,2,1,0:T(8,128)S(1)}, u32[]{:S(2)}, u32[]{:S(2)}) collective-permute-start(f32[5,3,64,128]{3,2,1,0:T(8,128)S(1)} %split_own.1.z_own.refs_6_), channel_id=1, source_target_pairs={{0,1},{1,0},{2,3},{3,2},{4,5},{5,4},{6,7},{7,6},{8,9},{9,8},{10,11... | collective-permute-start | bytes 1474568 | tf_op jit(solution)/shard_map/ppermute | solution.py:361
  20.0 12.0 %collective-permute-start.13 = (f32[5,3,32,128]{3,2,1,0:T(8,128)S(1)}, f32[5,3,32,128]{3,2,1,0:T(8,128)S(1)}, u32[]{:S(2)}, u32[]{:S(2)}) collective-permute-start(f32[5,3,32,128]{3,2,1,0:T(8,128)S(1)} %collective-permute-done.refs_11_.z_oth), channel_id=1, source_target_pairs={{0,2},{2,0},{4,6},{6,4},{8,10},{10,8},{12,14},{14,12},{16,18},{18,... | collective-permute-start | bytes 737288 | tf_op jit(solution)/shard_map/ppermute | solution.py:364
  20.1 15.0 %collective-permute-start.14 = (f32[5,3,32,128]{3,2,1,0:T(8,128)S(1)}, f32[5,3,32,128]{3,2,1,0:T(8,128)S(1)}, u32[]{:S(2)}, u32[]{:S(2)}) collective-permute-start(f32[5,3,32,128]{3,2,1,0:T(8,128)S(1)} %collective-permute-done.refs_11_.z_oth), channel_id=1, source_target_pairs={{2,4},{6,8},{10,12},{14,16},{18,20},{22,24},{26,28},{4,2},{8,6},{1... | collective-permute-start | bytes 737288 | tf_op jit(solution)/shard_map/ppermute | solution.py:368
  26.9 11.7 %collective-permute-start.7 = (f32[5,3,32,128]{3,2,1,0:T(8,128)S(1)}, f32[5,3,32,128]{3,2,1,0:T(8,128)S(1)}, u32[]{:S(2)}, u32[]{:S(2)}) collective-permute-start(f32[5,3,32,128]{3,2,1,0:T(8,128)S(1)} %first_half_product.2.refs_0_), channel_id=1, source_target_pairs={{2,4},{6,8},{10,12},{14,16},{18,20},{22,24},{26,28},{4,2},{8,6},{1... | collective-permute-start | bytes 737288 | tf_op jit(solution)/shard_map/ppermute | solution.py:368
  29.8 10.7 %collective-permute-start.6 = (f32[5,3,32,128]{3,2,1,0:T(8,128)S(1)}, f32[5,3,32,128]{3,2,1,0:T(8,128)S(1)}, u32[]{:S(2)}, u32[]{:S(2)}) collective-permute-start(f32[5,3,32,128]{3,2,1,0:T(8,128)S(1)} %first_half_product.2.refs_0_), channel_id=1, source_target_pairs={{0,2},{2,0},{4,6},{6,4},{8,10},{10,8},{12,14},{14,12},{16,18},{18,... | collective-permute-start | bytes 737288 | tf_op jit(solution)/shard_map/ppermute | solution.py:364
  32.1 12.2 %collective-permute-start.10 = (f32[5,3,32,128]{3,2,1,0:T(8,128)S(1)}, f32[5,3,32,128]{3,2,1,0:T(8,128)S(1)}, u32[]{:S(2)}, u32[]{:S(2)}) collective-permute-start(f32[5,3,32,128]{3,2,1,0:T(8,128)S(1)} %first_half_product.3.refs_3_), channel_id=1, source_target_pairs={{2,4},{6,8},{10,12},{14,16},{18,20},{22,24},{26,28},{4,2},{8,6},{1... | collective-permute-start | bytes 737288 | tf_op jit(solution)/shard_map/ppermute | solution.py:368
  35.1 10.2 %collective-permute-start.9 = (f32[5,3,32,128]{3,2,1,0:T(8,128)S(1)}, f32[5,3,32,128]{3,2,1,0:T(8,128)S(1)}, u32[]{:S(2)}, u32[]{:S(2)}) collective-permute-start(f32[5,3,32,128]{3,2,1,0:T(8,128)S(1)} %first_half_product.3.refs_3_), channel_id=1, source_target_pairs={{0,2},{2,0},{4,6},{6,4},{8,10},{10,8},{12,14},{14,12},{16,18},{18,... | collective-permute-start | bytes 737288 | tf_op jit(solution)/shard_map/ppermute | solution.py:364
  38.6 12.8 %collective-permute-start.16 = (f32[5,3,32,128]{3,2,1,0:T(8,128)S(1)}, f32[5,3,32,128]{3,2,1,0:T(8,128)S(1)}, u32[]{:S(2)}, u32[]{:S(2)}) collective-permute-start(f32[5,3,32,128]{3,2,1,0:T(8,128)S(1)} %get-tuple-element.64.refs_0_), channel_id=1, source_target_pairs={{2,4},{6,8},{10,12},{14,16},{18,20},{22,24},{26,28},{4,2},{8,6},{1... | collective-permute-start | bytes 737288 | tf_op jit(solution)/shard_map/ppermute | solution.py:368
  40.5 10.8 %collective-permute-start.15 = (f32[5,3,32,128]{3,2,1,0:T(8,128)S(1)}, f32[5,3,32,128]{3,2,1,0:T(8,128)S(1)}, u32[]{:S(2)}, u32[]{:S(2)}) collective-permute-start(f32[5,3,32,128]{3,2,1,0:T(8,128)S(1)} %get-tuple-element.64.refs_0_), channel_id=1, source_target_pairs={{0,2},{2,0},{4,6},{6,4},{8,10},{10,8},{12,14},{14,12},{16,18},{18,... | collective-permute-start | bytes 737288 | tf_op jit(solution)/shard_map/ppermute | solution.py:364
  41.6 12.4 %collective-permute-start.18 = (f32[5,3,32,128]{3,2,1,0:T(8,128)S(1)}, f32[5,3,32,128]{3,2,1,0:T(8,128)S(1)}, u32[]{:S(2)}, u32[]{:S(2)}) collective-permute-start(f32[5,3,32,128]{3,2,1,0:T(8,128)S(1)} %get-tuple-element.65.refs_3_), channel_id=1, source_target_pairs={{2,4},{6,8},{10,12},{14,16},{18,20},{22,24},{26,28},{4,2},{8,6},{1... | collective-permute-start | bytes 737288 | tf_op jit(solution)/shard_map/ppermute | solution.py:368
  44.3 9.7 %collective-permute-start.17 = (f32[5,3,32,128]{3,2,1,0:T(8,128)S(1)}, f32[5,3,32,128]{3,2,1,0:T(8,128)S(1)}, u32[]{:S(2)}, u32[]{:S(2)}) collective-permute-start(f32[5,3,32,128]{3,2,1,0:T(8,128)S(1)} %get-tuple-element.65.refs_3_), channel_id=1, source_target_pairs={{0,2},{2,0},{4,6},{6,4},{8,10},{10,8},{12,14},{14,12},{16,18},{18,... | collective-permute-start | bytes 737288 | tf_op jit(solution)/shard_map/ppermute | solution.py:364
  47.9 8.9 %copy-start.1 = (f32[5,6,64,128]{3,2,1,0:T(8,128)S(1)}, f32[5,6,64,128]{3,2,1,0:T(8,128)}, u32[]{:S(2)}) copy-start(f32[5,6,64,128]{3,2,1,0:T(8,128)} %z_ref.5) | copy-start | bytes 2949124
  47.9 8.9 %collective-permute-start.12 = (f32[5,3,32,128]{3,2,1,0:T(8,128)S(1)}, f32[5,3,32,128]{3,2,1,0:T(8,128)S(1)}, u32[]{:S(2)}, u32[]{:S(2)}) collective-permute-start(f32[5,3,32,128]{3,2,1,0:T(8,128)S(1)} %get-tuple-element.61), channel_id=1, source_target_pairs={{0,1},{1,0},{2,3},{3,2},{4,5},{5,4},{6,7},{7,6},{8,9},{9,8},{10,11... | collective-permute-start | bytes 737288 | tf_op jit(solution)/shard_map/ppermute | solution.py:361
  56.0 6.3 %collective-permute-start.19 = (f32[5,3,32,128]{3,2,1,0:T(8,128)S(1)}, f32[5,3,32,128]{3,2,1,0:T(8,128)S(1)}, u32[]{:S(2)}, u32[]{:S(2)}) collective-permute-start(f32[5,3,32,128]{3,2,1,0:T(8,128)S(1)} %get-tuple-element.68), channel_id=1, source_target_pairs={{0,1},{1,0},{2,3},{3,2},{4,5},{5,4},{6,7},{7,6},{8,9},{9,8},{10,11... | collective-permute-start | bytes 737288 | tf_op jit(solution)/shard_map/ppermute | solution.py:361
  (1 other events, 1.2 us)

commit v8 on v7

--- a/solution.py
+++ b/solution.py
@@ -247,7 +247,8 @@
         total = gather_dot(index_ref, i, slots, 2 * pairs, z_high, z_low, lhs_high, lhs_low,
                            (j_both[i], j_both[i, : 2 * half]), ((1,), (1,)))
         total = total.reshape(2 * pairs, depth, lanes)
-        p_ref[i], p_rest_ref[i] = total[:pairs], total[pairs:]
+        part = p_ref.shape[2]
+        p_ref[i], p_rest_ref[i] = total[:, :part], total[:, part:]
 
 
 def first_half_product(start, index_ref, near_high, near_low, off_own, off_oth, rows_high, rows_low,
@@ -279,7 +280,8 @@
 
 
 def second_product(packed, index_ref, *refs):
-    sources, (l_both, own_ref, send_ref, p_high, p_low, lhs_high, lhs_low) = refs[:6], refs[6:]
+    count = 6 if packed else 3
+    sources, (l_both, own_ref, send_ref, p_high, p_low, lhs_high, lhs_low) = refs[:count], refs[count:]
     rows, pairs, depth, lanes = own_ref.shape
     slots = 2 * pairs
     blank = p_high.shape[0] - 1
@@ -288,13 +290,13 @@
     for g in range(3):
         for i in range(rows):
             for j in range(pairs):
-                blocks = sources[g][i, j], sources[3 + g][i, j]
-                places = j, pairs + j
+                at = (0, 2, 1)[g]
                 if packed:
-                    blocks = unzip_lanes(*blocks)
-                    places = 2 * j, 2 * j + 1
-                for slot, block in zip(places, blocks):
-                    at = (g * rows + i) * slots + slot
+                    blocks = unzip_lanes(sources[at][i, j], sources[3 + g][i, j])
+                else:
+                    blocks = sources[at][i, 2 * j], sources[at][i, 2 * j + 1]
+                for slot, block in enumerate(blocks):
+                    at = (g * rows + i) * slots + 2 * j + slot
                     p_high[at], p_low[at] = halves(block)
     for i in range(rows):
         total = gather_dot(index_ref, i, slots, slots, p_high, p_low, lhs_high, lhs_low,
@@ -330,12 +332,14 @@
             out_ref[i, pair] = 2.0 * z_ref[i, pair] - turned.reshape(2, half, lanes)
 
 
-def finish(begun_ref, own_ref, oth_ref, out_ref, staged, sems):
+def finish(begun_ref, own_one, own_two, oth_one, oth_two, out_ref, staged, sems):
     rows, slots, half, lanes = begun_ref.shape
     copies = []
     for i in range(rows):
         for j in range(slots // 2):
-            turned = turned_back(half - own_ref.shape[2], half, own_ref[i, j], oth_ref[i, j])
+            own = jnp.concatenate([own_one[i, j], own_two[i, j]], axis=0)
+            oth = jnp.concatenate([oth_one[i, j], oth_two[i, j]], axis=0)
+            turned = turned_back(half - own.shape[0], half, own, oth)
             pair = slice(2 * j, 2 * j + 2)
             staged[i, pair] = begun_ref[i, pair] - turned.reshape(2, half, lanes)
         copies.append(pltpu.make_async_copy(staged.at[i], out_ref.at[i], sems.at[i]))
@@ -387,10 +391,11 @@
     z_oth = [across(x) for x in z_send]
     off_own = off_swap(z_own)
     z_send = list(z_send)
-    on_own = on_swap(z_own)
     after = lax.optimization_barrier
     inverse_pattern, z_own = after((inverse_pattern, z_own))
     flat_one, flat_two = find(hardness_pattern, inverse_pattern)
+    later, flat_one = after((z_own, flat_one))
+    on_own = on_swap(later)
     z_oth[1], flat_one = after((z_oth[1], flat_one))
     later, flat_one = after((hardness_blocks, flat_one))
     j_oth = across(later)
@@ -406,10 +411,10 @@
             functools.partial(merge_near, start), (bf16((2 * rows * slots, depth, lanes)),) * 2, "merge_near"
         )(z_own, z_oth, on_own, on_oth)
 
-    def first(body, name, count, start, depth, near, off_oth, j_rows):
+    def first(body, name, shapes, start, depth, near, off_oth, j_rows):
         return call(
             functools.partial(body, start),
-            (f32((rows, pairs, depth, lanes)),) * count,
+            shapes,
             name,
             scratch=[pltpu.VMEM((rows, pairs, depth, lanes), jnp.float32)]
             + [bf16_buffer((blocks, depth, lanes))] * 2
@@ -434,28 +439,31 @@
     near = beside(0, depth_one, z_near, on_oth[0])
     later, *near = after((z_own, *near))
     z_rest = across(later)
-    (one,) = first(first_half_product, "first_half_product", 1, 0, depth_one, near, off_oth[0], j_own)
+    packs = (f32((rows, pairs, depth_one, lanes)),)
+    (one,) = first(first_half_product, "first_half_product", packs, 0, depth_one, near, off_oth[0], j_own)
     one_on, one_off = on_swap(one), off_swap(one)
     j_other = take_rows(j_oth)
-    (two,) = first(first_half_product, "first_half_product", 1, 0, depth_one, near, off_oth[0], j_other)
+    (two,) = first(first_half_product, "first_half_product", packs, 0, depth_one, near, off_oth[0], j_other)
     two_on, two_off = on_swap(two), off_swap(two)
     near = beside(depth_one, depth_two, z_oth[1], on_oth[1])
-    three = first(first_product, "first_product", 2, depth_one, depth_two, near, off_oth[1], (*j_own, *j_other))
+    parts = (f32((rows, slots, depth_two // 2, lanes)),) * 2
+    three = first(first_product, "first_product", parts, depth_one, depth_two, near, off_oth[1], (*j_own, *j_other))
     three_on, three_off = [on_swap(x) for x in three], [off_swap(x) for x in three]
 
     mine_one, send_one, left = second(
         left_and_second_product,
         "left_and_second_product",
         depth_one,
-        (one, one_on, one_off, two, two_on, two_off, z_own, z_rest, *z_send, *z_oth),
+        (one, one_off, one_on, two, two_on, two_off, z_own, z_rest, *z_send, *z_oth),
         bf16((rows, slots * lanes, 2 * lanes)),
     )
-    mine_two, send_two = second(
-        functools.partial(second_product, False),
-        "second_product",
-        depth_two,
-        (*(x[h] for h in range(2) for x in (three, three_on, three_off)), left),
-    )
+    mine_two, oth_two = [], []
+    for operands in zip(three, three_off, three_on):
+        mine, send = second(
+            functools.partial(second_product, False), "second_product", depth_two // 2, (*operands, left)
+        )
+        mine_two.append(mine)
+        oth_two.append(across(send))
     begun = call(begin_finish, f32(inverse_blocks.shape), "begin_finish", specs=[vmem] * 3)(
         inverse_blocks, mine_one, across(send_one)
     )
@@ -464,9 +472,9 @@
         f32(inverse_blocks.shape),
         "finish",
         scratch=[pltpu.VMEM(inverse_blocks.shape, jnp.float32), pltpu.SemaphoreType.DMA((rows,))],
-        specs=[vmem] * 3,
+        specs=[vmem] * 5,
         out_specs=anywhere,
-    )(begun, mine_two, across(send_two))
+    )(begun, *mine_two, *oth_two)
 
 
 def solution(mesh):

time: 63.9 us -> 64.8 us (1.014)
  the two profiles are of different devices: /device:TPU:14 before, /device:TPU:0 now
where the time goes in v8:
time: 64.8 us; the launch traced here: 64.5 us
  starting transfers between devices  29.7 us (46%)
  Pallas kernels  19.1 us (29%)
  waiting for transfers between devices  14 us (22%)
  local copies, waits for them, and re-layouts  1.41 us (2%)
    ppermute x7, starting transfers between devices, on_swap(): return lax.ppermute(x, 'rows', [(i, i ^ 1) for i in range(count)])  15.6 us
    ppermute x7, waiting for transfers between devices, across(): return lax.ppermute(x, 'inner', [(0, 1), (1, 0)])  13.4 us
    ppermute x7, starting transfers between devices, across(): return lax.ppermute(x, 'inner', [(0, 1), (1, 0)])  9.31 us
    pallas_call x3, Pallas kernels, first(): call(functools.partial(body, start), shapes, name, scratch=[pltpu.VMEM((r...  5.72 us
    pallas_call x3, Pallas kernels, second(): call(body, (f32((rows, pairs, depth, lanes)),) * 2 + more, name, scratch=...  5.68 us
    ppermute x7, starting transfers between devices, off_swap(): return lax.ppermute(x, 'rows', inside + [(b, a) for a, b in inside])  4.72 us
    pallas_call x1, Pallas kernels, half_shards(): flat_one, flat_two = find(hardness_pattern, inverse_pattern)  3.98 us
    pallas_call x1, Pallas kernels, half_shards(): call(finish, f32(inverse_blocks.shape), 'finish', scratch=[pltpu.VMEM(inv...  1.36 us
  transfers between devices with their start and end apart: 21, of which 6 were waited for; matrix products, arithmetic and copies ran while one was open for 0% of the time, Pallas kernels for 27%

profile of v8, /device:TPU:0, one launch (start us, length us, event | category | flops | bytes accessed | tf_op | source)
XLA Modules:
  0.0 64.5 jit_solution(5807592332530053220)
XLA Ops:
  0.0 1.2 %copy-done = f32[5,6,64,128]{3,2,1,0:T(8,128)S(1)} copy-done((f32[5,6,64,128]{3,2,1,0:T(8,128)S(1)}, f32[5,6,64,128]{3,2,1,0:T(8,128)}, u32[]{:S(2)}) %copy-start) | copy-done | bytes 983064
  1.5 3.0 %collective-permute-start = (f32[5,3,32,128]{3,2,1,0:T(8,128)S(1)}, f32[5,3,32,128]{3,2,1,0:T(8,128)S(1)}, u32[]{:S(2)}, u32[]{:S(2)}) collective-permute-start(f32[5,3,32,128]{3,2,1,0:T(8,128)S(1)} %get-tuple-element.44.refs_9_), channel_id=1, source_target_pairs={{0,1},{1,0},{2,3},{3,2},{4,5},{5,4},{6,7},{7,6},{8,9},{9,8},{10,11... | collective-permute-start | bytes 737288 | tf_op jit(solution)/shard_map/ppermute | solution.py:365
  5.9 4.0 %find_blocks.1 = (s32[120]{0:T(128)S(1)}, s32[180]{0:T(256)S(1)}) custom-call(s32[5,4]{1,0:T(8,128)S(1)} %copy.5.left_ref, s32[80,6]{1,0:T(8,128)S(1)} %copy.6.pattern_ref), custom_call_target="tpu_custom_call" | custom-call | tf_op jit(solution)/shard_map/find_blocks/pallas_call | solution.py:396
  9.9 3.3 %collective-permute-start.3 = (f32[5,3,64,128]{3,2,1,0:T(8,128)S(1)}, f32[5,3,64,128]{3,2,1,0:T(8,128)S(1)}, u32[]{:S(2)}, u32[]{:S(2)}) collective-permute-start(f32[5,3,64,128]{3,2,1,0:T(8,128)S(1)} %split_own.1.z_own.refs_6_), channel_id=1, source_target_pairs={{0,2},{2,0},{4,6},{6,4},{8,10},{10,8},{12,14},{14,12},{16,18},{18,... | collective-permute-start | bytes 1474568 | tf_op jit(solution)/shard_map/ppermute | solution.py:368
  13.2 1.5 %collective-permute-start.8 = (f32[5,4,64,128]{3,2,1,0:T(8,128)S(1)}, f32[5,4,64,128]{3,2,1,0:T(8,128)S(1)}, u32[]{:S(2)}, u32[]{:S(2)}) collective-permute-start(f32[5,4,64,128]{3,2,1,0:T(8,128)S(1)} %copy-done.2), channel_id=1, source_target_pairs={{0,1},{1,0},{2,3},{3,2},{4,5},{5,4},{6,7},{7,6},{8,9},{9,8},{10,11... | collective-permute-start | bytes 1966088 | tf_op jit(solution)/shard_map/ppermute | solution.py:365
  14.7 1.1 %collective-permute-done.1.z_oth.refs_10_ = f32[5,3,32,128]{3,2,1,0:T(8,128)S(1)} collective-permute-done((f32[5,3,32,128]{3,2,1,0:T(8,128)S(1)}, f32[5,3,32,128]{3,2,1,0:T(8,128)S(1)}, u32[]{:S(2)}, u32[]{:S(2)}) %collective-permute-start.1) | collective-permute-done | bytes 245792 | tf_op jit(solution)/shard_map/ppermute | solution.py:365
  17.6 1.9 %collective-permute-start.11 = (f32[5,3,64,128]{3,2,1,0:T(8,128)S(1)}, f32[5,3,64,128]{3,2,1,0:T(8,128)S(1)}, u32[]{:S(2)}, u32[]{:S(2)}) collective-permute-start(f32[5,3,64,128]{3,2,1,0:T(8,128)S(1)} %split_own.1.z_own.refs_6_), channel_id=1, source_target_pairs={{0,1},{1,0},{2,3},{3,2},{4,5},{5,4},{6,7},{7,6},{8,9},{9,8},{10,11... | collective-permute-start | bytes 1474568 | tf_op jit(solution)/shard_map/ppermute | solution.py:365
  19.5 2.4 %collective-permute-start.13 = (f32[5,3,32,128]{3,2,1,0:T(8,128)S(1)}, f32[5,3,32,128]{3,2,1,0:T(8,128)S(1)}, u32[]{:S(2)}, u32[]{:S(2)}) collective-permute-start(f32[5,3,32,128]{3,2,1,0:T(8,128)S(1)} %collective-permute-done.refs_11_.z_oth), channel_id=1, source_target_pairs={{0,2},{2,0},{4,6},{6,4},{8,10},{10,8},{12,14},{14,12},{16,18},{18,... | collective-permute-start | bytes 737288 | tf_op jit(solution)/shard_map/ppermute | solution.py:368
  22.5 1.9 %first_half_product.2.refs_0_ = f32[5,3,32,128]{3,2,1,0:T(8,128)S(1)} custom-call(s32[120]{0:T(128)S(1)} %get-tuple-element.49.index_ref, bf16[60,32,128]{2,1,0:T(8,128)(2,1)S(1)} %get-tuple-element.56.near_high, bf16[60,32,128]{2,1,0:T(8,128)(2,1)S(1)} %get-tuple-element.57.near_low, f32[5,3,64,128]{3,2,1,0:T(8,128)S(1)} %collective-permute-done.2.off_own, ...), custom_call_target="tpu_custom_call" | custom-call | tf_op jit(solution)/shard_map/first_half_product/pallas_call | solution.py:415
  25.1 5.7 %collective-permute-done.8.j_ref = f32[5,4,64,128]{3,2,1,0:T(8,128)S(1)} collective-permute-done((f32[5,4,64,128]{3,2,1,0:T(8,128)S(1)}, f32[5,4,64,128]{3,2,1,0:T(8,128)S(1)}, u32[]{:S(2)}, u32[]{:S(2)}) %collective-permute-start.8) | collective-permute-done | bytes 655392 | tf_op jit(solution)/shard_map/ppermute | solution.py:365
  30.8 0.9 %collective-permute-start.7 = (f32[5,3,32,128]{3,2,1,0:T(8,128)S(1)}, f32[5,3,32,128]{3,2,1,0:T(8,128)S(1)}, u32[]{:S(2)}, u32[]{:S(2)}) collective-permute-start(f32[5,3,32,128]{3,2,1,0:T(8,128)S(1)} %first_half_product.2.refs_0_), channel_id=1, source_target_pairs={{0,2},{2,0},{4,6},{6,4},{8,10},{10,8},{12,14},{14,12},{16,18},{18,... | collective-permute-start | bytes 737288 | tf_op jit(solution)/shard_map/ppermute | solution.py:368
  31.9 1.9 %first_half_product.3.refs_3_ = f32[5,3,32,128]{3,2,1,0:T(8,128)S(1)} custom-call(s32[120]{0:T(128)S(1)} %get-tuple-element.49.index_ref, bf16[60,32,128]{2,1,0:T(8,128)(2,1)S(1)} %get-tuple-element.56.near_high, bf16[60,32,128]{2,1,0:T(8,128)(2,1)S(1)} %get-tuple-element.57.near_low, f32[5,3,64,128]{3,2,1,0:T(8,128)S(1)} %collective-permute-done.2.off_own, ...), custom_call_target="tpu_custom_call" | custom-call | tf_op jit(solution)/shard_map/first_half_product/pallas_call | solution.py:415
  34.5 3.2 %collective-permute-start.9 = (f32[5,3,32,128]{3,2,1,0:T(8,128)S(1)}, f32[5,3,32,128]{3,2,1,0:T(8,128)S(1)}, u32[]{:S(2)}, u32[]{:S(2)}) collective-permute-start(f32[5,3,32,128]{3,2,1,0:T(8,128)S(1)} %first_half_product.3.refs_3_), channel_id=1, source_target_pairs={{0,2},{2,0},{4,6},{6,4},{8,10},{10,8},{12,14},{14,12},{16,18},{18,... | collective-permute-start | bytes 737288 | tf_op jit(solution)/shard_map/ppermute | solution.py:368
  38.1 1.9 %first_product.1 = (f32[5,6,16,128]{3,2,1,0:T(8,128)S(1)}, f32[5,6,16,128]{3,2,1,0:T(8,128)S(1)}) custom-call(s32[120]{0:T(128)S(1)} %get-tuple-element.49.index_ref, bf16[60,32,128]{2,1,0:T(8,128)(2,1)S(1)} %get-tuple-element.68.near_high, bf16[60,32,128]{2,1,0:T(8,128)(2,1)S(1)} %get-tuple-element.69.near_low, ...), custom_call_target="tpu_custom_call" | custom-call | tf_op jit(solution)/shard_map/first_product/pallas_call | solution.py:415
  40.7 2.6 %collective-permute-start.18 = (f32[5,6,16,128]{3,2,1,0:T(8,128)S(1)}, f32[5,6,16,128]{3,2,1,0:T(8,128)S(1)}, u32[]{:S(2)}, u32[]{:S(2)}) collective-permute-start(f32[5,6,16,128]{3,2,1,0:T(8,128)S(1)} %get-tuple-element.73.refs_0_), channel_id=1, source_target_pairs={{0,2},{2,0},{4,6},{6,4},{8,10},{10,8},{12,14},{14,12},{16,18},{18,... | collective-permute-start | bytes 737288 | tf_op jit(solution)/shard_map/ppermute | solution.py:368
  44.0 3.2 %collective-permute-start.16 = (f32[5,6,16,128]{3,2,1,0:T(8,128)S(1)}, f32[5,6,16,128]{3,2,1,0:T(8,128)S(1)}, u32[]{:S(2)}, u32[]{:S(2)}) collective-permute-start(f32[5,6,16,128]{3,2,1,0:T(8,128)S(1)} %get-tuple-element.70.refs_0_), channel_id=1, source_target_pairs={{0,2},{2,0},{4,6},{6,4},{8,10},{10,8},{12,14},{14,12},{16,18},{18,... | collective-permute-start | bytes 737288 | tf_op jit(solution)/shard_map/ppermute | solution.py:368
  47.2 2.6 %left_and_second_product.1 = (f32[5,3,32,128]{3,2,1,0:T(8,128)S(1)}, f32[5,3,32,128]{3,2,1,0:T(8,128)S(1)}, bf16[5,768,256]{2,1,0:T(8,128)(2,1)S(1)}) custom-call(s32[180]{0:T(256)S(1)} %get-tuple-element.43.index_ref, f32[5,3,32,128]{3,2,1,0:T(8,128)S(1)} %first_half_product.2.refs_0_, f32[5,3,32,128]{3,2,1,0:T(8,128)S(1)} %collective-permute-done.6.refs_1_, ...), custom_call_target="tpu_custom_call" | custom-call | tf_op jit(solution)/shard_map/left_and_second_product/pallas_call | solution.py:428
  50.6 1.5 %second_product.3 = (f32[5,3,16,128]{3,2,1,0:T(8,128)S(1)}, f32[5,3,16,128]{3,2,1,0:T(8,128)S(1)}) custom-call(s32[180]{0:T(256)S(1)} %get-tuple-element.43.index_ref, f32[5,6,16,128]{3,2,1,0:T(8,128)S(1)} %get-tuple-element.73.refs_0_, f32[5,6,16,128]{3,2,1,0:T(8,128)S(1)} %collective-permute-done.17.refs_1_, ...), custom_call_target="tpu_custom_call" | custom-call | tf_op jit(solution)/shard_map/second_product/pallas_call | solution.py:428
  52.1 1.5 %collective-permute-start.20 = (f32[5,3,16,128]{3,2,1,0:T(8,128)S(1)}, f32[5,3,16,128]{3,2,1,0:T(8,128)S(1)}, u32[]{:S(2)}, u32[]{:S(2)}) collective-permute-start(f32[5,3,16,128]{3,2,1,0:T(8,128)S(1)} %get-tuple-element.76), channel_id=1, source_target_pairs={{0,1},{1,0},{2,3},{3,2},{4,5},{5,4},{6,7},{7,6},{8,9},{9,8},{10,11... | collective-permute-start | bytes 368648 | tf_op jit(solution)/shard_map/ppermute | solution.py:365
  53.6 1.5 %second_product.2 = (f32[5,3,16,128]{3,2,1,0:T(8,128)S(1)}, f32[5,3,16,128]{3,2,1,0:T(8,128)S(1)}) custom-call(s32[180]{0:T(256)S(1)} %get-tuple-element.43.index_ref, f32[5,6,16,128]{3,2,1,0:T(8,128)S(1)} %get-tuple-element.70.refs_0_, f32[5,6,16,128]{3,2,1,0:T(8,128)S(1)} %collective-permute-done.15.refs_1_, ...), custom_call_target="tpu_custom_call" | custom-call | tf_op jit(solution)/shard_map/second_product/pallas_call | solution.py:428
  55.8 3.0 %collective-permute-done.12.oth_ref = f32[5,3,32,128]{3,2,1,0:T(8,128)S(1)} collective-permute-done((f32[5,3,32,128]{3,2,1,0:T(8,128)S(1)}, f32[5,3,32,128]{3,2,1,0:T(8,128)S(1)}, u32[]{:S(2)}, u32[]{:S(2)}) %collective-permute-start.12) | collective-permute-done | bytes 245792 | tf_op jit(solution)/shard_map/ppermute | solution.py:365
  59.4 2.0 %collective-permute-done.20.oth_two = f32[5,3,16,128]{3,2,1,0:T(8,128)S(1)} collective-permute-done((f32[5,3,16,128]{3,2,1,0:T(8,128)S(1)}, f32[5,3,16,128]{3,2,1,0:T(8,128)S(1)}, u32[]{:S(2)}, u32[]{:S(2)}) %collective-permute-start.20) | collective-permute-done | bytes 122912 | tf_op jit(solution)/shard_map/ppermute | solution.py:365
  61.4 1.7 %collective-permute-done.19.oth_one = f32[5,3,16,128]{3,2,1,0:T(8,128)S(1)} collective-permute-done((f32[5,3,16,128]{3,2,1,0:T(8,128)S(1)}, f32[5,3,16,128]{3,2,1,0:T(8,128)S(1)}, u32[]{:S(2)}, u32[]{:S(2)}) %collective-permute-start.19) | collective-permute-done | bytes 122912 | tf_op jit(solution)/shard_map/ppermute | solution.py:365
  63.1 1.4 %finish.1 = f32[5,6,64,128]{3,2,1,0:T(8,128)} custom-call(f32[5,6,64,128]{3,2,1,0:T(8,128)S(1)} %begin_finish.1.begun_ref, f32[5,3,16,128]{3,2,1,0:T(8,128)S(1)} %get-tuple-element.72.own_one, f32[5,3,16,128]{3,2,1,0:T(8,128)S(1)} %get-tuple-element.74.own_two, f32[5,3,16,128]{3,2,1,0:T(8,128)S(1)} %collective-permute-done.19.oth_one, ...), custom_call_target="tpu_custom_call" | custom-call | tf_op jit(solution)/shard_map/finish/pallas_call | solution.py:470
  (45 shorter events, 9.3 us)
Async XLA Ops:
  1.2 4.6 %copy-start.4 = (s32[5,4]{0,1:T(4,128)S(1)}, s32[5,4]{0,1:T(4,128)}, u32[]{:S(2)}) copy-start(s32[5,4]{0,1:T(4,128)} %param.6) | copy-start | bytes 244
  1.2 12.0 %copy-start.2 = (f32[5,4,64,128]{3,2,1,0:T(8,128)S(1)}, f32[5,4,64,128]{3,2,1,0:T(8,128)}, u32[]{:S(2)}) copy-start(f32[5,4,64,128]{3,2,1,0:T(8,128)} %j_ref) | copy-start | bytes 1966084
  1.5 11.7 %collective-permute-start = (f32[5,3,32,128]{3,2,1,0:T(8,128)S(1)}, f32[5,3,32,128]{3,2,1,0:T(8,128)S(1)}, u32[]{:S(2)}, u32[]{:S(2)}) collective-permute-start(f32[5,3,32,128]{3,2,1,0:T(8,128)S(1)} %get-tuple-element.44.refs_9_), channel_id=1, source_target_pairs={{0,1},{1,0},{2,3},{3,2},{4,5},{5,4},{6,7},{7,6},{8,9},{9,8},{10,11... | collective-permute-start | bytes 737288 | tf_op jit(solution)/shard_map/ppermute | solution.py:365
  4.6 11.2 %collective-permute-start.1 = (f32[5,3,32,128]{3,2,1,0:T(8,128)S(1)}, f32[5,3,32,128]{3,2,1,0:T(8,128)S(1)}, u32[]{:S(2)}, u32[]{:S(2)}) collective-permute-start(f32[5,3,32,128]{3,2,1,0:T(8,128)S(1)} %get-tuple-element.41.refs_0_.refs_8_), channel_id=1, source_target_pairs={{0,1},{1,0},{2,3},{3,2},{4,5},{5,4},{6,7},{7,6},{8,9},{9,8},{10,11... | collective-permute-start | bytes 737288 | tf_op jit(solution)/shard_map/ppermute | solution.py:365
  5.0 11.5 %collective-permute-start.2 = (f32[5,3,64,128]{3,2,1,0:T(8,128)S(1)}, f32[5,3,64,128]{3,2,1,0:T(8,128)S(1)}, u32[]{:S(2)}, u32[]{:S(2)}) collective-permute-start(f32[5,3,64,128]{3,2,1,0:T(8,128)S(1)} %split_own.1.z_own.refs_6_), channel_id=1, source_target_pairs={{2,4},{6,8},{10,12},{14,16},{18,20},{22,24},{26,28},{4,2},{8,6},{1... | collective-permute-start | bytes 1474568 | tf_op jit(solution)/shard_map/ppermute | solution.py:372
  9.9 6.8 %collective-permute-start.3 = (f32[5,3,64,128]{3,2,1,0:T(8,128)S(1)}, f32[5,3,64,128]{3,2,1,0:T(8,128)S(1)}, u32[]{:S(2)}, u32[]{:S(2)}) collective-permute-start(f32[5,3,64,128]{3,2,1,0:T(8,128)S(1)} %split_own.1.z_own.refs_6_), channel_id=1, source_target_pairs={{0,2},{2,0},{4,6},{6,4},{8,10},{10,8},{12,14},{14,12},{16,18},{18,... | collective-permute-start | bytes 1474568 | tf_op jit(solution)/shard_map/ppermute | solution.py:368
  13.2 17.6 %collective-permute-start.8 = (f32[5,4,64,128]{3,2,1,0:T(8,128)S(1)}, f32[5,4,64,128]{3,2,1,0:T(8,128)S(1)}, u32[]{:S(2)}, u32[]{:S(2)}) collective-permute-start(f32[5,4,64,128]{3,2,1,0:T(8,128)S(1)} %copy-done.2), channel_id=1, source_target_pairs={{0,1},{1,0},{2,3},{3,2},{4,5},{5,4},{6,7},{7,6},{8,9},{9,8},{10,11... | collective-permute-start | bytes 1966088 | tf_op jit(solution)/shard_map/ppermute | solution.py:365
  15.8 1.5 %collective-permute-start.4 = (f32[5,3,32,128]{3,2,1,0:T(8,128)S(1)}, f32[5,3,32,128]{3,2,1,0:T(8,128)S(1)}, u32[]{:S(2)}, u32[]{:S(2)}) collective-permute-start(f32[5,3,32,128]{3,2,1,0:T(8,128)S(1)} %collective-permute-done.1.z_oth.refs_10_), channel_id=1, source_target_pairs={{0,2},{2,0},{4,6},{6,4},{8,10},{10,8},{12,14},{14,12},{16,18},{18,... | collective-permute-start | bytes 737288 | tf_op jit(solution)/shard_map/ppermute | solution.py:368
  15.8 6.7 %collective-permute-start.5 = (f32[5,3,32,128]{3,2,1,0:T(8,128)S(1)}, f32[5,3,32,128]{3,2,1,0:T(8,128)S(1)}, u32[]{:S(2)}, u32[]{:S(2)}) collective-permute-start(f32[5,3,32,128]{3,2,1,0:T(8,128)S(1)} %collective-permute-done.1.z_oth.refs_10_), channel_id=1, source_target_pairs={{2,4},{6,8},{10,12},{14,16},{18,20},{22,24},{26,28},{4,2},{8,6},{1... | collective-permute-start | bytes 737288 | tf_op jit(solution)/shard_map/ppermute | solution.py:372
  17.6 25.7 %collective-permute-start.11 = (f32[5,3,64,128]{3,2,1,0:T(8,128)S(1)}, f32[5,3,64,128]{3,2,1,0:T(8,128)S(1)}, u32[]{:S(2)}, u32[]{:S(2)}) collective-permute-start(f32[5,3,64,128]{3,2,1,0:T(8,128)S(1)} %split_own.1.z_own.refs_6_), channel_id=1, source_target_pairs={{0,1},{1,0},{2,3},{3,2},{4,5},{5,4},{6,7},{7,6},{8,9},{9,8},{10,11... | collective-permute-start | bytes 1474568 | tf_op jit(solution)/shard_map/ppermute | solution.py:365
  19.5 14.3 %collective-permute-start.13 = (f32[5,3,32,128]{3,2,1,0:T(8,128)S(1)}, f32[5,3,32,128]{3,2,1,0:T(8,128)S(1)}, u32[]{:S(2)}, u32[]{:S(2)}) collective-permute-start(f32[5,3,32,128]{3,2,1,0:T(8,128)S(1)} %collective-permute-done.refs_11_.z_oth), channel_id=1, source_target_pairs={{0,2},{2,0},{4,6},{6,4},{8,10},{10,8},{12,14},{14,12},{16,18},{18,... | collective-permute-start | bytes 737288 | tf_op jit(solution)/shard_map/ppermute | solution.py:368
  21.9 12.7 %collective-permute-start.14 = (f32[5,3,32,128]{3,2,1,0:T(8,128)S(1)}, f32[5,3,32,128]{3,2,1,0:T(8,128)S(1)}, u32[]{:S(2)}, u32[]{:S(2)}) collective-permute-start(f32[5,3,32,128]{3,2,1,0:T(8,128)S(1)} %collective-permute-done.refs_11_.z_oth), channel_id=1, source_target_pairs={{2,4},{6,8},{10,12},{14,16},{18,20},{22,24},{26,28},{4,2},{8,6},{1... | collective-permute-start | bytes 737288 | tf_op jit(solution)/shard_map/ppermute | solution.py:372
  24.5 15.5 %collective-permute-start.6 = (f32[5,3,32,128]{3,2,1,0:T(8,128)S(1)}, f32[5,3,32,128]{3,2,1,0:T(8,128)S(1)}, u32[]{:S(2)}, u32[]{:S(2)}) collective-permute-start(f32[5,3,32,128]{3,2,1,0:T(8,128)S(1)} %first_half_product.2.refs_0_), channel_id=1, source_target_pairs={{2,4},{6,8},{10,12},{14,16},{18,20},{22,24},{26,28},{4,2},{8,6},{1... | collective-permute-start | bytes 737288 | tf_op jit(solution)/shard_map/ppermute | solution.py:372
  30.8 9.9 %collective-permute-start.7 = (f32[5,3,32,128]{3,2,1,0:T(8,128)S(1)}, f32[5,3,32,128]{3,2,1,0:T(8,128)S(1)}, u32[]{:S(2)}, u32[]{:S(2)}) collective-permute-start(f32[5,3,32,128]{3,2,1,0:T(8,128)S(1)} %first_half_product.2.refs_0_), channel_id=1, source_target_pairs={{0,2},{2,0},{4,6},{6,4},{8,10},{10,8},{12,14},{14,12},{16,18},{18,... | collective-permute-start | bytes 737288 | tf_op jit(solution)/shard_map/ppermute | solution.py:368
  33.8 10.2 %collective-permute-start.10 = (f32[5,3,32,128]{3,2,1,0:T(8,128)S(1)}, f32[5,3,32,128]{3,2,1,0:T(8,128)S(1)}, u32[]{:S(2)}, u32[]{:S(2)}) collective-permute-start(f32[5,3,32,128]{3,2,1,0:T(8,128)S(1)} %first_half_product.3.refs_3_), channel_id=1, source_target_pairs={{2,4},{6,8},{10,12},{14,16},{18,20},{22,24},{26,28},{4,2},{8,6},{1... | collective-permute-start | bytes 737288 | tf_op jit(solution)/shard_map/ppermute | solution.py:372
  34.5 12.7 %collective-permute-start.9 = (f32[5,3,32,128]{3,2,1,0:T(8,128)S(1)}, f32[5,3,32,128]{3,2,1,0:T(8,128)S(1)}, u32[]{:S(2)}, u32[]{:S(2)}) collective-permute-start(f32[5,3,32,128]{3,2,1,0:T(8,128)S(1)} %first_half_product.3.refs_3_), channel_id=1, source_target_pairs={{0,2},{2,0},{4,6},{6,4},{8,10},{10,8},{12,14},{14,12},{16,18},{18,... | collective-permute-start | bytes 737288 | tf_op jit(solution)/shard_map/ppermute | solution.py:368
  40.0 10.6 %collective-permute-start.17 = (f32[5,6,16,128]{3,2,1,0:T(8,128)S(1)}, f32[5,6,16,128]{3,2,1,0:T(8,128)S(1)}, u32[]{:S(2)}, u32[]{:S(2)}) collective-permute-start(f32[5,6,16,128]{3,2,1,0:T(8,128)S(1)} %get-tuple-element.73.refs_0_), channel_id=1, source_target_pairs={{2,4},{6,8},{10,12},{14,16},{18,20},{22,24},{26,28},{4,2},{8,6},{1... | collective-permute-start | bytes 737288 | tf_op jit(solution)/shard_map/ppermute | solution.py:372
  40.7 9.9 %collective-permute-start.18 = (f32[5,6,16,128]{3,2,1,0:T(8,128)S(1)}, f32[5,6,16,128]{3,2,1,0:T(8,128)S(1)}, u32[]{:S(2)}, u32[]{:S(2)}) collective-permute-start(f32[5,6,16,128]{3,2,1,0:T(8,128)S(1)} %get-tuple-element.73.refs_0_), channel_id=1, source_target_pairs={{0,2},{2,0},{4,6},{6,4},{8,10},{10,8},{12,14},{14,12},{16,18},{18,... | collective-permute-start | bytes 737288 | tf_op jit(solution)/shard_map/ppermute | solution.py:368
  43.3 10.3 %collective-permute-start.15 = (f32[5,6,16,128]{3,2,1,0:T(8,128)S(1)}, f32[5,6,16,128]{3,2,1,0:T(8,128)S(1)}, u32[]{:S(2)}, u32[]{:S(2)}) collective-permute-start(f32[5,6,16,128]{3,2,1,0:T(8,128)S(1)} %get-tuple-element.70.refs_0_), channel_id=1, source_target_pairs={{2,4},{6,8},{10,12},{14,16},{18,20},{22,24},{26,28},{4,2},{8,6},{1... | collective-permute-start | bytes 737288 | tf_op jit(solution)/shard_map/ppermute | solution.py:372
  44.0 9.6 %collective-permute-start.16 = (f32[5,6,16,128]{3,2,1,0:T(8,128)S(1)}, f32[5,6,16,128]{3,2,1,0:T(8,128)S(1)}, u32[]{:S(2)}, u32[]{:S(2)}) collective-permute-start(f32[5,6,16,128]{3,2,1,0:T(8,128)S(1)} %get-tuple-element.70.refs_0_), channel_id=1, source_target_pairs={{0,2},{2,0},{4,6},{6,4},{8,10},{10,8},{12,14},{14,12},{16,18},{18,... | collective-permute-start | bytes 737288 | tf_op jit(solution)/shard_map/ppermute | solution.py:368
  49.9 8.9 %collective-permute-start.12 = (f32[5,3,32,128]{3,2,1,0:T(8,128)S(1)}, f32[5,3,32,128]{3,2,1,0:T(8,128)S(1)}, u32[]{:S(2)}, u32[]{:S(2)}) collective-permute-start(f32[5,3,32,128]{3,2,1,0:T(8,128)S(1)} %get-tuple-element.67), channel_id=1, source_target_pairs={{0,1},{1,0},{2,3},{3,2},{4,5},{5,4},{6,7},{7,6},{8,9},{9,8},{10,11... | collective-permute-start | bytes 737288 | tf_op jit(solution)/shard_map/ppermute | solution.py:365
  52.1 6.7 %copy-start.1 = (f32[5,6,64,128]{3,2,1,0:T(8,128)S(1)}, f32[5,6,64,128]{3,2,1,0:T(8,128)}, u32[]{:S(2)}) copy-start(f32[5,6,64,128]{3,2,1,0:T(8,128)} %z_ref.5) | copy-start | bytes 2949124
  52.1 9.3 %collective-permute-start.20 = (f32[5,3,16,128]{3,2,1,0:T(8,128)S(1)}, f32[5,3,16,128]{3,2,1,0:T(8,128)S(1)}, u32[]{:S(2)}, u32[]{:S(2)}) collective-permute-start(f32[5,3,16,128]{3,2,1,0:T(8,128)S(1)} %get-tuple-element.76), channel_id=1, source_target_pairs={{0,1},{1,0},{2,3},{3,2},{4,5},{5,4},{6,7},{7,6},{8,9},{9,8},{10,11... | collective-permute-start | bytes 368648 | tf_op jit(solution)/shard_map/ppermute | solution.py:365
  55.1 8.0 %collective-permute-start.19 = (f32[5,3,16,128]{3,2,1,0:T(8,128)S(1)}, f32[5,3,16,128]{3,2,1,0:T(8,128)S(1)}, u32[]{:S(2)}, u32[]{:S(2)}) collective-permute-start(f32[5,3,16,128]{3,2,1,0:T(8,128)S(1)} %get-tuple-element.75), channel_id=1, source_target_pairs={{0,1},{1,0},{2,3},{3,2},{4,5},{5,4},{6,7},{7,6},{8,9},{9,8},{10,11... | collective-permute-start | bytes 368648 | tf_op jit(solution)/shard_map/ppermute | solution.py:365
  (2 other events, 5.7 us)
